TPU v7x, 512 devices: a whole 4x8x8 slice. The times are simulated.
512 devices in a mesh: scen: 8 (over y), col: 64 (over z, x, core).
Axes of the slice: x: 4, y: 8, z: 8, core: 2. Of those that a mesh axis runs over, the one named last changes fastest.
Arguments:
- border: float32 [16, 1536, 16384], P('scen', None, 'col'), may hold values from -6 to 6
- barrier: float32 [16, 1536], P('scen'), may hold values from 0.1 to 10
- row_counts: int32 [16], P('scen'), may hold values from 1024 to 1536, as said below
Outputs:
- factor_panel: float32 [64, 8, 32, 512], P('col', 'scen')
Inputs may be any that keep to these rules, and one draw needn't show every extreme that they name: `row_counts`: every value lies between 1024 and 1536, and at least one scenario uses all 1536 rows.
All inputs are finite; a program needn't handle non-finite values.
Results may differ from a plain program's by a relative error of at most 0.0003.
Values sent between devices are 32-bit elements; how exact they have to be, the bound alone decides.
No kernel may reach another device: no remote copies, remote signals or barrier semaphores. Data moves between devices by JAX's collectives and lax.ppermute only.
A program may use at most 64 MiB of HBM per device.

v0:
```python
import jax
import jax.numpy as jnp
from jax import lax
from jax.sharding import PartitionSpec as P

PANEL = 512


def sent_to_all(array, axis):
    copies = jnp.broadcast_to(array, (lax.axis_size(axis), *array.shape))
    return lax.all_to_all(copies, axis, split_axis=0, concat_axis=0, tiled=True)


def in_order(tiles, dim):
    lengths = list(tiles.shape[1:])
    lengths[dim] *= tiles.shape[0]
    return jnp.moveaxis(tiles, 0, dim).reshape(lengths)


def gather_directly(array, axis, dim):
    tiles = sent_to_all(array, axis)
    return in_order(tiles, dim)


def body(border, barrier, row_counts):
    scen_here = border.shape[0]
    capacity = border.shape[1]
    own_cols = border.shape[2]
    per_owner = PANEL // lax.axis_size("col")
    rows_owned = own_cols // lax.axis_size("scen")
    positions = lax.iota(jnp.int32, capacity)
    weights = jnp.where(positions[None, :] < row_counts[:, None], 1.0 / barrier, jnp.float32(0.0))
    weighted = (border * weights[:, :, None]).reshape(scen_here * capacity, own_cols)
    panel_part = jnp.transpose(border[:, :, :per_owner], (2, 0, 1)).reshape(
        per_owner, scen_here * capacity
    )
    schur_part = jnp.einsum(
        "rc,kr->ck",
        weighted,
        lax.all_gather(panel_part, "col", axis=0, tiled=True),
        precision=lax.Precision.HIGHEST,
        preferred_element_type=jnp.float32,
    )
    summed_rows = lax.psum(schur_part[:per_owner], "scen")
    block = gather_directly(summed_rows, "col", 0)
    lower = jnp.linalg.cholesky(block)
    owned = lax.psum_scatter(schur_part, "scen", scatter_dimension=0, tiled=True)
    solved = lax.linalg.triangular_solve(
        lower, owned, left_side=False, lower=True, transpose_a=True
    )
    return solved.reshape(1, 1, rows_owned, PANEL)


def solution(mesh):
    placed = (P("scen", None, "col"), P("scen", None), P("scen"))
    return jax.shard_map(
        body, mesh=mesh, in_specs=placed, out_specs=P("col", "scen", None, None), check_vma=False
    )
```

profile of v0, /device:TPU:1, one launch (start us, length us, event | category | flops | bytes accessed | tf_op | source)
XLA Modules:
  0.0 325.5 jit_solution(17585274431209889643)
XLA Ops:
  6.5 1.5 slice_bitcast_fusion
  8.1 1.1 copy.7
  9.3 2.4 broadcast_multiply_fusion
  11.6 92.2 %all-gather.2.cloned.1.call-done = f32[512,3072]{1,0:T(8,128)} async-done(((f32[8,3072]{1,0:T(8,128)}), f32[512,3072]{1,0:T(8,128)}) %all-gather.2.cloned.1.call-update) | async-done | bytes 6291472 | tf_op jit(solution)/shard_map/all_gather | solution.py:40
  103.8 13.0 %fusion.31 = f32[256,512]{1,0:T(8,128)} fusion(f32[3072,256]{1,0:T(8,128)S(1)} %bitcast.58, f32[512,3072]{1,0:T(8,128)} %all-gather.2.cloned.1.call-done), kind=kOutput, calls=%fused_computation.70 | convolution fusion | flops 4831838208 | bytes 9961472 | tf_op jit(solution)/shard_map/rc,kr->ck/dot_general | solution.py:37
  116.9 0.7 slice.122
  117.6 22.7 %psum.7 = f32[8,512]{1,0:T(8,128)S(1)} all-reduce(f32[8,512]{1,0:T(8,128)S(1)} %slice.122), channel_id=1, replica_groups=mesh['scen'=8,'col'=64] {'scen'}, use_global_device_ids=true, to_apply=%region_1.2 | all-reduce | flops 4096 | bytes 32768 | tf_op jit(solution)/shard_map/psum | solution.py:44
  140.3 1.1 broadcast_in_dim.13
  141.4 12.5 %all-to-all-start = ((f32[64,8,512]{2,1,0:T(8,128)}), f32[64,8,512]{2,1,0:T(8,128)S(1)}, u32[]{:S(2)}, u32[]{:S(2)}) async-start(f32[64,8,512]{2,1,0:T(8,128)} %broadcast_in_dim.13), calls=%async_computation.1 | async-start | bytes 2097152 | tf_op jit(solution)/shard_map/all_to_all | solution.py:11
  153.9 0.2 reduce-scatter.2.cloned.1.call-start
  154.2 0.5 reduce-scatter.2.cloned.1.call-update
  154.7 27.2 %all-to-all-done = f32[64,8,512]{2,1,0:T(8,128)S(1)} async-done(((f32[64,8,512]{2,1,0:T(8,128)}), f32[64,8,512]{2,1,0:T(8,128)S(1)}, u32[]{:S(2)}, u32[]{:S(2)}) %all-to-all-start) | async-done | bytes 1048608 | tf_op jit(solution)/shard_map/all_to_all | solution.py:11
  181.9 0.3 copy.8
  182.2 0.2 fusion
  182.5 11.7 %cholesky.104 = f32[128,128]{1,0:T(8,128)S(1)} custom-call(f32[128,128]{1,0:T(8,128)S(1)} %cholesky.266), custom_call_target="Cholesky" | custom-call | tf_op jit(solution)/shard_map/jit(cholesky)/cholesky | solution.py:46
  194.2 9.8 %custom-call.30 = f32[1,128,128]{1,2,0:T(8,128)S(1)} custom-call(f32[1,128,128]{2,1,0:T(8,128)S(1)} %get-tuple-element.32), custom_call_target="InvertDiagBlocksLowerTriangular" | custom-call | tf_op jit(solution)/shard_map/jit(cholesky)/cholesky | solution.py:46
  204.2 0.3 constant_dynamic-update-slice_fusion.3
  204.5 0.3 convolution_subtract_fusion
  204.8 11.7 %cholesky.217 = f32[128,128]{1,0:T(8,128)S(1)} custom-call(f32[128,128]{1,0:T(8,128)S(1)} %cholesky.270), custom_call_target="Cholesky" | custom-call | tf_op jit(solution)/shard_map/jit(cholesky)/cholesky | solution.py:46
  216.6 10.0 %custom-call.31 = f32[1,128,128]{1,2,0:T(8,128)S(1)} custom-call(f32[1,128,128]{2,1,0:T(8,128)S(1)} %get-tuple-element.29), custom_call_target="InvertDiagBlocksLowerTriangular" | custom-call | tf_op jit(solution)/shard_map/jit(cholesky)/cholesky | solution.py:46
  226.6 0.3 convolution_dynamic-update-slice_fusion
  226.9 0.4 convolution_subtract_fusion.1
  227.3 11.7 %cholesky.238 = f32[128,128]{1,0:T(8,128)S(1)} custom-call(f32[128,128]{1,0:T(8,128)S(1)} %cholesky.275), custom_call_target="Cholesky" | custom-call | tf_op jit(solution)/shard_map/jit(cholesky)/cholesky | solution.py:46
  239.0 0.7 compare_reduce_fusion.1
  239.7 9.8 %custom-call.32 = f32[1,128,128]{1,2,0:T(8,128)S(1)} custom-call(f32[1,128,128]{2,1,0:T(8,128)S(1)} %get-tuple-element.26), custom_call_target="InvertDiagBlocksLowerTriangular" | custom-call | tf_op jit(solution)/shard_map/jit(cholesky)/cholesky | solution.py:46
  249.6 0.2 convolution_dynamic-update-slice_fusion.1
  249.8 0.4 convolution_subtract_fusion.2
  250.2 11.7 %cholesky.255 = f32[128,128]{1,0:T(8,128)S(1)} custom-call(f32[128,128]{1,0:T(8,128)S(1)} %convolution_subtract_fusion.2), custom_call_target="Cholesky" | custom-call | tf_op jit(solution)/shard_map/jit(cholesky)/cholesky | solution.py:46
  261.9 0.6 compare_reduce_fusion
  262.5 0.7 compare_reduce_fusion.2
  266.2 8.1 %while.1 = (s32[]{:T(128)}, f32[512,512]{1,0:T(8,128)S(1)}, s32[4,2]{0,1:T(2,128)S(1)}, f32[4,128,128]{2,1,0:T(8,128)S(1)}, s32[]{:T(128)}) while((s32[]{:T(128)}, f32[512,512]{1,0:T(8,128)S(1)}, s32[4,2]{0,1:T(2,128)S(1)}, f32[4,128,128]{2,1,0:T(8,128)S(1)}, s32[]{:T(128)}) %tuple.27), condition=%wide.while_cond, body=%wide.while_body.sunk | while | flops 2 | bytes 131181 | solution.py:48
  266.3 0.6 fusion.40
  266.9 1.3 bitcast_dynamic-update-slice_fusion.2
  268.3 0.6 fusion.40
  268.9 1.3 bitcast_dynamic-update-slice_fusion.2
  270.3 0.6 fusion.40
  270.9 1.3 bitcast_dynamic-update-slice_fusion.2
  272.4 0.6 fusion.40
  273.0 1.3 bitcast_dynamic-update-slice_fusion.2
  274.3 39.3 %custom-call.33 = f32[4,128,128]{1,2,0:T(8,128)S(1)} custom-call(f32[4,128,128]{2,1,0:T(8,128)S(1)} %get-tuple-element.12), custom_call_target="InvertDiagBlocksLowerTriangular" | custom-call | tf_op jit(solution)/shard_map/triangular_solve | solution.py:48
  313.7 0.9 fusion.13
  314.6 0.9 convolution_subtract_fusion.5
  315.5 0.2 fusion.11
  315.7 1.0 convolution_subtract_fusion.4
  316.6 0.2 fusion.10
  316.8 1.0 convolution_subtract_fusion.3
  317.9 0.2 fusion.9
  318.0 0.6 maximum_bitcast_fusion
  (24 shorter events, 0.8 us)
Async XLA Ops:
  6.5 2.6 copy-start
  6.5 2.6 copy-start.1
  6.5 97.3 %all-gather.2.cloned.1.call-start = ((), (), s32[]{:S(2)}) async-start(), calls=%async_computation.2 | async-start | bytes 6389760 | tf_op jit(solution)/shard_map/all_gather | solution.py:40
  141.4 40.5 %all-to-all-start = ((f32[64,8,512]{2,1,0:T(8,128)}), f32[64,8,512]{2,1,0:T(8,128)S(1)}, u32[]{:S(2)}, u32[]{:S(2)}) async-start(f32[64,8,512]{2,1,0:T(8,128)} %broadcast_in_dim.13), calls=%async_computation.1 | async-start | bytes 2097152 | tf_op jit(solution)/shard_map/all_to_all | solution.py:11
  153.9 159.8 %reduce-scatter.2.cloned.1.call-start = ((), (), s32[]{:S(2)}) async-start(), calls=%async_computation.3 | async-start | bytes 589824 | tf_op jit(solution)/shard_map/reduce_scatter | solution.py:47
Sparse Core Ops, SparseCore 0:
  10.7 93.0 all-gather.1
  157.5 33.9 reduce-scatter.1
where the time goes:
time: 326 us
  other arithmetic  121 us (37%)
  waiting for transfers between devices  120 us (37%)
  blocking collectives  22.7 us (7%)
  matrix products  19.2 us (6%)
  between operations  16.5 us (5%)
  local copies, waits for them, and re-layouts  13 us (4%)
  starting transfers between devices  12.7 us (4%)
    all_gather x1, waiting for transfers between devices, body(): lax.all_gather(panel_part, 'col', axis=0, tiled=True)  92.2 us
    another operation x14, other arithmetic, body(): lower = jnp.linalg.cholesky(block)  78.7 us
    another operation x3, other arithmetic, body(): lax.linalg.triangular_solve(lower, owned, left_side=False, lower=True, tr...  39.4 us
    all_to_all x1, waiting for transfers between devices, sent_to_all(): return lax.all_to_all(copies, axis, split_axis=0, concat_axis=0, tiled=True)  27.2 us
    psum x1, blocking collectives, body(): summed_rows = lax.psum(schur_part[:per_owner], 'scen')  22.7 us
    dot_general x1, matrix products, body(): jnp.einsum('rc,kr->ck', weighted, lax.all_gather(panel_part, 'col', axis=...  13 us
    all_to_all x1, starting transfers between devices, sent_to_all(): return lax.all_to_all(copies, axis, split_axis=0, concat_axis=0, tiled=True)  12.5 us
    another operation x12, local copies, waits for them, and re-layouts  8.06 us
  transfers between devices with their start and end apart: 3, of which 2 were waited for; matrix products, arithmetic and copies ran while one was open for 40% of the time, Pallas kernels for 0%

commit v1 on v0

v1 whole, which is shorter than its diff:
```python
import jax
import jax.numpy as jnp
from jax import lax
from jax.experimental import pallas as pl
from jax.experimental.pallas import tpu as pltpu
from jax.sharding import Mesh, PartitionSpec as P

PANEL = 512
BLOCK = 128
TILE = 8
COL = ("z", "x", "core")
SWAP = [(0, 1), (1, 0)]


def dot(a, b, dim_a, dim_b):
    return lax.dot_general(
        a, b, (((dim_a,), (dim_b,)), ((), ())),
        precision=lax.Precision.HIGHEST, preferred_element_type=jnp.float32,
    )


def factor_inverse(diagonal):
    count = BLOCK // TILE
    row_of = lax.broadcasted_iota(jnp.int32, (TILE, BLOCK), 0)
    col_of = lax.broadcasted_iota(jnp.int32, (TILE, BLOCK), 1)
    below = lax.broadcasted_iota(jnp.int32, (TILE, 1), 0)
    left = [diagonal[TILE * t:TILE * (t + 1), :] for t in range(count)]
    right = [jnp.where(col_of == row_of + TILE * t, jnp.float32(1.0), jnp.float32(0.0)) for t in range(count)]
    for j in range(BLOCK):
        first, r = divmod(j, TILE)
        row = left[first][r:r + 1, :]
        scale = 1.0 / row[:, j:j + 1]
        row_left = row * scale
        row_right = right[first][r:r + 1, :] * scale
        for t in range(first, count):
            if t == first and r == TILE - 1:
                continue
            factor = left[t][:, j:j + 1]
            if t == first:
                factor = jnp.where(below > r, factor, 0.0)
            left[t] = left[t] - factor * row_left
            right[t] = right[t] - factor * row_right
    rows = []
    for t in range(count):
        pivots = jnp.sum(jnp.where(col_of == row_of + TILE * t, left[t], 0.0), axis=1, keepdims=True)
        rows.append(right[t] * lax.rsqrt(pivots))
    return jnp.concatenate(rows, axis=0)


def inverse_kernel(block_ref, out_ref, rest, sums):
    rest[...] = block_ref[...]
    sums[...] = jnp.zeros_like(sums)
    out_ref[...] = jnp.zeros_like(out_ref)
    for a in range(0, PANEL, BLOCK):
        b = a + BLOCK
        inverse = factor_inverse(rest[a:b, a:b])
        out_ref[a:b, a:b] = inverse
        if a > 0:
            out_ref[a:b, 0:a] = -dot(inverse, sums[a:b, 0:a], 1, 0)
        if b < PANEL:
            upper = dot(inverse, rest[a:b, b:PANEL], 1, 0)
            rest[b:PANEL, b:PANEL] = rest[b:PANEL, b:PANEL] - dot(upper, upper, 0, 0)
            sums[b:PANEL, 0:b] = sums[b:PANEL, 0:b] + dot(upper, out_ref[a:b, 0:b], 0, 0)


def inverse_factor(block):
    shape = (PANEL, PANEL)
    return pl.pallas_call(
        inverse_kernel,
        out_shape=jax.ShapeDtypeStruct(shape, jnp.float32),
        in_specs=[pl.BlockSpec(memory_space=pltpu.VMEM)],
        out_specs=pl.BlockSpec(memory_space=pltpu.VMEM),
        scratch_shapes=[pltpu.VMEM(shape, jnp.float32), pltpu.VMEM(shape, jnp.float32)],
        compiler_params=pltpu.CompilerParams(vmem_limit_bytes=32 << 20),
        cost_estimate=pl.CostEstimate(flops=4 * PANEL ** 3, bytes_accessed=8 * PANEL ** 2, transcendentals=PANEL),
        name="inverse_factor",
    )(block)


def product(weighted, panel):
    return jnp.einsum(
        "rc,kr->ck", weighted, panel,
        precision=lax.Precision.HIGH, preferred_element_type=jnp.float32,
    )


def body(border, barrier, row_counts):
    capacity = border.shape[1]
    own_cols = border.shape[2]
    n_scen = lax.axis_size("scen")
    n_x = lax.axis_size("x")
    n_z = lax.axis_size("z")
    per_owner = PANEL // (n_z * n_x * 2)
    rows_owned = own_cols // n_scen
    core = lax.axis_index("core")

    panel_part = jnp.transpose(border[:, :, :per_owner], (0, 2, 1))
    to_send = jnp.broadcast_to(panel_part[None], (n_x, 2, per_owner, capacity))
    beside = lax.all_to_all(
        to_send.reshape(n_x * 2, per_owner, capacity), ("x", "core"), split_axis=0, concat_axis=0, tiled=True
    ).reshape(n_x * 2 * per_owner, capacity)
    panel = lax.all_gather(beside, "z", axis=0, tiled=True)

    positions = lax.iota(jnp.int32, capacity)
    here = lax.dynamic_index_in_dim(barrier, core, 0, keepdims=False)
    count = lax.dynamic_index_in_dim(row_counts, core, 0, keepdims=False)
    weights = jnp.where(positions < count, 1.0 / here, jnp.float32(0.0))

    mine = lax.dynamic_index_in_dim(border, core, 0, keepdims=False)
    other = lax.ppermute(lax.dynamic_index_in_dim(border, 1 - core, 0, keepdims=False), "core", SWAP)

    chip_rows = lax.dynamic_slice_in_dim(beside, lax.axis_index("x") * 2 * per_owner, 2 * per_owner, 0)
    block_part = jnp.einsum(
        "ir,kr->ik", chip_rows * weights[None, :], panel,
        precision=lax.Precision.HIGHEST, preferred_element_type=jnp.float32,
    )
    parts = jnp.broadcast_to(block_part.reshape(1, 2, per_owner, PANEL), (n_scen, 2, per_owner, PANEL))
    parts = lax.all_to_all(
        parts.reshape(n_scen * 2, per_owner, PANEL), ("scen", "core"), split_axis=0, concat_axis=0, tiled=True
    )
    summed_rows = jnp.sum(parts, axis=0)
    copies = jnp.broadcast_to(summed_rows, (PANEL // per_owner, per_owner, PANEL))
    block = lax.all_to_all(copies, COL, split_axis=0, concat_axis=0, tiled=True).reshape(PANEL, PANEL)
    inverse = inverse_factor(block)

    schur_mine = product(mine * weights[:, None], panel)
    schur_other = product(other * weights[:, None], panel)
    schur_part = schur_mine + lax.ppermute(schur_other, "core", SWAP)
    owned = lax.psum_scatter(schur_part, "scen", scatter_dimension=0, tiled=True)
    solved = dot(owned, inverse, 1, 1)
    return solved.reshape(1, 1, rows_owned, PANEL)


def solution(mesh):
    inner = Mesh(mesh.devices.reshape(mesh.shape["scen"], 8, 4, 2), ("scen",) + COL)
    placed = (P("scen", None, COL), P("scen", None), P("scen"))
    return jax.shard_map(
        body, mesh=inner, in_specs=placed, out_specs=P(COL, "scen", None, None), check_vma=False
    )
```

time: 326 us -> 192 us (0.59)
  other arithmetic: 121 us -> 2.38 us
  waiting for transfers between devices: 120 us -> 56.4 us
  Pallas kernels: 0 us -> 45.8 us
  blocking collectives: 22.7 us -> 36.9 us
  local copies, waits for them, and re-layouts: 13 us -> 7.78 us
    another operation x17 -> x0, other arithmetic: 118 us -> none  [the longest x14 78.7 us: body(): lower = jnp.linalg.cholesky(block)]
    all_gather x1, waiting for transfers between devices: 92.2 us -> 42 us  [body(): panel = lax.all_gather(beside, 'z', axis=0, tiled=True)]
    pallas_call x0 -> x1, Pallas kernels: none -> 45.8 us  [inverse_factor(): pl.pallas_call(inverse_kernel, out_shape=jax.ShapeDtypeStruct(shape, jnp....]
    all_to_all x0 -> x2, blocking collectives: none -> 36.9 us  [the longest x1 18.9 us: body(): lax.all_to_all(parts.reshape(n_scen * 2, per_owner, PANEL), ('scen', 'cor...]
    psum x1 -> x0, blocking collectives: 22.7 us -> none  [body(): summed_rows = lax.psum(schur_part[:per_owner], 'scen')]
    all_to_all x1, waiting for transfers between devices: 27.2 us -> 14.3 us  [body(): lax.all_to_all(copies, COL, split_axis=0, concat_axis=0, tiled=True)]
    another operation x17 -> x0, local copies, waits for them, and re-layouts: 8.2 us -> none
    another operation x13 -> x0, matrix products: 6.16 us -> none  [the longest x7 4.28 us: body(): lax.linalg.triangular_solve(lower, owned, left_side=False, lower=True, tr...]
  transfers between devices with their start and end apart: 3 -> 5, of which waited for: 2 -> 2; matrix products, arithmetic and copies ran while one was open for 40% -> 10% of each run, Pallas kernels for 0% -> 24%
where the time goes in v1:
time: 192 us
  waiting for transfers between devices  56.4 us (29%)
  Pallas kernels  45.8 us (24%)
  blocking collectives  36.9 us (19%)
  matrix products  16.4 us (9%)
  between operations  13.6 us (7%)
  starting transfers between devices  12.6 us (7%)
  local copies, waits for them, and re-layouts  7.78 us (4%)
  other arithmetic  2.38 us (1%)
    pallas_call x1, Pallas kernels, inverse_factor(): pl.pallas_call(inverse_kernel, out_shape=jax.ShapeDtypeStruct(shape, jnp....  45.8 us
    all_gather x1, waiting for transfers between devices, body(): panel = lax.all_gather(beside, 'z', axis=0, tiled=True)  42 us
    all_to_all x1, blocking collectives, body(): lax.all_to_all(parts.reshape(n_scen * 2, per_owner, PANEL), ('scen', 'cor...  18.9 us
    all_to_all x1, blocking collectives, body(): lax.all_to_all(to_send.reshape(n_x * 2, per_owner, capacity), ('x', 'core...  18 us
    all_to_all x1, waiting for transfers between devices, body(): lax.all_to_all(copies, COL, split_axis=0, concat_axis=0, tiled=True)  14.3 us
    dot_general x2, matrix products, product(): jnp.einsum('rc,kr->ck', weighted, panel, precision=lax.Precision.HIGH, pr...  9.34 us
    all_to_all x1, starting transfers between devices, body(): lax.all_to_all(copies, COL, split_axis=0, concat_axis=0, tiled=True)  7.23 us
    transpose x2, local copies, waits for them, and re-layouts, body(): panel_part = jnp.transpose(border[:, :, :per_owner], (0, 2, 1))  4.69 us
  transfers between devices with their start and end apart: 5, of which 2 were waited for; matrix products, arithmetic and copies ran while one was open for 10% of the time, Pallas kernels for 24%

profile of v1, /device:TPU:1, one launch (start us, length us, event | category | flops | bytes accessed | tf_op | source)
XLA Modules:
  0.0 191.8 jit_solution(12761854708069291746)
XLA Ops:
  6.5 0.0 copy-start.1
  6.5 0.0 all-gather.2.cloned.1.call-start
  6.5 2.8 %slice_bitcast_fusion = f32[2,8,1536]{1,2,0:T(8,128)} fusion(f32[2,1536,256]{2,1,0:T(8,128)} %param.3), kind=kLoop, calls=%fused_computation.5 | loop fusion | bytes 196608 | tf_op jit(solution)/shard_map/transpose | solution.py:97
  9.4 0.0 copy-start.3
  9.4 0.0 copy-start.2
  9.4 1.9 copy.5
  11.3 18.0 %all_to_all.15 = f32[8,8,1536]{2,1,0:T(8,128)} all-to-all(f32[8,8,1536]{2,1,0:T(8,128)S(1)} %bitcast.24), channel_id=1, replica_groups=mesh['scen'=8,'z'=8,'x'=4,'core'=2] {'x','core'}, dimensions={0} | all-to-all | bytes 786432 | tf_op jit(solution)/shard_map/all_to_all | solution.py:99
  29.3 0.0 all-gather.2.cloned.1.call-update
  29.3 0.0 copy-done.1
  29.3 1.3 dynamic-slice_bitcast_fusion
  30.6 2.8 %collective-permute-start = (f32[1536,256]{1,0:T(8,128)}, f32[1536,256]{1,0:T(8,128)S(1)}, u32[]{:S(2)}, u32[]{:S(2)}) collective-permute-start(f32[1536,256]{1,0:T(8,128)} %dynamic-slice_bitcast_fusion), channel_id=1, source_target_pairs={{0,1},{1,0},{2,3},{3,2},{4,5},{5,4},{6,7},{7,6},{8,9},{9,8},{10,11... | collective-permute-start | bytes 4718600 | tf_op jit(solution)/shard_map/ppermute | solution.py:110
  33.4 0.0 copy-done.3
  33.4 0.6 dynamic_slice.19
  34.0 0.0 copy-done.2
  34.0 0.7 fusion.10
  34.7 42.0 %all-gather.2.cloned.1.call-done = f32[512,1536]{1,0:T(8,128)} async-done(((f32[64,1536]{1,0:T(8,128)}), f32[512,1536]{1,0:T(8,128)}) %all-gather.2.cloned.1.call-update) | async-done | bytes 3145744 | tf_op jit(solution)/shard_map/all_gather | solution.py:102
  76.7 4.6 %convolution_bitcast_fusion.1 = f32[2,8,512]{2,1,0:T(8,128)S(1)} fusion(f32[512,1536]{1,0:T(8,128)} %all-gather.2.cloned.1.call-done, f32[64,1536]{1,0:T(8,128)} %bitcast.23, s32[]{:T(128)S(6)} %select_n.28, f32[1536]{0:T(1024)S(1)} %get-tuple-element.5), kind=kOutput, calls=%fused_computation.8 | convolution fusion | flops 151019520 | bytes 3282948 | tf_op jit(solution)/shard_map/ir,kr->ik/dot_general | solution.py:113
  81.3 18.9 %all_to_all.16 = f32[16,8,512]{2,1,0:T(8,128)S(1)} all-to-all(f32[16,8,512]{2,1,0:T(8,128)S(1)} %bitcast.25), channel_id=1, replica_groups=mesh['scen'=8,'z'=8,'x'=4,'core'=2] {'scen','core'}, dimensions={0} | all-to-all | bytes 524288 | tf_op jit(solution)/shard_map/all_to_all | solution.py:118
  100.2 1.2 broadcast_in_dim.30
  101.4 7.2 %all-to-all-start.2 = ((f32[64,8,512]{2,1,0:T(8,128)}), f32[64,8,512]{2,1,0:T(8,128)S(1)}, u32[]{:S(2)}, u32[]{:S(2)}) async-start(f32[64,8,512]{2,1,0:T(8,128)} %broadcast_in_dim.30), calls=%async_computation.3 | async-start | bytes 2097152 | tf_op jit(solution)/shard_map/all_to_all | solution.py:123
  108.6 0.0 reduce-scatter.2.cloned.1.call-start
  108.7 0.0 copy-start
  108.7 0.8 fusion.9
  109.5 0.0 collective-permute-done
  109.5 4.9 %fusion.1 = f32[256,512]{1,0:T(8,128)S(1)} fusion(f32[512,1536]{1,0:T(8,128)} %all-gather.2.cloned.1.call-done, f32[1536,256]{1,0:T(8,128)S(1)} %collective-permute-done, f32[1536]{0:T(1024)S(1)} %fusion.9), kind=kOutput, calls=%fused_computation.2 | convolution fusion | flops 1208352768 | bytes 5249024 | tf_op jit(solution)/shard_map/rc,kr->ck/dot_general | solution.py:81
  114.4 2.5 %collective-permute-start.1 = (f32[256,512]{1,0:T(8,128)S(1)}, f32[256,512]{1,0:T(8,128)S(1)}, u32[]{:S(2)}, u32[]{:S(2)}) collective-permute-start(f32[256,512]{1,0:T(8,128)S(1)} %fusion.1), channel_id=1, source_target_pairs={{0,1},{1,0},{2,3},{3,2},{4,5},{5,4},{6,7},{7,6},{8,9},{9,8},{10,11... | collective-permute-start | bytes 1572872 | tf_op jit(solution)/shard_map/ppermute | solution.py:128
  117.0 0.0 copy-done
  117.0 4.4 %fusion = f32[256,512]{1,0:T(8,128)S(1)} fusion(f32[512,1536]{1,0:T(8,128)S(1)} %copy-done, f32[2,1536,256]{2,1,0:T(8,128)} %param.3, s32[]{:T(128)S(6)} %select_n.25, f32[1536]{0:T(1024)S(1)} %fusion.9), kind=kOutput, calls=%fused_computation.1 | convolution fusion | flops 1208352768 | bytes 5249028 | tf_op jit(solution)/shard_map/rc,kr->ck/dot_general | solution.py:81
  121.4 0.0 collective-permute-done.1
  121.4 0.9 add.22
  122.3 0.0 reduce-scatter.2.cloned.1.call-update
  122.3 14.3 %all-to-all-done.2 = f32[64,8,512]{2,1,0:T(8,128)S(1)} async-done(((f32[64,8,512]{2,1,0:T(8,128)}), f32[64,8,512]{2,1,0:T(8,128)S(1)}, u32[]{:S(2)}, u32[]{:S(2)}) %all-to-all-start.2) | async-done | bytes 1048608 | tf_op jit(solution)/shard_map/all_to_all | solution.py:123
  136.6 45.8 %inverse_factor.1 = f32[512,512]{1,0:T(8,128)S(1)} custom-call(f32[512,512]{1,0:T(8,128)S(1)} %bitcast.21), custom_call_target="tpu_custom_call" | custom-call | flops 536870912 | bytes 2097152 | tf_op jit(solution)/shard_map/inverse_factor/pallas_call | solution.py:68
  182.4 0.0 reduce-scatter.2.cloned.1.call-done
  182.4 2.5 %convolution_bitcast_fusion = f32[1,1,32,512]{3,2,1,0:T(8,128)} fusion(f32[32,512]{1,0:T(8,128)} %reduce-scatter.2.cloned.1.call-done, f32[512,512]{1,0:T(8,128)S(1)} %inverse_factor.1), kind=kOutput, calls=%fused_computation.7 | convolution fusion | flops 100663296 | bytes 1179648 | tf_op jit(solution)/shard_map/dot_general | solution.py:16
  (3 shorter events, 0.1 us)
Async XLA Ops:
  6.5 22.8 %copy-start.1 = (f32[2,1536,256]{2,1,0:T(8,128)S(1)}, f32[2,1536,256]{2,1,0:T(8,128)}, u32[]{:S(2)}) copy-start(f32[2,1536,256]{2,1,0:T(8,128)} %param.3) | copy-start | bytes 9437188
  6.5 70.1 %all-gather.2.cloned.1.call-start = ((), (), s32[]{:S(2)}) async-start(), calls=%async_computation.4 | async-start | bytes 3538944 | tf_op jit(solution)/shard_map/all_gather | solution.py:102
  9.4 24.0 %copy-start.3 = (s32[2]{0:T(128)S(1)}, s32[2]{0:T(128)}, u32[]{:S(2)}) copy-start(s32[2]{0:T(128)} %param.5) | copy-start | bytes 28
  9.4 24.6 %copy-start.2 = (f32[2,1536]{1,0:T(2,128)S(1)}, f32[2,1536]{1,0:T(2,128)}, u32[]{:S(2)}) copy-start(f32[2,1536]{1,0:T(2,128)} %param.4) | copy-start | bytes 36868
  30.6 78.9 %collective-permute-start = (f32[1536,256]{1,0:T(8,128)}, f32[1536,256]{1,0:T(8,128)S(1)}, u32[]{:S(2)}, u32[]{:S(2)}) collective-permute-start(f32[1536,256]{1,0:T(8,128)} %dynamic-slice_bitcast_fusion), channel_id=1, source_target_pairs={{0,1},{1,0},{2,3},{3,2},{4,5},{5,4},{6,7},{7,6},{8,9},{9,8},{10,11... | collective-permute-start | bytes 4718600 | tf_op jit(solution)/shard_map/ppermute | solution.py:110
  101.4 35.2 %all-to-all-start.2 = ((f32[64,8,512]{2,1,0:T(8,128)}), f32[64,8,512]{2,1,0:T(8,128)S(1)}, u32[]{:S(2)}, u32[]{:S(2)}) async-start(f32[64,8,512]{2,1,0:T(8,128)} %broadcast_in_dim.30), calls=%async_computation.3 | async-start | bytes 2097152 | tf_op jit(solution)/shard_map/all_to_all | solution.py:123
  108.6 73.8 %reduce-scatter.2.cloned.1.call-start = ((), (), s32[]{:S(2)}) async-start(), calls=%async_computation.5 | async-start | bytes 589824 | tf_op jit(solution)/shard_map/reduce_scatter | solution.py:129
  108.7 8.3 %copy-start = (f32[512,1536]{1,0:T(8,128)S(1)}, f32[512,1536]{1,0:T(8,128)}, u32[]{:S(2)}) copy-start(f32[512,1536]{1,0:T(8,128)} %all-gather.2.cloned.1.call-done) | copy-start | bytes 9437188
  114.4 7.0 %collective-permute-start.1 = (f32[256,512]{1,0:T(8,128)S(1)}, f32[256,512]{1,0:T(8,128)S(1)}, u32[]{:S(2)}, u32[]{:S(2)}) collective-permute-start(f32[256,512]{1,0:T(8,128)S(1)} %fusion.1), channel_id=1, source_target_pairs={{0,1},{1,0},{2,3},{3,2},{4,5},{5,4},{6,7},{7,6},{8,9},{9,8},{10,11... | collective-permute-start | bytes 1572872 | tf_op jit(solution)/shard_map/ppermute | solution.py:128
Sparse Core Ops, SparseCore 0:
  29.4 47.1 all-gather.1
  122.4 31.3 reduce-scatter.1

commit v2 on v1

--- a/solution.py
+++ b/solution.py
@@ -19,36 +19,72 @@
     )
 
 
+def reciprocal(x):
+    first = pltpu.reciprocal(x, approx=True)
+    return first * (2.0 - x * first)
+
+
+def spread(piece):
+    return jnp.broadcast_to(piece, (TILE, BLOCK))
+
+
 def factor_inverse(diagonal):
     count = BLOCK // TILE
     row_of = lax.broadcasted_iota(jnp.int32, (TILE, BLOCK), 0)
     col_of = lax.broadcasted_iota(jnp.int32, (TILE, BLOCK), 1)
-    below = lax.broadcasted_iota(jnp.int32, (TILE, 1), 0)
     left = [diagonal[TILE * t:TILE * (t + 1), :] for t in range(count)]
     right = [jnp.where(col_of == row_of + TILE * t, jnp.float32(1.0), jnp.float32(0.0)) for t in range(count)]
-    for j in range(BLOCK):
-        first, r = divmod(j, TILE)
-        row = left[first][r:r + 1, :]
-        scale = 1.0 / row[:, j:j + 1]
-        row_left = row * scale
-        row_right = right[first][r:r + 1, :] * scale
-        for t in range(first, count):
-            if t == first and r == TILE - 1:
-                continue
-            factor = left[t][:, j:j + 1]
-            if t == first:
-                factor = jnp.where(below > r, factor, 0.0)
-            left[t] = left[t] - factor * row_left
-            right[t] = right[t] - factor * row_right
     rows = []
-    for t in range(count):
-        pivots = jnp.sum(jnp.where(col_of == row_of + TILE * t, left[t], 0.0), axis=1, keepdims=True)
-        rows.append(right[t] * lax.rsqrt(pivots))
+    for s in range(count):
+        own = [spread(left[s][:, TILE * s + c:TILE * s + c + 1]) for c in range(TILE)]
+        rest = [[spread(own[c][r:r + 1, :]) for c in range(r + 1)] for r in range(TILE)]
+        up_left = [spread(left[s][r:r + 1, :]) for r in range(TILE)]
+        up_right = [spread(right[s][r:r + 1, :]) for r in range(TILE)]
+        inverse = [None] * TILE
+        factor = [[None] * TILE for _ in range(TILE)]
+        for c in range(TILE):
+            inverse[c] = reciprocal(rest[c][c])
+            for r in range(c + 1, TILE):
+                factor[r][c] = rest[r][c] * inverse[c]
+            for r in range(c + 1, TILE):
+                for q in range(c + 1, r + 1):
+                    rest[r][q] = rest[r][q] - factor[r][c] * rest[q][c]
+                up_left[r] = up_left[r] - factor[r][c] * up_left[c]
+                up_right[r] = up_right[r] - factor[r][c] * up_right[c]
+        if s < count - 1:
+            down_left = [None] * TILE
+            down_right = [None] * TILE
+            for c in range(TILE - 1, -1, -1):
+                down_left[c] = inverse[c] * up_left[c]
+                down_right[c] = inverse[c] * up_right[c]
+                for r in range(c + 1, TILE):
+                    down_left[c] = down_left[c] - factor[r][c] * down_left[r]
+                    down_right[c] = down_right[c] - factor[r][c] * down_right[r]
+            for t in range(s + 1, count):
+                across = [spread(left[t][:, TILE * s + c:TILE * s + c + 1]) for c in range(TILE)]
+                for c in range(TILE - 1, -1, -1):
+                    left[t] = left[t] - across[c] * down_left[c]
+                    right[t] = right[t] - across[c] * down_right[c]
+        scaled = lax.rsqrt(rest[0][0]) * up_right[0]
+        for r in range(1, TILE):
+            scaled = jnp.where(row_of == r, lax.rsqrt(rest[r][r]) * up_right[r], scaled)
+        rows.append(scaled)
     return jnp.concatenate(rows, axis=0)
 
 
-def inverse_kernel(block_ref, out_ref, rest, sums):
-    rest[...] = block_ref[...]
+def inverse_kernel(core_ref, own_ref, other_ref, out_ref, rest, sums):
+    core = core_ref[0]
+    for half_ref, half in ((own_ref, core), (other_ref, 1 - core)):
+        for x in range(4):
+            for k in range(2):
+                for pair in range(4):
+                    one = half_ref[8 * pair + x, 16 * k:16 * (k + 1), :]
+                    two = half_ref[8 * pair + 4 + x, 16 * k:16 * (k + 1), :]
+                    for h in range(2):
+                        at = pl.multiple_of(half * 256, 256) + h * 128 + k * 64 + x * 16
+                        rest[pl.ds(at, 16), pl.ds(128 * pair, 128)] = jnp.concatenate(
+                            [one[:, 64 * h:64 * (h + 1)], two[:, 64 * h:64 * (h + 1)]], axis=1
+                        )
     sums[...] = jnp.zeros_like(sums)
     out_ref[...] = jnp.zeros_like(out_ref)
     for a in range(0, PANEL, BLOCK):
@@ -63,18 +99,18 @@
             sums[b:PANEL, 0:b] = sums[b:PANEL, 0:b] + dot(upper, out_ref[a:b, 0:b], 0, 0)
 
 
-def inverse_factor(block):
+def inverse_factor(core, own, other):
     shape = (PANEL, PANEL)
     return pl.pallas_call(
         inverse_kernel,
         out_shape=jax.ShapeDtypeStruct(shape, jnp.float32),
-        in_specs=[pl.BlockSpec(memory_space=pltpu.VMEM)],
+        in_specs=[pl.BlockSpec(memory_space=pltpu.SMEM)] + [pl.BlockSpec(memory_space=pltpu.VMEM)] * 2,
         out_specs=pl.BlockSpec(memory_space=pltpu.VMEM),
         scratch_shapes=[pltpu.VMEM(shape, jnp.float32), pltpu.VMEM(shape, jnp.float32)],
         compiler_params=pltpu.CompilerParams(vmem_limit_bytes=32 << 20),
         cost_estimate=pl.CostEstimate(flops=4 * PANEL ** 3, bytes_accessed=8 * PANEL ** 2, transcendentals=PANEL),
         name="inverse_factor",
-    )(block)
+    )(core, own, other)
 
 
 def product(weighted, panel):
@@ -110,18 +146,20 @@
     other = lax.ppermute(lax.dynamic_index_in_dim(border, 1 - core, 0, keepdims=False), "core", SWAP)
 
     chip_rows = lax.dynamic_slice_in_dim(beside, lax.axis_index("x") * 2 * per_owner, 2 * per_owner, 0)
+    along = lax.all_gather(chip_rows, "z", axis=0, tiled=True)
     block_part = jnp.einsum(
-        "ir,kr->ik", chip_rows * weights[None, :], panel,
+        "qr,pr->qp", along, beside * weights[None, :],
         precision=lax.Precision.HIGHEST, preferred_element_type=jnp.float32,
     )
-    parts = jnp.broadcast_to(block_part.reshape(1, 2, per_owner, PANEL), (n_scen, 2, per_owner, PANEL))
-    parts = lax.all_to_all(
-        parts.reshape(n_scen * 2, per_owner, PANEL), ("scen", "core"), split_axis=0, concat_axis=0, tiled=True
-    )
-    summed_rows = jnp.sum(parts, axis=0)
-    copies = jnp.broadcast_to(summed_rows, (PANEL // per_owner, per_owner, PANEL))
-    block = lax.all_to_all(copies, COL, split_axis=0, concat_axis=0, tiled=True).reshape(PANEL, PANEL)
-    inverse = inverse_factor(block)
+    halves = block_part.reshape(2, 2, 4 * per_owner, 8 * per_owner)
+    halves = jnp.concatenate([halves[:, 0], halves[:, 1]], axis=-1)
+    part = halves.shape[1:]
+    parts = jnp.broadcast_to(halves[None], (n_scen, 2) + part).reshape((n_scen * 2,) + part)
+    parts = lax.all_to_all(parts, ("scen", "core"), split_axis=0, concat_axis=0, tiled=True)
+    copies = jnp.broadcast_to(jnp.sum(parts, axis=0), (n_z * n_x,) + part)
+    own_half = lax.all_to_all(copies, ("z", "x"), split_axis=0, concat_axis=0, tiled=True)
+    other_half = lax.ppermute(own_half, "core", SWAP)
+    inverse = inverse_factor(jnp.reshape(core, (1,)), own_half, other_half)
 
     schur_mine = product(mine * weights[:, None], panel)
     schur_other = product(other * weights[:, None], panel)

time: 192 us -> 149 us (0.78)
  waiting for transfers between devices: 56.4 us -> 17.5 us
  Pallas kernels: 45.8 us -> 26.8 us
  starting transfers between devices: 12.6 us -> 24.2 us
  blocking collectives: 36.9 us -> 43.1 us
  matrix products: 16.4 us -> 12.6 us
    all_gather x1, waiting for transfers between devices: 42 us -> 0.02 us  [body(): panel = lax.all_gather(beside, 'z', axis=0, tiled=True)]
    all_gather x0 -> x1, blocking collectives: none -> 25 us  [body(): along = lax.all_gather(chip_rows, 'z', axis=0, tiled=True)]
    pallas_call x1, Pallas kernels: 45.8 us -> 26.8 us  [inverse_factor(): pl.pallas_call(inverse_kernel, out_shape=jax.ShapeDtypeStruct(shape, jnp....]
    all_to_all x1 -> x0, blocking collectives: 18.9 us -> none  [body(): lax.all_to_all(parts.reshape(n_scen * 2, per_owner, PANEL), ('scen', 'cor...]
    all_to_all x1 -> x2, starting transfers between devices: 7.23 us -> 16.9 us  [the longest x1 11.8 us: body(): lax.all_to_all(parts, ('scen', 'core'), split_axis=0, concat_axis=0, tile...]
    dot_general x1, matrix products: 4.59 us -> 0.77 us  [body(): jnp.einsum('qr,pr->qp', along, beside * weights[None, :], precision=lax.P...]
    ppermute x0 -> x1, starting transfers between devices: none -> 2.64 us  [body(): other_half = lax.ppermute(own_half, 'core', SWAP)]
    all_to_all x1 -> x2, waiting for transfers between devices: 14.3 us -> 16.1 us  [the longest x1 11.1 us: body(): lax.all_to_all(parts, ('scen', 'core'), split_axis=0, concat_axis=0, tile...]
  transfers between devices with their start and end apart: 5 -> 7, of which waited for: 2 -> 3; matrix products, arithmetic and copies ran while one was open for 10% -> 11% of each run, Pallas kernels for 24% -> 18%
where the time goes in v2:
time: 149 us; the launch traced here: 148 us
  blocking collectives  43.1 us (29%)
  Pallas kernels  26.8 us (18%)
  starting transfers between devices  24.2 us (16%)
  waiting for transfers between devices  17.5 us (12%)
  between operations  13.6 us (9%)
  matrix products  12.6 us (8%)
  local copies, waits for them, and re-layouts  8.26 us (6%)
  other arithmetic  2.29 us (2%)
    pallas_call x1, Pallas kernels, inverse_factor(): pl.pallas_call(inverse_kernel, out_shape=jax.ShapeDtypeStruct(shape, jnp....  26.8 us
    all_gather x1, blocking collectives, body(): along = lax.all_gather(chip_rows, 'z', axis=0, tiled=True)  25 us
    all_to_all x1, blocking collectives, body(): lax.all_to_all(to_send.reshape(n_x * 2, per_owner, capacity), ('x', 'core...  18 us
    all_to_all x1, starting transfers between devices, body(): lax.all_to_all(parts, ('scen', 'core'), split_axis=0, concat_axis=0, tile...  11.8 us
    all_to_all x1, waiting for transfers between devices, body(): lax.all_to_all(parts, ('scen', 'core'), split_axis=0, concat_axis=0, tile...  11.1 us
    dot_general x2, matrix products, product(): jnp.einsum('rc,kr->ck', weighted, panel, precision=lax.Precision.HIGH, pr...  9.35 us
    all_to_all x1, starting transfers between devices, body(): lax.all_to_all(copies, ('z', 'x'), split_axis=0, concat_axis=0, tiled=True)  5.08 us
    all_to_all x1, waiting for transfers between devices, body(): lax.all_to_all(copies, ('z', 'x'), split_axis=0, concat_axis=0, tiled=True)  5.06 us
  transfers between devices with their start and end apart: 7, of which 3 were waited for; matrix products, arithmetic and copies ran while one was open for 11% of the time, Pallas kernels for 18%

profile of v2, /device:TPU:1, one launch (start us, length us, event | category | flops | bytes accessed | tf_op | source)
XLA Modules:
  0.0 148.5 jit_solution(6794485800169241679)
XLA Ops:
  6.5 0.0 all-gather.2.cloned.1.call-start
  6.5 2.7 %slice_bitcast_fusion = f32[2,8,1536]{1,2,0:T(8,128)} fusion(f32[2,1536,256]{2,1,0:T(8,128)} %param.3), kind=kLoop, calls=%fused_computation.5 | loop fusion | bytes 196608 | tf_op jit(solution)/shard_map/transpose | solution.py:133
  9.2 0.0 copy-start.1
  9.2 2.0 %copy.6 = f32[2,8,1536]{2,1,0:T(8,128)S(1)} copy(f32[2,8,1536]{1,2,0:T(8,128)} %slice_bitcast_fusion) | data formatting | bytes 196608 | tf_op jit(solution)/shard_map/transpose | solution.py:133
  11.2 18.0 %all_to_all.15 = f32[8,8,1536]{2,1,0:T(8,128)} all-to-all(f32[8,8,1536]{2,1,0:T(8,128)S(1)} %bitcast.36), channel_id=1, replica_groups=mesh['scen'=8,'z'=8,'x'=4,'core'=2] {'x','core'}, dimensions={0} | all-to-all | bytes 786432 | tf_op jit(solution)/shard_map/all_to_all | solution.py:135
  29.3 0.0 all-gather.2.cloned.1.call-update
  29.3 0.0 copy-done.1
  29.3 0.0 copy-start.4
  29.3 0.0 copy-start.3
  29.3 0.0 copy-start.2
  29.3 1.3 dynamic-slice_bitcast_fusion
  30.6 2.8 %collective-permute-start = (f32[1536,256]{1,0:T(8,128)}, f32[1536,256]{1,0:T(8,128)S(1)}, u32[]{:S(2)}, u32[]{:S(2)}) collective-permute-start(f32[1536,256]{1,0:T(8,128)} %dynamic-slice_bitcast_fusion), channel_id=1, source_target_pairs={{0,1},{1,0},{2,3},{3,2},{4,5},{5,4},{6,7},{7,6},{8,9},{9,8},{10,11... | collective-permute-start | bytes 4718600 | tf_op jit(solution)/shard_map/ppermute | solution.py:146
  33.4 0.0 copy-done.4
  33.4 0.7 dynamic_slice.19
  34.0 0.0 copy-done.3
  34.0 0.7 fusion.11
  34.7 0.0 copy-done.2
  34.8 25.0 %all_gather.7 = f32[128,1536]{1,0:T(8,128)S(1)} all-gather(f32[16,1536]{1,0:T(8,128)S(1)} %constant_dynamic-slice_fusion), channel_id=1, replica_groups=mesh['scen'=8,'z'=8,'x'=4,'core'=2] {'z'}, dimensions={0}, use_global_device_ids=true | all-gather | bytes 884736 | tf_op jit(solution)/shard_map/all_gather | solution.py:149
  59.8 0.8 fusion.6
  60.6 0.1 pad_maximum_fusion
  60.7 0.8 broadcast_in_dim.27
  61.4 11.8 %all-to-all-start.1 = ((f32[16,32,128]{2,1,0:T(8,128)}), f32[16,32,128]{2,1,0:T(8,128)S(1)}, u32[]{:S(2)}, u32[]{:S(2)}) async-start(f32[16,32,128]{2,1,0:T(8,128)} %bitcast.13), calls=%async_computation.2 | async-start | bytes 524288 | tf_op jit(solution)/shard_map/all_to_all | solution.py:158
  73.2 0.6 fusion.10
  73.9 11.1 %all-to-all-done.1 = f32[16,32,128]{2,1,0:T(8,128)S(1)} async-done(((f32[16,32,128]{2,1,0:T(8,128)}), f32[16,32,128]{2,1,0:T(8,128)S(1)}, u32[]{:S(2)}, u32[]{:S(2)}) %all-to-all-start.1) | async-done | bytes 262176 | tf_op jit(solution)/shard_map/all_to_all | solution.py:158
  84.9 0.9 broadcast_in_dim.28
  85.8 5.1 %all-to-all-start.2 = ((f32[32,32,128]{2,1,0:T(8,128)}), f32[32,32,128]{2,1,0:T(8,128)S(1)}, u32[]{:S(2)}, u32[]{:S(2)}) async-start(f32[32,32,128]{2,1,0:T(8,128)} %broadcast_in_dim.28), calls=%async_computation.3 | async-start | bytes 1048576 | tf_op jit(solution)/shard_map/all_to_all | solution.py:160
  90.9 0.0 reduce-scatter.2.cloned.1.call-start
  90.9 0.0 collective-permute-done
  90.9 0.0 all-gather.2.cloned.1.call-done
  91.0 0.0 copy-start
  91.0 4.9 %fusion.1 = f32[256,512]{1,0:T(8,128)S(1)} fusion(f32[512,1536]{1,0:T(8,128)} %all-gather.2.cloned.1.call-done, f32[1536,256]{1,0:T(8,128)S(1)} %collective-permute-done, f32[1536]{0:T(1024)S(1)} %fusion.10), kind=kOutput, calls=%fused_computation.2 | convolution fusion | flops 1208352768 | bytes 5249024 | tf_op jit(solution)/shard_map/rc,kr->ck/dot_general | solution.py:117
  95.9 1.9 %collective-permute-start.1 = (f32[256,512]{1,0:T(8,128)S(1)}, f32[256,512]{1,0:T(8,128)S(1)}, u32[]{:S(2)}, u32[]{:S(2)}) collective-permute-start(f32[256,512]{1,0:T(8,128)S(1)} %fusion.1), channel_id=1, source_target_pairs={{0,1},{1,0},{2,3},{3,2},{4,5},{5,4},{6,7},{7,6},{8,9},{9,8},{10,11... | collective-permute-start | bytes 1572872 | tf_op jit(solution)/shard_map/ppermute | solution.py:166
  97.8 0.0 copy-done
  97.8 4.4 %fusion = f32[256,512]{1,0:T(8,128)S(1)} fusion(f32[512,1536]{1,0:T(8,128)S(1)} %copy-done, f32[2,1536,256]{2,1,0:T(8,128)} %param.3, s32[]{:T(128)S(6)} %select_n.25, f32[1536]{0:T(1024)S(1)} %fusion.10), kind=kOutput, calls=%fused_computation.1 | convolution fusion | flops 1208352768 | bytes 5249028 | tf_op jit(solution)/shard_map/rc,kr->ck/dot_general | solution.py:117
  102.3 0.0 collective-permute-done.1
  102.3 0.9 add.22
  103.2 0.0 reduce-scatter.2.cloned.1.call-update
  103.2 5.1 %all-to-all-done.2.own_ref = f32[32,32,128]{2,1,0:T(8,128)S(1)} async-done(((f32[32,32,128]{2,1,0:T(8,128)}), f32[32,32,128]{2,1,0:T(8,128)S(1)}, u32[]{:S(2)}, u32[]{:S(2)}) %all-to-all-start.2) | async-done | bytes 524320 | tf_op jit(solution)/shard_map/all_to_all | solution.py:160
  108.3 2.6 %collective-permute-start.2 = (f32[32,32,128]{2,1,0:T(8,128)S(1)}, f32[32,32,128]{2,1,0:T(8,128)S(1)}, u32[]{:S(2)}, u32[]{:S(2)}) collective-permute-start(f32[32,32,128]{2,1,0:T(8,128)S(1)} %all-to-all-done.2.own_ref), channel_id=1, source_target_pairs={{0,1},{1,0},{2,3},{3,2},{4,5},{5,4},{6,7},{7,6},{8,9},{9,8},{10,11... | collective-permute-start | bytes 1572872 | tf_op jit(solution)/shard_map/ppermute | solution.py:161
  110.9 1.3 collective-permute-done.2.other_ref
  112.2 26.8 %inverse_factor.1 = f32[512,512]{1,0:T(8,128)S(1)} custom-call(s32[1]{0:T(128)} %bitcast.6.core_ref, f32[32,32,128]{2,1,0:T(8,128)S(1)} %all-to-all-done.2.own_ref, f32[32,32,128]{2,1,0:T(8,128)S(1)} %collective-permute-done.2.other_ref), custom_call_target="tpu_custom_call" | custom-call | flops 536870912 | bytes 2097152 | tf_op jit(solution)/shard_map/inverse_factor/pallas_call | solution.py:104
  139.1 0.0 reduce-scatter.2.cloned.1.call-done
  139.1 2.5 %convolution_bitcast_fusion = f32[1,1,32,512]{3,2,1,0:T(8,128)} fusion(f32[32,512]{1,0:T(8,128)} %reduce-scatter.2.cloned.1.call-done, f32[512,512]{1,0:T(8,128)S(1)} %inverse_factor.1), kind=kOutput, calls=%fused_computation.7 | convolution fusion | flops 100663296 | bytes 1179648 | tf_op jit(solution)/shard_map/dot_general | solution.py:16
  (4 shorter events, 0.1 us)
Async XLA Ops:
  6.5 84.4 %all-gather.2.cloned.1.call-start = ((), (), s32[]{:S(2)}) async-start(), calls=%async_computation.4 | async-start | bytes 3538944 | tf_op jit(solution)/shard_map/all_gather | solution.py:138
  9.2 20.1 %copy-start.1 = (f32[2,1536,256]{2,1,0:T(8,128)S(1)}, f32[2,1536,256]{2,1,0:T(8,128)}, u32[]{:S(2)}) copy-start(f32[2,1536,256]{2,1,0:T(8,128)} %param.3) | copy-start | bytes 9437188
  29.3 4.1 %copy-start.4 = (s32[2]{0:T(128)S(1)}, s32[2]{0:T(128)}, u32[]{:S(2)}) copy-start(s32[2]{0:T(128)} %param.5) | copy-start | bytes 28
  29.3 4.7 %copy-start.3 = (f32[2,1536]{1,0:T(2,128)S(1)}, f32[2,1536]{1,0:T(2,128)}, u32[]{:S(2)}) copy-start(f32[2,1536]{1,0:T(2,128)} %param.4) | copy-start | bytes 36868
  29.3 5.4 %copy-start.2 = (f32[8,8,1536]{2,1,0:T(8,128)S(1)}, f32[8,8,1536]{2,1,0:T(8,128)}, u32[]{:S(2)}) copy-start(f32[8,8,1536]{2,1,0:T(8,128)} %all_to_all.15) | copy-start | bytes 1179652
  30.6 60.3 %collective-permute-start = (f32[1536,256]{1,0:T(8,128)}, f32[1536,256]{1,0:T(8,128)S(1)}, u32[]{:S(2)}, u32[]{:S(2)}) collective-permute-start(f32[1536,256]{1,0:T(8,128)} %dynamic-slice_bitcast_fusion), channel_id=1, source_target_pairs={{0,1},{1,0},{2,3},{3,2},{4,5},{5,4},{6,7},{7,6},{8,9},{9,8},{10,11... | collective-permute-start | bytes 4718600 | tf_op jit(solution)/shard_map/ppermute | solution.py:146
  61.4 23.5 %all-to-all-start.1 = ((f32[16,32,128]{2,1,0:T(8,128)}), f32[16,32,128]{2,1,0:T(8,128)S(1)}, u32[]{:S(2)}, u32[]{:S(2)}) async-start(f32[16,32,128]{2,1,0:T(8,128)} %bitcast.13), calls=%async_computation.2 | async-start | bytes 524288 | tf_op jit(solution)/shard_map/all_to_all | solution.py:158
  85.8 22.5 %all-to-all-start.2 = ((f32[32,32,128]{2,1,0:T(8,128)}), f32[32,32,128]{2,1,0:T(8,128)S(1)}, u32[]{:S(2)}, u32[]{:S(2)}) async-start(f32[32,32,128]{2,1,0:T(8,128)} %broadcast_in_dim.28), calls=%async_computation.3 | async-start | bytes 1048576 | tf_op jit(solution)/shard_map/all_to_all | solution.py:160
  90.9 48.2 %reduce-scatter.2.cloned.1.call-start = ((), (), s32[]{:S(2)}) async-start(), calls=%async_computation.5 | async-start | bytes 589824 | tf_op jit(solution)/shard_map/reduce_scatter | solution.py:167
  91.0 6.9 %copy-start = (f32[512,1536]{1,0:T(8,128)S(1)}, f32[512,1536]{1,0:T(8,128)}, u32[]{:S(2)}) copy-start(f32[512,1536]{1,0:T(8,128)} %all-gather.2.cloned.1.call-done) | copy-start | bytes 9437188
  95.9 6.4 %collective-permute-start.1 = (f32[256,512]{1,0:T(8,128)S(1)}, f32[256,512]{1,0:T(8,128)S(1)}, u32[]{:S(2)}, u32[]{:S(2)}) collective-permute-start(f32[256,512]{1,0:T(8,128)S(1)} %fusion.1), channel_id=1, source_target_pairs={{0,1},{1,0},{2,3},{3,2},{4,5},{5,4},{6,7},{7,6},{8,9},{9,8},{10,11... | collective-permute-start | bytes 1572872 | tf_op jit(solution)/shard_map/ppermute | solution.py:166
  108.3 4.0 %collective-permute-start.2 = (f32[32,32,128]{2,1,0:T(8,128)S(1)}, f32[32,32,128]{2,1,0:T(8,128)S(1)}, u32[]{:S(2)}, u32[]{:S(2)}) collective-permute-start(f32[32,32,128]{2,1,0:T(8,128)S(1)} %all-to-all-done.2.own_ref), channel_id=1, source_target_pairs={{0,1},{1,0},{2,3},{3,2},{4,5},{5,4},{6,7},{7,6},{8,9},{9,8},{10,11... | collective-permute-start | bytes 1572872 | tf_op jit(solution)/shard_map/ppermute | solution.py:161
Sparse Core Ops, SparseCore 0:
  29.4 52.6 all-gather.1
  103.3 31.5 reduce-scatter.1

commit v3 on v2

--- a/solution.py
+++ b/solution.py
@@ -72,7 +72,7 @@
     return jnp.concatenate(rows, axis=0)
 
 
-def inverse_kernel(core_ref, own_ref, other_ref, out_ref, rest, sums):
+def inverse_kernel(core_ref, own_ref, other_ref, out_ref, rest, sums, lower):
     core = core_ref[0]
     for half_ref, half in ((own_ref, core), (other_ref, 1 - core)):
         for x in range(4):
@@ -86,17 +86,24 @@
                             [one[:, 64 * h:64 * (h + 1)], two[:, 64 * h:64 * (h + 1)]], axis=1
                         )
     sums[...] = jnp.zeros_like(sums)
-    out_ref[...] = jnp.zeros_like(out_ref)
+    lower[...] = jnp.zeros_like(lower)
     for a in range(0, PANEL, BLOCK):
         b = a + BLOCK
         inverse = factor_inverse(rest[a:b, a:b])
-        out_ref[a:b, a:b] = inverse
+        lower[a:b, a:b] = inverse
         if a > 0:
-            out_ref[a:b, 0:a] = -dot(inverse, sums[a:b, 0:a], 1, 0)
+            lower[a:b, 0:a] = -dot(inverse, sums[a:b, 0:a], 1, 0)
         if b < PANEL:
             upper = dot(inverse, rest[a:b, b:PANEL], 1, 0)
             rest[b:PANEL, b:PANEL] = rest[b:PANEL, b:PANEL] - dot(upper, upper, 0, 0)
-            sums[b:PANEL, 0:b] = sums[b:PANEL, 0:b] + dot(upper, out_ref[a:b, 0:b], 0, 0)
+            sums[b:PANEL, 0:b] = sums[b:PANEL, 0:b] + dot(upper, lower[a:b, 0:b], 0, 0)
+    for k in range(0, PANEL, BLOCK):
+        for a in range(0, PANEL, BLOCK):
+            turned = jnp.transpose(lower[a:a + BLOCK, k:k + BLOCK]) if a >= k else jnp.zeros((BLOCK, BLOCK), jnp.float32)
+            for piece in range(0, BLOCK, 16):
+                z, x = divmod((k + piece) // 16, 4)
+                to = 128 * x + 16 * z
+                out_ref[to:to + 16, a:a + BLOCK] = turned[piece:piece + 16, :]
 
 
 def inverse_factor(core, own, other):
@@ -106,66 +113,113 @@
         out_shape=jax.ShapeDtypeStruct(shape, jnp.float32),
         in_specs=[pl.BlockSpec(memory_space=pltpu.SMEM)] + [pl.BlockSpec(memory_space=pltpu.VMEM)] * 2,
         out_specs=pl.BlockSpec(memory_space=pltpu.VMEM),
-        scratch_shapes=[pltpu.VMEM(shape, jnp.float32), pltpu.VMEM(shape, jnp.float32)],
-        compiler_params=pltpu.CompilerParams(vmem_limit_bytes=32 << 20),
+        scratch_shapes=[pltpu.VMEM(shape, jnp.float32)] * 3,
+        compiler_params=pltpu.CompilerParams(vmem_limit_bytes=16 << 20),
         cost_estimate=pl.CostEstimate(flops=4 * PANEL ** 3, bytes_accessed=8 * PANEL ** 2, transcendentals=PANEL),
         name="inverse_factor",
     )(core, own, other)
 
 
-def product(weighted, panel):
+def prepare_kernel(counts_ref, barrier_ref, border_ref, along_ref, beside_ref, columns, arrived):
+    capacity = barrier_ref.shape[1]
+    copies = [
+        pltpu.make_async_copy(border_ref.at[s, :, pl.ds(0, 128)], columns.at[s], arrived.at[s]) for s in range(2)
+    ]
+    for copy in copies:
+        copy.start()
+    position = lax.broadcasted_iota(jnp.int32, (1, capacity), 1)
+    for s in range(2):
+        weights = jnp.where(position < counts_ref[s], 1.0 / barrier_ref[s:s + 1, :], 0.0)
+        copies[s].wait()
+        tiles = [jnp.transpose(columns[s, a:a + 128, :])[:TILE, :] for a in range(0, capacity, 128)]
+        panel = jnp.concatenate(tiles, axis=1)
+        weighted = panel * weights
+        for z in range(8):
+            along_ref[2 * z + s] = weighted
+        for x in range(4):
+            beside_ref[2 * x + s] = panel
+
+
+def prepare(row_counts, barrier, border):
+    capacity = border.shape[1]
+    vmem = pl.BlockSpec(memory_space=pltpu.VMEM)
+    return pl.pallas_call(
+        prepare_kernel,
+        out_shape=(
+            jax.ShapeDtypeStruct((16, TILE, capacity), jnp.float32),
+            jax.ShapeDtypeStruct((8, TILE, capacity), jnp.float32),
+        ),
+        in_specs=[pl.BlockSpec(memory_space=pltpu.SMEM), vmem, pl.BlockSpec(memory_space=pltpu.HBM)],
+        out_specs=(vmem, vmem),
+        scratch_shapes=[pltpu.VMEM((2, capacity, 128), jnp.float32), pltpu.SemaphoreType.DMA((2,))],
+        compiler_params=pltpu.CompilerParams(vmem_limit_bytes=60 << 20),
+        name="prepare",
+    )(row_counts, barrier, border)
+
+
+def block_kernel(along_ref, beside_ref, out_ref):
+    along = along_ref[...].reshape(16 * TILE, -1)
+    beside = beside_ref[...].reshape(8 * TILE, -1)
+    part = dot(along, beside, 1, 1)
+    quarter = 4 * TILE
+    for c in range(2):
+        first = part[2 * c * quarter:(2 * c + 1) * quarter]
+        second = part[(2 * c + 1) * quarter:(2 * c + 2) * quarter]
+        packed = jnp.concatenate([first, second], axis=1)
+        for y in range(8):
+            out_ref[2 * y + c] = packed
+
+
+def block_part(along, beside):
+    vmem = pl.BlockSpec(memory_space=pltpu.VMEM)
+    return pl.pallas_call(
+        block_kernel,
+        out_shape=jax.ShapeDtypeStruct((16, 4 * TILE, 16 * TILE), jnp.float32),
+        in_specs=[vmem, vmem],
+        out_specs=vmem,
+        compiler_params=pltpu.CompilerParams(vmem_limit_bytes=16 << 20),
+        name="block_part",
+    )(along, beside)
+
+
+def product(columns, panel):
     return jnp.einsum(
-        "rc,kr->ck", weighted, panel,
+        "rc,kr->ck", columns, panel,
         precision=lax.Precision.HIGH, preferred_element_type=jnp.float32,
     )
+
+
+def exchange(array, axes):
+    return lax.all_to_all(array, axes, split_axis=0, concat_axis=0, tiled=True)
 
 
 def body(border, barrier, row_counts):
     capacity = border.shape[1]
     own_cols = border.shape[2]
     n_scen = lax.axis_size("scen")
-    n_x = lax.axis_size("x")
-    n_z = lax.axis_size("z")
-    per_owner = PANEL // (n_z * n_x * 2)
     rows_owned = own_cols // n_scen
     core = lax.axis_index("core")
 
-    panel_part = jnp.transpose(border[:, :, :per_owner], (0, 2, 1))
-    to_send = jnp.broadcast_to(panel_part[None], (n_x, 2, per_owner, capacity))
-    beside = lax.all_to_all(
-        to_send.reshape(n_x * 2, per_owner, capacity), ("x", "core"), split_axis=0, concat_axis=0, tiled=True
-    ).reshape(n_x * 2 * per_owner, capacity)
-    panel = lax.all_gather(beside, "z", axis=0, tiled=True)
-
-    positions = lax.iota(jnp.int32, capacity)
-    here = lax.dynamic_index_in_dim(barrier, core, 0, keepdims=False)
-    count = lax.dynamic_index_in_dim(row_counts, core, 0, keepdims=False)
-    weights = jnp.where(positions < count, 1.0 / here, jnp.float32(0.0))
-
+    to_along, to_beside = prepare(row_counts, barrier, border)
+    along = exchange(to_along, ("z", "core"))
+    panel = lax.all_gather(along.reshape(16 * TILE, capacity), "x", axis=0, tiled=True)
+
+    beside = exchange(to_beside, ("x", "core"))
+    piece = block_part(along, beside)
+    parts = exchange(piece, ("scen", "core"))
+    copies = jnp.broadcast_to(jnp.sum(parts, axis=0), (32,) + parts.shape[1:])
+    own_half = exchange(copies, ("z", "x"))
+    other_half = lax.ppermute(own_half, "core", SWAP)
+    inverse = inverse_factor(jnp.reshape(core, (1,)), own_half, other_half)
+
+    border, _ = lax.optimization_barrier((border, piece))
     mine = lax.dynamic_index_in_dim(border, core, 0, keepdims=False)
     other = lax.ppermute(lax.dynamic_index_in_dim(border, 1 - core, 0, keepdims=False), "core", SWAP)
-
-    chip_rows = lax.dynamic_slice_in_dim(beside, lax.axis_index("x") * 2 * per_owner, 2 * per_owner, 0)
-    along = lax.all_gather(chip_rows, "z", axis=0, tiled=True)
-    block_part = jnp.einsum(
-        "qr,pr->qp", along, beside * weights[None, :],
-        precision=lax.Precision.HIGHEST, preferred_element_type=jnp.float32,
-    )
-    halves = block_part.reshape(2, 2, 4 * per_owner, 8 * per_owner)
-    halves = jnp.concatenate([halves[:, 0], halves[:, 1]], axis=-1)
-    part = halves.shape[1:]
-    parts = jnp.broadcast_to(halves[None], (n_scen, 2) + part).reshape((n_scen * 2,) + part)
-    parts = lax.all_to_all(parts, ("scen", "core"), split_axis=0, concat_axis=0, tiled=True)
-    copies = jnp.broadcast_to(jnp.sum(parts, axis=0), (n_z * n_x,) + part)
-    own_half = lax.all_to_all(copies, ("z", "x"), split_axis=0, concat_axis=0, tiled=True)
-    other_half = lax.ppermute(own_half, "core", SWAP)
-    inverse = inverse_factor(jnp.reshape(core, (1,)), own_half, other_half)
-
-    schur_mine = product(mine * weights[:, None], panel)
-    schur_other = product(other * weights[:, None], panel)
+    schur_other = product(other, panel)
+    schur_mine = product(mine, panel)
     schur_part = schur_mine + lax.ppermute(schur_other, "core", SWAP)
     owned = lax.psum_scatter(schur_part, "scen", scatter_dimension=0, tiled=True)
-    solved = dot(owned, inverse, 1, 1)
+    solved = dot(owned, inverse, 1, 0)
     return solved.reshape(1, 1, rows_owned, PANEL)
 
 

time: 149 us -> 151 us (1.013)
  the two profiles are of different devices: /device:TPU:1 before, /device:TPU:6 now
where the time goes in v3:
time: 151 us; the launch traced here: 150 us
  blocking collectives  51.2 us (34%)
  Pallas kernels  31.4 us (21%)
  waiting for transfers between devices  20.4 us (14%)
  starting transfers between devices  17.7 us (12%)
  between operations  13.5 us (9%)
  matrix products  11.8 us (8%)
  local copies, waits for them, and re-layouts  3.34 us (2%)
    all_to_all x2, blocking collectives, exchange(): return lax.all_to_all(array, axes, split_axis=0, concat_axis=0, tiled=True)  51.2 us
    pallas_call x1, Pallas kernels, inverse_factor(): pl.pallas_call(inverse_kernel, out_shape=jax.ShapeDtypeStruct(shape, jnp....  26.9 us
    all_to_all x2, waiting for transfers between devices, exchange(): return lax.all_to_all(array, axes, split_axis=0, concat_axis=0, tiled=True)  12 us
    all_to_all x2, starting transfers between devices, exchange(): return lax.all_to_all(array, axes, split_axis=0, concat_axis=0, tiled=True)  10.9 us
    dot_general x2, matrix products, product(): jnp.einsum('rc,kr->ck', columns, panel, precision=lax.Precision.HIGH, pre...  9.58 us
    reduce_scatter x1, waiting for transfers between devices, body(): lax.psum_scatter(schur_part, 'scen', scatter_dimension=0, tiled=True)  6.78 us
    pallas_call x1, Pallas kernels, prepare(): pl.pallas_call(prepare_kernel, out_shape=(jax.ShapeDtypeStruct((16, TILE,...  3.61 us
  transfers between devices with their start and end apart: 7, of which 4 were waited for; matrix products, arithmetic and copies ran while one was open for 8% of the time, Pallas kernels for 18%

profile of v3, /device:TPU:6, one launch (start us, length us, event | category | flops | bytes accessed | tf_op | source)
XLA Modules:
  0.0 150.2 jit_solution(1794073115132270750)
XLA Ops:
  6.5 0.0 copy-start.1
  6.5 0.0 all-gather.2.cloned.1.call-start
  6.5 3.6 %prepare.1 = (f32[16,8,1536]{2,1,0:T(8,128)}, f32[8,8,1536]{2,1,0:T(8,128)}) custom-call(s32[2]{0:T(128)} %counts_ref.1, f32[2,1536]{1,0:T(2,128)} %barrier_ref.1, f32[2,1536,256]{2,1,0:T(8,128)} %border_ref.1), custom_call_target="tpu_custom_call" | custom-call | tf_op jit(solution)/shard_map/prepare/pallas_call | solution.py:146
  10.2 32.9 %all_to_all.20.along_ref = f32[16,8,1536]{2,1,0:T(8,128)} all-to-all(f32[16,8,1536]{2,1,0:T(8,128)} %get-tuple-element.8), channel_id=1, replica_groups=mesh['scen'=8,'z'=8,'x'=4,'core'=2] {'z','core'}, dimensions={0} | all-to-all | bytes 1572864 | tf_op jit(solution)/shard_map/all_to_all | solution.py:193
  43.1 0.0 all-gather.2.cloned.1.call-update
  43.1 5.3 %all-to-all-start.1 = ((f32[8,8,1536]{2,1,0:T(8,128)}), f32[8,8,1536]{2,1,0:T(8,128)S(1)}, u32[]{:S(2)}, u32[]{:S(2)}) async-start(f32[8,8,1536]{2,1,0:T(8,128)} %get-tuple-element.9), calls=%async_computation.1 | async-start | bytes 786432 | tf_op jit(solution)/shard_map/all_to_all | solution.py:193
  48.5 6.9 %all-to-all-done.1.beside_ref = f32[8,8,1536]{2,1,0:T(8,128)S(1)} async-done(((f32[8,8,1536]{2,1,0:T(8,128)}), f32[8,8,1536]{2,1,0:T(8,128)S(1)}, u32[]{:S(2)}, u32[]{:S(2)}) %all-to-all-start.1) | async-done | bytes 393248 | tf_op jit(solution)/shard_map/all_to_all | solution.py:193
  55.3 0.0 copy-start
  55.3 1.2 copy-done
  56.5 0.8 block_part.1
  57.4 0.0 copy-done.1
  57.4 1.3 dynamic-slice_bitcast_fusion
  58.7 1.9 %collective-permute-start = (f32[1536,256]{1,0:T(8,128)}, f32[1536,256]{1,0:T(8,128)S(1)}, u32[]{:S(2)}, u32[]{:S(2)}) collective-permute-start(f32[1536,256]{1,0:T(8,128)} %dynamic-slice_bitcast_fusion), channel_id=1, source_target_pairs={{0,1},{1,0},{2,3},{3,2},{4,5},{5,4},{6,7},{7,6},{8,9},{9,8},{10,11... | collective-permute-start | bytes 4718600 | tf_op jit(solution)/shard_map/ppermute | solution.py:217
  60.6 18.3 %all_to_all.21 = f32[16,32,128]{2,1,0:T(8,128)S(1)} all-to-all(f32[16,32,128]{2,1,0:T(8,128)S(1)} %block_part.1), channel_id=1, replica_groups=mesh['scen'=8,'z'=8,'x'=4,'core'=2] {'scen','core'}, dimensions={0} | all-to-all | bytes 524288 | tf_op jit(solution)/shard_map/all_to_all | solution.py:193
  78.9 0.9 broadcast_in_dim.3
  79.8 5.6 %all-to-all-start.3 = ((f32[32,32,128]{2,1,0:T(8,128)}), f32[32,32,128]{2,1,0:T(8,128)S(1)}, u32[]{:S(2)}, u32[]{:S(2)}) async-start(f32[32,32,128]{2,1,0:T(8,128)} %broadcast_in_dim.3), calls=%async_computation.4 | async-start | bytes 1048576 | tf_op jit(solution)/shard_map/all_to_all | solution.py:193
  85.4 0.0 reduce-scatter.2.cloned.1.call-start
  85.4 0.0 collective-permute-done
  85.4 0.0 all-gather.2.cloned.1.call-done
  85.5 4.5 %fusion.4 = f32[256,512]{1,0:T(8,128)S(1)} fusion(f32[1536,256]{1,0:T(8,128)S(1)} %collective-permute-done, f32[512,1536]{1,0:T(8,128)} %all-gather.2.cloned.1.call-done), kind=kOutput, calls=%fused_computation.6 | convolution fusion | flops 1207959552 | bytes 5242880 | tf_op jit(solution)/shard_map/rc,kr->ck/dot_general | solution.py:186
  90.0 2.6 %collective-permute-start.1 = (f32[256,512]{1,0:T(8,128)S(1)}, f32[256,512]{1,0:T(8,128)S(1)}, u32[]{:S(2)}, u32[]{:S(2)}) collective-permute-start(f32[256,512]{1,0:T(8,128)S(1)} %fusion.4), channel_id=1, source_target_pairs={{0,1},{1,0},{2,3},{3,2},{4,5},{5,4},{6,7},{7,6},{8,9},{9,8},{10,11... | collective-permute-start | bytes 1572872 | tf_op jit(solution)/shard_map/ppermute | solution.py:220
  92.6 5.0 %fusion = f32[256,512]{1,0:T(8,128)S(1)} fusion(f32[512,1536]{1,0:T(8,128)} %all-gather.2.cloned.1.call-done, f32[2,1536,256]{2,1,0:T(8,128)} %border_ref.1, s32[]{:T(128)S(6)} %select_n.7), kind=kOutput, calls=%fused_computation | convolution fusion | flops 1207959552 | bytes 5242884 | tf_op jit(solution)/shard_map/rc,kr->ck/dot_general | solution.py:186
  97.6 0.0 collective-permute-done.1
  97.7 0.9 add.15
  98.5 0.0 reduce-scatter.2.cloned.1.call-update
  98.5 5.1 %all-to-all-done.3.own_ref = f32[32,32,128]{2,1,0:T(8,128)S(1)} async-done(((f32[32,32,128]{2,1,0:T(8,128)}), f32[32,32,128]{2,1,0:T(8,128)S(1)}, u32[]{:S(2)}, u32[]{:S(2)}) %all-to-all-start.3) | async-done | bytes 524320 | tf_op jit(solution)/shard_map/all_to_all | solution.py:193
  103.7 2.2 %collective-permute-start.2 = (f32[32,32,128]{2,1,0:T(8,128)S(1)}, f32[32,32,128]{2,1,0:T(8,128)S(1)}, u32[]{:S(2)}, u32[]{:S(2)}) collective-permute-start(f32[32,32,128]{2,1,0:T(8,128)S(1)} %all-to-all-done.3.own_ref), channel_id=1, source_target_pairs={{0,1},{1,0},{2,3},{3,2},{4,5},{5,4},{6,7},{7,6},{8,9},{9,8},{10,11... | collective-permute-start | bytes 1572872 | tf_op jit(solution)/shard_map/ppermute | solution.py:212
  105.9 1.6 %collective-permute-done.2.other_ref = f32[32,32,128]{2,1,0:T(8,128)S(1)} collective-permute-done((f32[32,32,128]{2,1,0:T(8,128)S(1)}, f32[32,32,128]{2,1,0:T(8,128)S(1)}, u32[]{:S(2)}, u32[]{:S(2)}) %collective-permute-start.2) | collective-permute-done | bytes 524320 | tf_op jit(solution)/shard_map/ppermute | solution.py:212
  107.5 26.9 %inverse_factor.1 = f32[512,512]{1,0:T(8,128)S(1)} custom-call(s32[1]{0:T(128)} %bitcast.3.core_ref, f32[32,32,128]{2,1,0:T(8,128)S(1)} %all-to-all-done.3.own_ref, f32[32,32,128]{2,1,0:T(8,128)S(1)} %collective-permute-done.2.other_ref), custom_call_target="tpu_custom_call" | custom-call | flops 536870912 | bytes 2097152 | tf_op jit(solution)/shard_map/inverse_factor/pallas_call | solution.py:111
  134.4 6.8 %reduce-scatter.2.cloned.1.call-done = f32[32,512]{1,0:T(8,128)} async-done(((f32[256,512]{1,0:T(8,128)}), f32[32,512]{1,0:T(8,128)}) %reduce-scatter.2.cloned.1.call-update) | async-done | bytes 65552 | tf_op jit(solution)/shard_map/reduce_scatter | solution.py:221
  141.2 2.2 %convolution_bitcast_fusion = f32[1,1,32,512]{3,2,1,0:T(8,128)} fusion(f32[32,512]{1,0:T(8,128)} %reduce-scatter.2.cloned.1.call-done, f32[512,512]{1,0:T(8,128)S(1)} %inverse_factor.1), kind=kOutput, calls=%fused_computation.4 | convolution fusion | flops 100663296 | bytes 1179648 | tf_op jit(solution)/shard_map/dot_general | solution.py:16
  (1 shorter events, 0.0 us)
Async XLA Ops:
  6.5 50.9 %copy-start.1 = (f32[2,1536,256]{2,1,0:T(8,128)S(1)}, f32[2,1536,256]{2,1,0:T(8,128)}, u32[]{:S(2)}) copy-start(f32[2,1536,256]{2,1,0:T(8,128)} %border_ref.1) | copy-start | bytes 9437188
  6.5 78.9 %all-gather.2.cloned.1.call-start = ((), (), s32[]{:S(2)}) async-start(), calls=%async_computation.5 | async-start | bytes 3932160 | tf_op jit(solution)/shard_map/all_gather | solution.py:205
  43.1 12.2 %all-to-all-start.1 = ((f32[8,8,1536]{2,1,0:T(8,128)}), f32[8,8,1536]{2,1,0:T(8,128)S(1)}, u32[]{:S(2)}, u32[]{:S(2)}) async-start(f32[8,8,1536]{2,1,0:T(8,128)} %get-tuple-element.9), calls=%async_computation.1 | async-start | bytes 786432 | tf_op jit(solution)/shard_map/all_to_all | solution.py:193
  55.3 1.2 copy-start
  58.7 26.8 %collective-permute-start = (f32[1536,256]{1,0:T(8,128)}, f32[1536,256]{1,0:T(8,128)S(1)}, u32[]{:S(2)}, u32[]{:S(2)}) collective-permute-start(f32[1536,256]{1,0:T(8,128)} %dynamic-slice_bitcast_fusion), channel_id=1, source_target_pairs={{0,1},{1,0},{2,3},{3,2},{4,5},{5,4},{6,7},{7,6},{8,9},{9,8},{10,11... | collective-permute-start | bytes 4718600 | tf_op jit(solution)/shard_map/ppermute | solution.py:217
  79.8 23.9 %all-to-all-start.3 = ((f32[32,32,128]{2,1,0:T(8,128)}), f32[32,32,128]{2,1,0:T(8,128)S(1)}, u32[]{:S(2)}, u32[]{:S(2)}) async-start(f32[32,32,128]{2,1,0:T(8,128)} %broadcast_in_dim.3), calls=%async_computation.4 | async-start | bytes 1048576 | tf_op jit(solution)/shard_map/all_to_all | solution.py:193
  85.4 55.8 %reduce-scatter.2.cloned.1.call-start = ((), (), s32[]{:S(2)}) async-start(), calls=%async_computation.6 | async-start | bytes 589824 | tf_op jit(solution)/shard_map/reduce_scatter | solution.py:221
  90.0 7.6 %collective-permute-start.1 = (f32[256,512]{1,0:T(8,128)S(1)}, f32[256,512]{1,0:T(8,128)S(1)}, u32[]{:S(2)}, u32[]{:S(2)}) collective-permute-start(f32[256,512]{1,0:T(8,128)S(1)} %fusion.4), channel_id=1, source_target_pairs={{0,1},{1,0},{2,3},{3,2},{4,5},{5,4},{6,7},{7,6},{8,9},{9,8},{10,11... | collective-permute-start | bytes 1572872 | tf_op jit(solution)/shard_map/ppermute | solution.py:220
  103.7 3.8 %collective-permute-start.2 = (f32[32,32,128]{2,1,0:T(8,128)S(1)}, f32[32,32,128]{2,1,0:T(8,128)S(1)}, u32[]{:S(2)}, u32[]{:S(2)}) collective-permute-start(f32[32,32,128]{2,1,0:T(8,128)S(1)} %all-to-all-done.3.own_ref), channel_id=1, source_target_pairs={{0,1},{1,0},{2,3},{3,2},{4,5},{5,4},{6,7},{7,6},{8,9},{9,8},{10,11... | collective-permute-start | bytes 1572872 | tf_op jit(solution)/shard_map/ppermute | solution.py:212
Sparse Core Ops, SparseCore 0:
  43.2 40.6 all-gather.1
  98.7 42.4 reduce-scatter.1

commit v4 on v3

--- a/solution.py
+++ b/solution.py
@@ -20,12 +20,25 @@
 
 
 def reciprocal(x):
-    first = pltpu.reciprocal(x, approx=True)
-    return first * (2.0 - x * first)
+    return pltpu.reciprocal(x, approx=True)
 
 
 def spread(piece):
     return jnp.broadcast_to(piece, (TILE, BLOCK))
+
+
+def rows_of(values):
+    row_of = lax.broadcasted_iota(jnp.int32, (TILE, BLOCK), 0)
+    tile = values[0]
+    for r in range(1, TILE):
+        tile = jnp.where(row_of == r, values[r], tile)
+    return tile
+
+
+def three_parts(x):
+    first = x.astype(jnp.bfloat16).astype(jnp.float32)
+    second = (x - first).astype(jnp.bfloat16).astype(jnp.float32)
+    return first, second, x - first - second
 
 
 def factor_inverse(diagonal):
@@ -34,42 +47,66 @@
     col_of = lax.broadcasted_iota(jnp.int32, (TILE, BLOCK), 1)
     left = [diagonal[TILE * t:TILE * (t + 1), :] for t in range(count)]
     right = [jnp.where(col_of == row_of + TILE * t, jnp.float32(1.0), jnp.float32(0.0)) for t in range(count)]
-    rows = []
+    done = []
     for s in range(count):
         own = [spread(left[s][:, TILE * s + c:TILE * s + c + 1]) for c in range(TILE)]
         rest = [[spread(own[c][r:r + 1, :]) for c in range(r + 1)] for r in range(TILE)]
-        up_left = [spread(left[s][r:r + 1, :]) for r in range(TILE)]
-        up_right = [spread(right[s][r:r + 1, :]) for r in range(TILE)]
-        inverse = [None] * TILE
+        up = [[spread(side[s][r:r + 1, :]) for r in range(TILE)] for side in (left, right)]
         factor = [[None] * TILE for _ in range(TILE)]
-        for c in range(TILE):
-            inverse[c] = reciprocal(rest[c][c])
-            for r in range(c + 1, TILE):
-                factor[r][c] = rest[r][c] * inverse[c]
-            for r in range(c + 1, TILE):
-                for q in range(c + 1, r + 1):
-                    rest[r][q] = rest[r][q] - factor[r][c] * rest[q][c]
-                up_left[r] = up_left[r] - factor[r][c] * up_left[c]
-                up_right[r] = up_right[r] - factor[r][c] * up_right[c]
-        if s < count - 1:
-            down_left = [None] * TILE
-            down_right = [None] * TILE
-            for c in range(TILE - 1, -1, -1):
-                down_left[c] = inverse[c] * up_left[c]
-                down_right[c] = inverse[c] * up_right[c]
-                for r in range(c + 1, TILE):
-                    down_left[c] = down_left[c] - factor[r][c] * down_left[r]
-                    down_right[c] = down_right[c] - factor[r][c] * down_right[r]
-            for t in range(s + 1, count):
-                across = [spread(left[t][:, TILE * s + c:TILE * s + c + 1]) for c in range(TILE)]
-                for c in range(TILE - 1, -1, -1):
-                    left[t] = left[t] - across[c] * down_left[c]
-                    right[t] = right[t] - across[c] * down_right[c]
-        scaled = lax.rsqrt(rest[0][0]) * up_right[0]
-        for r in range(1, TILE):
-            scaled = jnp.where(row_of == r, lax.rsqrt(rest[r][r]) * up_right[r], scaled)
-        rows.append(scaled)
-    return jnp.concatenate(rows, axis=0)
+        pivots = {}
+        scaled = [None] * TILE
+        for c in range(0, TILE, 2):
+            a, b, d = rest[c][c], rest[c + 1][c], rest[c + 1][c + 1]
+            determinant = a * d - b * b
+            over = reciprocal(determinant)
+            pivots[c] = (d * over, -(b * over), a * over)
+            for r in range(c + 2, TILE):
+                factor[r][c] = rest[r][c] * pivots[c][0] + rest[r][c + 1] * pivots[c][1]
+                factor[r][c + 1] = rest[r][c] * pivots[c][1] + rest[r][c + 1] * pivots[c][2]
+            for r in range(c + 2, TILE):
+                for q in range(c + 2, r + 1):
+                    rest[r][q] = rest[r][q] - (factor[r][c] * rest[q][c] + factor[r][c + 1] * rest[q][c + 1])
+                for rows in up:
+                    rows[r] = rows[r] - (factor[r][c] * rows[c] + factor[r][c + 1] * rows[c + 1])
+            over_a = reciprocal(a)
+            scaled[c] = lax.rsqrt(a) * up[1][c]
+            scaled[c + 1] = lax.rsqrt(determinant * over_a) * (up[1][c + 1] - (b * over_a) * up[1][c])
+        done.append(rows_of(scaled))
+        if s == count - 1:
+            break
+        down = []
+        for rows in up:
+            solved = [None] * TILE
+            for c in range(TILE - 2, -1, -2):
+                p, q, t = pivots[c]
+                one = p * rows[c] + q * rows[c + 1]
+                two = q * rows[c] + t * rows[c + 1]
+                for r in range(TILE - 1, c + 1, -1):
+                    one = one - factor[r][c] * solved[r]
+                    two = two - factor[r][c + 1] * solved[r]
+                solved[c], solved[c + 1] = one, two
+            down.append(solved)
+        across = [spread(left[s + 1][:, TILE * s + c:TILE * s + c + 1]) for c in range(TILE)]
+        for side, solved in zip((left, right), down):
+            terms = [across[c] * solved[c] for c in range(TILE)]
+            while len(terms) > 1:
+                terms = [terms[i] + terms[i + 1] for i in range(0, len(terms), 2)]
+            side[s + 1] = side[s + 1] - terms[0]
+        if s + 2 < count:
+            one, two, three = three_parts(left[s])
+            stacked = jnp.concatenate([one, one, two, two, one, three], axis=0).astype(jnp.bfloat16)
+            updates = []
+            for solved in down:
+                one, two, three = three_parts(rows_of(solved))
+                updates.append(jnp.concatenate([one, two, one, two, three, one], axis=0).astype(jnp.bfloat16))
+            update = lax.dot_general(
+                stacked, jnp.concatenate(updates, axis=1), (((0,), (0,)), ((), ())),
+                preferred_element_type=jnp.float32,
+            )
+            for t in range(s + 2, count):
+                left[t] = left[t] - update[TILE * t:TILE * (t + 1), :BLOCK]
+                right[t] = right[t] - update[TILE * t:TILE * (t + 1), BLOCK:]
+    return jnp.concatenate(done, axis=0)
 
 
 def inverse_kernel(core_ref, own_ref, other_ref, out_ref, rest, sums, lower):
@@ -207,18 +244,19 @@
     beside = exchange(to_beside, ("x", "core"))
     piece = block_part(along, beside)
     parts = exchange(piece, ("scen", "core"))
-    copies = jnp.broadcast_to(jnp.sum(parts, axis=0), (32,) + parts.shape[1:])
+    summed = jnp.sum(parts, axis=0)
+    copies = jnp.broadcast_to(summed, (32,) + summed.shape)
     own_half = exchange(copies, ("z", "x"))
     other_half = lax.ppermute(own_half, "core", SWAP)
     inverse = inverse_factor(jnp.reshape(core, (1,)), own_half, other_half)
 
-    border, _ = lax.optimization_barrier((border, piece))
+    border, _ = lax.optimization_barrier((border, summed))
     mine = lax.dynamic_index_in_dim(border, core, 0, keepdims=False)
     other = lax.ppermute(lax.dynamic_index_in_dim(border, 1 - core, 0, keepdims=False), "core", SWAP)
     schur_other = product(other, panel)
     schur_mine = product(mine, panel)
     schur_part = schur_mine + lax.ppermute(schur_other, "core", SWAP)
-    owned = lax.psum_scatter(schur_part, "scen", scatter_dimension=0, tiled=True)
+    owned = jnp.sum(exchange(schur_part.reshape(n_scen, rows_owned, PANEL), "scen"), axis=0)
     solved = dot(owned, inverse, 1, 0)
     return solved.reshape(1, 1, rows_owned, PANEL)
 

time: 151 us -> 140 us (0.927)
  the two profiles are of different devices: /device:TPU:6 before, /device:TPU:1 now
where the time goes in v4:
time: 140 us
  blocking collectives  47.6 us (34%)
  starting transfers between devices  24 us (17%)
  Pallas kernels  22.5 us (16%)
  waiting for transfers between devices  16.8 us (12%)
  between operations  13.5 us (10%)
  matrix products  10.9 us (8%)
  local copies, waits for them, and re-layouts  3.27 us (2%)
    all_to_all x2, blocking collectives, exchange(): return lax.all_to_all(array, axes, split_axis=0, concat_axis=0, tiled=True)  47.6 us
    pallas_call x1, Pallas kernels, inverse_factor(): pl.pallas_call(inverse_kernel, out_shape=jax.ShapeDtypeStruct(shape, jnp....  17.6 us
    all_to_all x3, starting transfers between devices, exchange(): return lax.all_to_all(array, axes, split_axis=0, concat_axis=0, tiled=True)  15.4 us
    all_to_all x3, waiting for transfers between devices, exchange(): return lax.all_to_all(array, axes, split_axis=0, concat_axis=0, tiled=True)  15.4 us
    dot_general x2, matrix products, product(): jnp.einsum('rc,kr->ck', columns, panel, precision=lax.Precision.HIGH, pre...  9.58 us
    ppermute x1, starting transfers between devices, body(): other_half = lax.ppermute(own_half, 'core', SWAP)  4.21 us
    pallas_call x1, Pallas kernels, prepare(): pl.pallas_call(prepare_kernel, out_shape=(jax.ShapeDtypeStruct((16, TILE,...  3.36 us
  transfers between devices with their start and end apart: 7, of which 3 were waited for; matrix products, arithmetic and copies ran while one was open for 9% of the time, Pallas kernels for 14%

profile of v4, /device:TPU:1, one launch (start us, length us, event | category | flops | bytes accessed | tf_op | source)
XLA Modules:
  0.0 139.5 jit_solution(220938580122299381)
XLA Ops:
  6.5 0.0 all-gather.2.cloned.1.call-start
  6.5 3.4 %prepare.1 = (f32[16,8,1536]{2,1,0:T(8,128)}, f32[8,8,1536]{2,1,0:T(8,128)}) custom-call(s32[2]{0:T(128)} %counts_ref.1, f32[2,1536]{1,0:T(2,128)} %barrier_ref.1, f32[2,1536,256]{2,1,0:T(8,128)} %border_ref.1), custom_call_target="tpu_custom_call" | custom-call | tf_op jit(solution)/shard_map/prepare/pallas_call | solution.py:183
  9.9 0.0 copy-start.1
  9.9 35.1 %all_to_all.25.along_ref = f32[16,8,1536]{2,1,0:T(8,128)} all-to-all(f32[16,8,1536]{2,1,0:T(8,128)} %get-tuple-element.8), channel_id=1, replica_groups=mesh['scen'=8,'z'=8,'x'=4,'core'=2] {'z','core'}, dimensions={0} | all-to-all | bytes 1572864 | tf_op jit(solution)/shard_map/all_to_all | solution.py:230
  45.1 0.0 all-gather.2.cloned.1.call-update
  45.1 12.5 %all_to_all.26.beside_ref = f32[8,8,1536]{2,1,0:T(8,128)S(1)} all-to-all(f32[8,8,1536]{2,1,0:T(8,128)} %get-tuple-element.9), channel_id=1, replica_groups=mesh['scen'=8,'z'=8,'x'=4,'core'=2] {'x','core'}, dimensions={0} | all-to-all | bytes 786432 | tf_op jit(solution)/shard_map/all_to_all | solution.py:230
  57.6 0.0 copy-start
  57.6 1.1 copy-done
  58.7 1.5 %block_part.1 = f32[16,32,128]{2,1,0:T(8,128)} custom-call(f32[16,8,1536]{2,1,0:T(8,128)S(1)} %copy-done, f32[8,8,1536]{2,1,0:T(8,128)S(1)} %all_to_all.26.beside_ref), custom_call_target="tpu_custom_call" | custom-call | tf_op jit(solution)/shard_map/block_part/pallas_call | solution.py:212
  60.3 8.0 %all-to-all-start.2 = ((f32[16,32,128]{2,1,0:T(8,128)}), f32[16,32,128]{2,1,0:T(8,128)S(1)}, u32[]{:S(2)}, u32[]{:S(2)}) async-start(f32[16,32,128]{2,1,0:T(8,128)} %block_part.1), calls=%async_computation.2 | async-start | bytes 524288 | tf_op jit(solution)/shard_map/all_to_all | solution.py:230
  68.3 11.7 %all-to-all-done.2 = f32[16,32,128]{2,1,0:T(8,128)S(1)} async-done(((f32[16,32,128]{2,1,0:T(8,128)}), f32[16,32,128]{2,1,0:T(8,128)S(1)}, u32[]{:S(2)}, u32[]{:S(2)}) %all-to-all-start.2) | async-done | bytes 262176 | tf_op jit(solution)/shard_map/all_to_all | solution.py:230
  80.1 0.0 copy-done.1
  80.1 1.3 dynamic-slice_bitcast_fusion
  81.3 1.9 %collective-permute-start = (f32[1536,256]{1,0:T(8,128)}, f32[1536,256]{1,0:T(8,128)S(1)}, u32[]{:S(2)}, u32[]{:S(2)}) collective-permute-start(f32[1536,256]{1,0:T(8,128)} %dynamic-slice_bitcast_fusion), channel_id=1, source_target_pairs={{0,1},{1,0},{2,3},{3,2},{4,5},{5,4},{6,7},{7,6},{8,9},{9,8},{10,11... | collective-permute-start | bytes 4718600 | tf_op jit(solution)/shard_map/ppermute | solution.py:255
  83.2 0.9 broadcast_in_dim.3
  84.1 3.9 %all-to-all-start.4 = ((f32[32,32,128]{2,1,0:T(8,128)}), f32[32,32,128]{2,1,0:T(8,128)S(1)}, u32[]{:S(2)}, u32[]{:S(2)}) async-start(f32[32,32,128]{2,1,0:T(8,128)} %broadcast_in_dim.3), calls=%async_computation.4 | async-start | bytes 1048576 | tf_op jit(solution)/shard_map/all_to_all | solution.py:230
  88.0 0.0 collective-permute-done
  88.0 0.0 all-gather.2.cloned.1.call-done
  88.0 4.5 %fusion.4 = f32[256,512]{1,0:T(8,128)S(1)} fusion(f32[1536,256]{1,0:T(8,128)S(1)} %collective-permute-done, f32[512,1536]{1,0:T(8,128)} %all-gather.2.cloned.1.call-done), kind=kOutput, calls=%fused_computation.6 | convolution fusion | flops 1207959552 | bytes 5242880 | tf_op jit(solution)/shard_map/rc,kr->ck/dot_general | solution.py:223
  92.6 2.4 %collective-permute-start.1 = (f32[256,512]{1,0:T(8,128)S(1)}, f32[256,512]{1,0:T(8,128)S(1)}, u32[]{:S(2)}, u32[]{:S(2)}) collective-permute-start(f32[256,512]{1,0:T(8,128)S(1)} %fusion.4), channel_id=1, source_target_pairs={{0,1},{1,0},{2,3},{3,2},{4,5},{5,4},{6,7},{7,6},{8,9},{9,8},{10,11... | collective-permute-start | bytes 1572872 | tf_op jit(solution)/shard_map/ppermute | solution.py:258
  95.0 5.0 %fusion = f32[256,512]{1,0:T(8,128)S(1)} fusion(f32[512,1536]{1,0:T(8,128)} %all-gather.2.cloned.1.call-done, f32[2,1536,256]{2,1,0:T(8,128)} %border_ref.1, s32[]{:T(128)S(6)} %select_n.7), kind=kOutput, calls=%fused_computation | convolution fusion | flops 1207959552 | bytes 5242884 | tf_op jit(solution)/shard_map/rc,kr->ck/dot_general | solution.py:223
  100.0 0.0 collective-permute-done.1
  100.1 0.9 add.13
  100.9 3.7 %all-to-all-done.4.own_ref = f32[32,32,128]{2,1,0:T(8,128)S(1)} async-done(((f32[32,32,128]{2,1,0:T(8,128)}), f32[32,32,128]{2,1,0:T(8,128)S(1)}, u32[]{:S(2)}, u32[]{:S(2)}) %all-to-all-start.4) | async-done | bytes 524320 | tf_op jit(solution)/shard_map/all_to_all | solution.py:230
  104.6 3.5 %all-to-all-start.3 = ((f32[8,32,512]{2,1,0:T(8,128)}), f32[8,32,512]{2,1,0:T(8,128)S(1)}, u32[]{:S(2)}, u32[]{:S(2)}) async-start(f32[8,32,512]{2,1,0:T(8,128)} %bitcast.3), calls=%async_computation.3 | async-start | bytes 1048576 | tf_op jit(solution)/shard_map/all_to_all | solution.py:230
  108.1 4.2 %collective-permute-start.2 = (f32[32,32,128]{2,1,0:T(8,128)S(1)}, f32[32,32,128]{2,1,0:T(8,128)S(1)}, u32[]{:S(2)}, u32[]{:S(2)}) collective-permute-start(f32[32,32,128]{2,1,0:T(8,128)S(1)} %all-to-all-done.4.own_ref), channel_id=1, source_target_pairs={{0,1},{1,0},{2,3},{3,2},{4,5},{5,4},{6,7},{7,6},{8,9},{9,8},{10,11... | collective-permute-start | bytes 1572872 | tf_op jit(solution)/shard_map/ppermute | solution.py:250
  112.3 1.3 collective-permute-done.2.other_ref
  113.7 17.6 %inverse_factor.1 = f32[512,512]{1,0:T(8,128)S(1)} custom-call(s32[1]{0:T(128)} %bitcast.4.core_ref, f32[32,32,128]{2,1,0:T(8,128)S(1)} %all-to-all-done.4.own_ref, f32[32,32,128]{2,1,0:T(8,128)S(1)} %collective-permute-done.2.other_ref), custom_call_target="tpu_custom_call" | custom-call | flops 536870912 | bytes 2097152 | tf_op jit(solution)/shard_map/inverse_factor/pallas_call | solution.py:148
  131.3 0.0 all-to-all-done.3
  131.4 1.3 convolution_bitcast_fusion
  (2 shorter events, 0.1 us)
Async XLA Ops:
  6.5 81.5 %all-gather.2.cloned.1.call-start = ((), (), s32[]{:S(2)}) async-start(), calls=%async_computation.5 | async-start | bytes 3932160 | tf_op jit(solution)/shard_map/all_gather | solution.py:242
  9.9 70.2 %copy-start.1 = (f32[2,1536,256]{2,1,0:T(8,128)S(1)}, f32[2,1536,256]{2,1,0:T(8,128)}, u32[]{:S(2)}) copy-start(f32[2,1536,256]{2,1,0:T(8,128)} %border_ref.1) | copy-start | bytes 9437188
  57.6 1.1 copy-start
  60.3 19.8 %all-to-all-start.2 = ((f32[16,32,128]{2,1,0:T(8,128)}), f32[16,32,128]{2,1,0:T(8,128)S(1)}, u32[]{:S(2)}, u32[]{:S(2)}) async-start(f32[16,32,128]{2,1,0:T(8,128)} %block_part.1), calls=%async_computation.2 | async-start | bytes 524288 | tf_op jit(solution)/shard_map/all_to_all | solution.py:230
  81.3 6.7 %collective-permute-start = (f32[1536,256]{1,0:T(8,128)}, f32[1536,256]{1,0:T(8,128)S(1)}, u32[]{:S(2)}, u32[]{:S(2)}) collective-permute-start(f32[1536,256]{1,0:T(8,128)} %dynamic-slice_bitcast_fusion), channel_id=1, source_target_pairs={{0,1},{1,0},{2,3},{3,2},{4,5},{5,4},{6,7},{7,6},{8,9},{9,8},{10,11... | collective-permute-start | bytes 4718600 | tf_op jit(solution)/shard_map/ppermute | solution.py:255
  84.1 20.5 %all-to-all-start.4 = ((f32[32,32,128]{2,1,0:T(8,128)}), f32[32,32,128]{2,1,0:T(8,128)S(1)}, u32[]{:S(2)}, u32[]{:S(2)}) async-start(f32[32,32,128]{2,1,0:T(8,128)} %broadcast_in_dim.3), calls=%async_computation.4 | async-start | bytes 1048576 | tf_op jit(solution)/shard_map/all_to_all | solution.py:230
  92.6 7.5 %collective-permute-start.1 = (f32[256,512]{1,0:T(8,128)S(1)}, f32[256,512]{1,0:T(8,128)S(1)}, u32[]{:S(2)}, u32[]{:S(2)}) collective-permute-start(f32[256,512]{1,0:T(8,128)S(1)} %fusion.4), channel_id=1, source_target_pairs={{0,1},{1,0},{2,3},{3,2},{4,5},{5,4},{6,7},{7,6},{8,9},{9,8},{10,11... | collective-permute-start | bytes 1572872 | tf_op jit(solution)/shard_map/ppermute | solution.py:258
  104.6 26.7 %all-to-all-start.3 = ((f32[8,32,512]{2,1,0:T(8,128)}), f32[8,32,512]{2,1,0:T(8,128)S(1)}, u32[]{:S(2)}, u32[]{:S(2)}) async-start(f32[8,32,512]{2,1,0:T(8,128)} %bitcast.3), calls=%async_computation.3 | async-start | bytes 1048576 | tf_op jit(solution)/shard_map/all_to_all | solution.py:230
  108.1 5.6 %collective-permute-start.2 = (f32[32,32,128]{2,1,0:T(8,128)S(1)}, f32[32,32,128]{2,1,0:T(8,128)S(1)}, u32[]{:S(2)}, u32[]{:S(2)}) collective-permute-start(f32[32,32,128]{2,1,0:T(8,128)S(1)} %all-to-all-done.4.own_ref), channel_id=1, source_target_pairs={{0,1},{1,0},{2,3},{3,2},{4,5},{5,4},{6,7},{7,6},{8,9},{9,8},{10,11... | collective-permute-start | bytes 1572872 | tf_op jit(solution)/shard_map/ppermute | solution.py:250
Sparse Core Ops, SparseCore 0:
  45.2 41.4 all-gather.1

commit v5 on v4

--- a/solution.py
+++ b/solution.py
@@ -10,6 +10,8 @@
 TILE = 8
 COL = ("z", "x", "core")
 SWAP = [(0, 1), (1, 0)]
+AHEAD = [(x, (x + 1) % 4) for x in range(4)]
+BEHIND = [(x, (x + 3) % 4) for x in range(4)]
 
 
 def dot(a, b, dim_a, dim_b):
@@ -109,8 +111,8 @@
     return jnp.concatenate(done, axis=0)
 
 
-def inverse_kernel(core_ref, own_ref, other_ref, out_ref, rest, sums, lower):
-    core = core_ref[0]
+def inverse_kernel(place_ref, own_ref, other_ref, out_ref, rest, sums, lower):
+    core = place_ref[0]
     for half_ref, half in ((own_ref, core), (other_ref, 1 - core)):
         for x in range(4):
             for k in range(2):
@@ -134,16 +136,20 @@
             upper = dot(inverse, rest[a:b, b:PANEL], 1, 0)
             rest[b:PANEL, b:PANEL] = rest[b:PANEL, b:PANEL] - dot(upper, upper, 0, 0)
             sums[b:PANEL, 0:b] = sums[b:PANEL, 0:b] + dot(upper, lower[a:b, 0:b], 0, 0)
+    slots = []
+    for x in range(4):
+        ahead = lax.rem(x - place_ref[1] + 4, 4)
+        slots.append(jnp.where(ahead == 0, 0, jnp.where(ahead == 3, 1, ahead + 1)))
     for k in range(0, PANEL, BLOCK):
         for a in range(0, PANEL, BLOCK):
             turned = jnp.transpose(lower[a:a + BLOCK, k:k + BLOCK]) if a >= k else jnp.zeros((BLOCK, BLOCK), jnp.float32)
             for piece in range(0, BLOCK, 16):
                 z, x = divmod((k + piece) // 16, 4)
-                to = 128 * x + 16 * z
-                out_ref[to:to + 16, a:a + BLOCK] = turned[piece:piece + 16, :]
-
-
-def inverse_factor(core, own, other):
+                to = pl.multiple_of(slots[x] * 128 + 16 * z, 16)
+                out_ref[pl.ds(to, 16), a:a + BLOCK] = turned[piece:piece + 16, :]
+
+
+def inverse_factor(place, own, other):
     shape = (PANEL, PANEL)
     return pl.pallas_call(
         inverse_kernel,
@@ -154,7 +160,7 @@
         compiler_params=pltpu.CompilerParams(vmem_limit_bytes=16 << 20),
         cost_estimate=pl.CostEstimate(flops=4 * PANEL ** 3, bytes_accessed=8 * PANEL ** 2, transcendentals=PANEL),
         name="inverse_factor",
-    )(core, own, other)
+    )(place, own, other)
 
 
 def prepare_kernel(counts_ref, barrier_ref, border_ref, along_ref, beside_ref, columns, arrived):
@@ -173,8 +179,7 @@
         weighted = panel * weights
         for z in range(8):
             along_ref[2 * z + s] = weighted
-        for x in range(4):
-            beside_ref[2 * x + s] = panel
+        beside_ref[s] = panel
 
 
 def prepare(row_counts, barrier, border):
@@ -184,7 +189,7 @@
         prepare_kernel,
         out_shape=(
             jax.ShapeDtypeStruct((16, TILE, capacity), jnp.float32),
-            jax.ShapeDtypeStruct((8, TILE, capacity), jnp.float32),
+            jax.ShapeDtypeStruct((2, TILE, capacity), jnp.float32),
         ),
         in_specs=[pl.BlockSpec(memory_space=pltpu.SMEM), vmem, pl.BlockSpec(memory_space=pltpu.HBM)],
         out_specs=(vmem, vmem),
@@ -194,9 +199,10 @@
     )(row_counts, barrier, border)
 
 
-def block_kernel(along_ref, beside_ref, out_ref):
+def block_kernel(core_ref, along_ref, beside_ref, out_ref):
     along = along_ref[...].reshape(16 * TILE, -1)
-    beside = beside_ref[...].reshape(8 * TILE, -1)
+    scenario = pl.ds(core_ref[0], 1)
+    beside = jnp.concatenate([beside_ref[p, scenario, :, :].reshape(TILE, -1) for p in range(8)], axis=0)
     part = dot(along, beside, 1, 1)
     quarter = 4 * TILE
     for c in range(2):
@@ -207,23 +213,47 @@
             out_ref[2 * y + c] = packed
 
 
-def block_part(along, beside):
+def block_part(core, along, beside):
     vmem = pl.BlockSpec(memory_space=pltpu.VMEM)
     return pl.pallas_call(
         block_kernel,
         out_shape=jax.ShapeDtypeStruct((16, 4 * TILE, 16 * TILE), jnp.float32),
-        in_specs=[vmem, vmem],
+        in_specs=[pl.BlockSpec(memory_space=pltpu.SMEM), vmem, vmem],
         out_specs=vmem,
         compiler_params=pltpu.CompilerParams(vmem_limit_bytes=16 << 20),
         name="block_part",
-    )(along, beside)
-
-
-def product(columns, panel):
-    return jnp.einsum(
-        "rc,kr->ck", columns, panel,
-        precision=lax.Precision.HIGH, preferred_element_type=jnp.float32,
-    )
+    )(core, along, beside)
+
+
+def two_parts(x):
+    first = x.astype(jnp.bfloat16)
+    return first, (x - first.astype(jnp.float32)).astype(jnp.bfloat16)
+
+
+def product_kernel(columns_ref, *refs):
+    *panel_refs, out_ref = refs
+    columns, columns_low = two_parts(columns_ref[...])
+    panel, panel_low = two_parts(jnp.concatenate([ref[...] for ref in panel_refs], axis=0))
+    total = jnp.dot(panel, columns, preferred_element_type=jnp.float32)
+    total = total + jnp.dot(panel, columns_low, preferred_element_type=jnp.float32)
+    total = total + jnp.dot(panel_low, columns, preferred_element_type=jnp.float32)
+    out_ref[...] = jnp.transpose(total)
+
+
+def product(columns, panels):
+    rows, width = columns.shape
+    vmem = pl.BlockSpec(memory_space=pltpu.VMEM)
+    return pl.pallas_call(
+        product_kernel,
+        out_shape=jax.ShapeDtypeStruct((width, PANEL), jnp.float32),
+        in_specs=[vmem] * (1 + len(panels)),
+        out_specs=vmem,
+        compiler_params=pltpu.CompilerParams(vmem_limit_bytes=32 << 20),
+        cost_estimate=pl.CostEstimate(
+            flops=6 * rows * width * PANEL, bytes_accessed=4 * rows * (width + PANEL), transcendentals=0
+        ),
+        name="product",
+    )(columns, *panels)
 
 
 def exchange(array, axes):
@@ -236,25 +266,33 @@
     n_scen = lax.axis_size("scen")
     rows_owned = own_cols // n_scen
     core = lax.axis_index("core")
+    place = jnp.stack([core, lax.axis_index("x")])
 
     to_along, to_beside = prepare(row_counts, barrier, border)
     along = exchange(to_along, ("z", "core"))
-    panel = lax.all_gather(along.reshape(16 * TILE, capacity), "x", axis=0, tiled=True)
-
-    beside = exchange(to_beside, ("x", "core"))
-    piece = block_part(along, beside)
-    parts = exchange(piece, ("scen", "core"))
-    summed = jnp.sum(parts, axis=0)
+    beside = lax.all_gather(to_beside, ("x", "core"), axis=0, tiled=False)
+    along, beside = lax.optimization_barrier((along, beside))
+
+    shard = along.reshape(16 * TILE, capacity)
+    behind = lax.ppermute(shard, "x", AHEAD)
+    ahead = lax.ppermute(shard, "x", BEHIND)
+
+    piece = block_part(place, along, beside)
+    summed = jnp.sum(exchange(piece, ("scen", "core")), axis=0)
+    behind, ahead, summed, later = lax.optimization_barrier((behind, ahead, summed, border))
     copies = jnp.broadcast_to(summed, (32,) + summed.shape)
     own_half = exchange(copies, ("z", "x"))
     other_half = lax.ppermute(own_half, "core", SWAP)
-    inverse = inverse_factor(jnp.reshape(core, (1,)), own_half, other_half)
-
-    border, _ = lax.optimization_barrier((border, summed))
-    mine = lax.dynamic_index_in_dim(border, core, 0, keepdims=False)
-    other = lax.ppermute(lax.dynamic_index_in_dim(border, 1 - core, 0, keepdims=False), "core", SWAP)
-    schur_other = product(other, panel)
-    schur_mine = product(mine, panel)
+    inverse = inverse_factor(place, own_half, other_half)
+
+    half = 8 * TILE
+    panels = (
+        shard, behind, ahead, lax.ppermute(behind[:half], "x", AHEAD), lax.ppermute(ahead[half:], "x", BEHIND)
+    )
+    other = lax.ppermute(lax.dynamic_index_in_dim(later, 1 - core, 0, keepdims=False), "core", SWAP)
+    mine = lax.dynamic_index_in_dim(later, core, 0, keepdims=False)
+    schur_other = product(other, panels)
+    schur_mine = product(mine, panels)
     schur_part = schur_mine + lax.ppermute(schur_other, "core", SWAP)
     owned = jnp.sum(exchange(schur_part.reshape(n_scen, rows_owned, PANEL), "scen"), axis=0)
     solved = dot(owned, inverse, 1, 0)

time: 140 us -> 133 us (0.950)
  blocking collectives: 47.6 us -> 13.7 us
  starting transfers between devices: 24 us -> 52.6 us
  between operations: 13.5 us -> 0.16 us
  matrix products: 10.9 us -> 1.34 us
  waiting for transfers between devices: 16.8 us -> 25.9 us
  Pallas kernels: 22.5 us -> 30 us
  local copies, waits for them, and re-layouts: 3.27 us -> 6.67 us
    all_to_all x2 -> x0, blocking collectives: 47.6 us -> none  [exchange(): return lax.all_to_all(array, axes, split_axis=0, concat_axis=0, tiled=True)]
    all_gather x0 -> x1, blocking collectives: none -> 13.7 us  [body(): beside = lax.all_gather(to_beside, ('x', 'core'), axis=0, tiled=False)]
    ppermute x1 -> x5, starting transfers between devices: 1.91 us -> 15 us  [the longest x1 4.56 us: body(): lax.ppermute(ahead[half:], 'x', BEHIND)]
    all_to_all x3 -> x4, starting transfers between devices: 15.4 us -> 27.7 us  [exchange(): return lax.all_to_all(array, axes, split_axis=0, concat_axis=0, tiled=True)]
    dot_general x2 -> x0, matrix products: 9.58 us -> none  [product(): jnp.einsum('rc,kr->ck', columns, panel, precision=lax.Precision.HIGH, pre...]
    all_to_all x3 -> x4, waiting for transfers between devices: 15.4 us -> 21.9 us  [exchange(): return lax.all_to_all(array, axes, split_axis=0, concat_axis=0, tiled=True)]
    pallas_call x0 -> x2, Pallas kernels: none -> 5.91 us  [product(): pl.pallas_call(product_kernel, out_shape=jax.ShapeDtypeStruct((width, PAN...]
    ppermute x1, starting transfers between devices: 2.41 us -> 5.15 us  [body(): schur_part = schur_mine + lax.ppermute(schur_other, 'core', SWAP)]
  transfers between devices with their start and end apart: 7 -> 11, of which waited for: 3 -> 5; matrix products, arithmetic and copies ran while one was open for 9% -> 4% of each run, Pallas kernels for 14% -> 20%
where the time goes in v5:
time: 133 us; the launch traced here: 132 us
  starting transfers between devices  52.6 us (40%)
  Pallas kernels  30 us (23%)
  waiting for transfers between devices  25.9 us (19%)
  blocking collectives  13.7 us (10%)
  local copies, waits for them, and re-layouts  6.67 us (5%)
  other arithmetic  1.61 us (1%)
  matrix products  1.34 us (1%)
    all_to_all x4, starting transfers between devices, exchange(): return lax.all_to_all(array, axes, split_axis=0, concat_axis=0, tiled=True)  27.7 us
    all_to_all x4, waiting for transfers between devices, exchange(): return lax.all_to_all(array, axes, split_axis=0, concat_axis=0, tiled=True)  21.9 us
    pallas_call x1, Pallas kernels, inverse_factor(): pl.pallas_call(inverse_kernel, out_shape=jax.ShapeDtypeStruct(shape, jnp....  18.7 us
    all_gather x1, blocking collectives, body(): beside = lax.all_gather(to_beside, ('x', 'core'), axis=0, tiled=False)  13.7 us
    pallas_call x2, Pallas kernels, product(): pl.pallas_call(product_kernel, out_shape=jax.ShapeDtypeStruct((width, PAN...  5.91 us
    ppermute x1, starting transfers between devices, body(): schur_part = schur_mine + lax.ppermute(schur_other, 'core', SWAP)  5.15 us
    ppermute x1, starting transfers between devices, body(): other_half = lax.ppermute(own_half, 'core', SWAP)  4.71 us
    ppermute x1, starting transfers between devices, body(): lax.ppermute(ahead[half:], 'x', BEHIND)  4.56 us
  transfers between devices with their start and end apart: 11, of which 5 were waited for; matrix products, arithmetic and copies ran while one was open for 4% of the time, Pallas kernels for 20%

profile of v5, /device:TPU:1, one launch (start us, length us, event | category | flops | bytes accessed | tf_op | source)
XLA Modules:
  0.0 131.9 jit_solution(10419377882666960867)
XLA Ops:
  0.0 3.3 %prepare.1 = (f32[16,8,1536]{2,1,0:T(8,128)}, f32[2,8,1536]{2,1,0:T(8,128)}) custom-call(s32[2]{0:T(128)} %counts_ref.1, f32[2,1536]{1,0:T(2,128)} %barrier_ref.1, f32[2,1536,256]{2,1,0:T(8,128)} %border_ref.1), custom_call_target="tpu_custom_call" | custom-call | tf_op jit(solution)/shard_map/prepare/pallas_call | solution.py:188
  3.3 0.0 copy-start
  3.3 12.0 %all-to-all-start = ((f32[16,8,1536]{2,1,0:T(8,128)}), f32[16,8,1536]{2,1,0:T(8,128)S(1)}, u32[]{:S(2)}, u32[]{:S(2)}) async-start(f32[16,8,1536]{2,1,0:T(8,128)} %get-tuple-element.13), calls=%async_computation | async-start | bytes 1572864 | tf_op jit(solution)/shard_map/all_to_all | solution.py:260
  15.3 0.0 copy-done
  15.3 13.7 %all-gather = f32[16,8,1536]{2,1,0:T(8,128)S(1)} all-gather(f32[2,8,1536]{2,1,0:T(8,128)S(1)} %copy-done), channel_id=2, replica_groups=mesh['scen'=8,'z'=8,'x'=4,'core'=2] {'x','core'}, dimensions={0}, use_global_device_ids=true | all-gather | bytes 884736 | tf_op jit(solution)/shard_map/all_gather | solution.py:273
  29.0 9.0 %all-to-all-done.along_ref = f32[16,8,1536]{2,1,0:T(8,128)S(1)} async-done(((f32[16,8,1536]{2,1,0:T(8,128)}), f32[16,8,1536]{2,1,0:T(8,128)S(1)}, u32[]{:S(2)}, u32[]{:S(2)}) %all-to-all-start) | async-done | bytes 786464 | tf_op jit(solution)/shard_map/all_to_all | solution.py:260
  37.9 3.1 %collective-permute-start = (f32[128,1536]{1,0:T(8,128)S(1)}, f32[128,1536]{1,0:T(8,128)S(1)}, u32[]{:S(2)}, u32[]{:S(2)}) collective-permute-start(f32[128,1536]{1,0:T(8,128)S(1)} %bitcast.13), channel_id=1, source_target_pairs={{0,2},{2,4},{4,6},{6,0},{1,3},{3,5},{5,7},{7,1},{8,10},{10,12},{12... | collective-permute-start | bytes 2359304 | tf_op jit(solution)/shard_map/ppermute | solution.py:277
  41.1 3.4 %collective-permute-start.1 = (f32[128,1536]{1,0:T(8,128)S(1)}, f32[128,1536]{1,0:T(8,128)}, u32[]{:S(2)}, u32[]{:S(2)}) collective-permute-start(f32[128,1536]{1,0:T(8,128)S(1)} %bitcast.14), channel_id=1, source_target_pairs={{0,6},{2,0},{4,2},{6,4},{1,7},{3,1},{5,3},{7,5},{8,14},{10,8},{12,... | collective-permute-start | bytes 2359304 | tf_op jit(solution)/shard_map/ppermute | solution.py:278
  44.4 0.1 pad_add_fusion.core_ref.place_ref
  44.5 2.1 %block_part.1 = f32[16,32,128]{2,1,0:T(8,128)} custom-call(s32[2]{0:T(128)S(1)} %pad_add_fusion.core_ref.place_ref, f32[16,8,1536]{2,1,0:T(8,128)S(1)} %all-to-all-done.along_ref, f32[8,2,8,1536]{3,2,1,0:T(8,128)S(1)} %bitcast.17), custom_call_target="tpu_custom_call" | custom-call | tf_op jit(solution)/shard_map/block_part/pallas_call | solution.py:218
  46.6 7.2 %all-to-all-start.1 = ((f32[16,32,128]{2,1,0:T(8,128)}), f32[16,32,128]{2,1,0:T(8,128)S(1)}, u32[]{:S(2)}, u32[]{:S(2)}) async-start(f32[16,32,128]{2,1,0:T(8,128)} %block_part.1), calls=%async_computation.1 | async-start | bytes 524288 | tf_op jit(solution)/shard_map/all_to_all | solution.py:260
  53.8 11.7 %all-to-all-done.1 = f32[16,32,128]{2,1,0:T(8,128)S(1)} async-done(((f32[16,32,128]{2,1,0:T(8,128)}), f32[16,32,128]{2,1,0:T(8,128)S(1)}, u32[]{:S(2)}, u32[]{:S(2)}) %all-to-all-start.1) | async-done | bytes 262176 | tf_op jit(solution)/shard_map/all_to_all | solution.py:260
  65.5 0.6 reduce_sum.18
  66.2 0.0 collective-permute-done.refs_1_
  66.2 0.0 collective-permute-done.1.refs_2_
  66.2 3.2 %dynamic-slice_bitcast_fusion = (f32[1536,256]{1,0:T(8,128)}, f32[1536,256]{1,0:T(8,128)S(1)}) fusion(f32[2,1536,256]{2,1,0:T(8,128)} %border_ref.1, s32[]{:T(128)S(6)} %select_n.8, s32[]{:T(128)S(6)} %select_n.7), kind=kLoop, calls=%fused_computation | loop fusion | bytes 6291464 | tf_op jit(solution)/shard_map/jit(dynamic_index_in_dim)/squeeze | solution.py:292
  69.4 0.0 copy-start.1
  69.4 2.0 %collective-permute-start.4 = (f32[1536,256]{1,0:T(8,128)}, f32[1536,256]{1,0:T(8,128)}, u32[]{:S(2)}, u32[]{:S(2)}) collective-permute-start(f32[1536,256]{1,0:T(8,128)} %get-tuple-element.21), channel_id=1, source_target_pairs={{0,1},{1,0},{2,3},{3,2},{4,5},{5,4},{6,7},{7,6},{8,9},{9,8},{10,11... | collective-permute-start | bytes 4718600 | tf_op jit(solution)/shard_map/ppermute | solution.py:292
  71.5 0.8 slice.6
  72.3 1.9 %collective-permute-start.2 = (f32[64,1536]{1,0:T(8,128)}, f32[64,1536]{1,0:T(8,128)S(1)}, u32[]{:S(2)}, u32[]{:S(2)}) collective-permute-start(f32[64,1536]{1,0:T(8,128)} %slice.6), channel_id=1, source_target_pairs={{0,2},{2,4},{4,6},{6,0},{1,3},{3,5},{5,7},{7,1},{8,10},{10,12},{12... | collective-permute-start | bytes 1179656 | tf_op jit(solution)/shard_map/ppermute | solution.py:290
  74.2 1.8 %slice.7 = f32[64,1536]{1,0:T(8,128)} slice(f32[128,1536]{1,0:T(8,128)} %collective-permute-done.1.refs_2_), slice={[64:128], [0:1536]} | slice | bytes 786432 | tf_op jit(solution)/shard_map/slice | solution.py:290
  75.9 4.6 %collective-permute-start.3 = (f32[64,1536]{1,0:T(8,128)}, f32[64,1536]{1,0:T(8,128)}, u32[]{:S(2)}, u32[]{:S(2)}) collective-permute-start(f32[64,1536]{1,0:T(8,128)} %slice.7), channel_id=1, source_target_pairs={{0,6},{2,0},{4,2},{6,4},{1,7},{3,1},{5,3},{7,5},{8,14},{10,8},{12,... | collective-permute-start | bytes 1179656 | tf_op jit(solution)/shard_map/ppermute | solution.py:290
  80.5 0.0 copy-done.1
  80.5 0.9 broadcast_in_dim.3
  81.4 4.6 %all-to-all-start.3 = ((f32[32,32,128]{2,1,0:T(8,128)}), f32[32,32,128]{2,1,0:T(8,128)}, u32[]{:S(2)}, u32[]{:S(2)}) async-start(f32[32,32,128]{2,1,0:T(8,128)} %broadcast_in_dim.3), calls=%async_computation.3 | async-start | bytes 1048576 | tf_op jit(solution)/shard_map/all_to_all | solution.py:260
  86.0 0.0 collective-permute-done.2.refs_3_
  86.0 2.5 %collective-permute-done.3.refs_4_ = f32[64,1536]{1,0:T(8,128)} collective-permute-done((f32[64,1536]{1,0:T(8,128)}, f32[64,1536]{1,0:T(8,128)}, u32[]{:S(2)}, u32[]{:S(2)}) %collective-permute-start.3) | collective-permute-done | bytes 393248 | tf_op jit(solution)/shard_map/ppermute | solution.py:290
  88.5 0.0 collective-permute-done.4.columns_ref
  88.5 3.2 %product.3 = f32[256,512]{1,0:T(8,128)S(1)} custom-call(f32[1536,256]{1,0:T(8,128)} %collective-permute-done.4.columns_ref, f32[128,1536]{1,0:T(8,128)S(1)} %bitcast.15, f32[128,1536]{1,0:T(8,128)S(1)} %collective-permute-done.refs_1_, f32[128,1536]{1,0:T(8,128)} %collective-permute-done.1.refs_2_, f32[64,1536]{1,0:T(8,128)S(1)} %collective-permute-done.2.refs_3_, ...), custom_call_target="tpu_custom_call" | custom-call | flops 1207959552 | bytes 4718592 | tf_op jit(solution)/shard_map/product/pallas_call | solution.py:246
  91.7 5.2 %collective-permute-start.5 = (f32[256,512]{1,0:T(8,128)S(1)}, f32[256,512]{1,0:T(8,128)S(1)}, u32[]{:S(2)}, u32[]{:S(2)}) collective-permute-start(f32[256,512]{1,0:T(8,128)S(1)} %product.3), channel_id=1, source_target_pairs={{0,1},{1,0},{2,3},{3,2},{4,5},{5,4},{6,7},{7,6},{8,9},{9,8},{10,11... | collective-permute-start | bytes 1572872 | tf_op jit(solution)/shard_map/ppermute | solution.py:296
  96.8 2.7 %product.2 = f32[256,512]{1,0:T(8,128)S(1)} custom-call(f32[1536,256]{1,0:T(8,128)S(1)} %get-tuple-element.22.columns_ref, f32[128,1536]{1,0:T(8,128)S(1)} %bitcast.16, f32[128,1536]{1,0:T(8,128)S(1)} %collective-permute-done.refs_1_, f32[128,1536]{1,0:T(8,128)} %collective-permute-done.1.refs_2_, f32[64,1536]{1,0:T(8,128)S(1)} %collective-permute-done.2.refs_3_, ...), custom_call_target="tpu_custom_call" | custom-call | flops 1207959552 | bytes 4718592 | tf_op jit(solution)/shard_map/product/pallas_call | solution.py:246
  99.6 0.0 collective-permute-done.5
  99.6 0.9 add.13
  100.5 1.2 all-to-all-done.3.own_ref
  101.6 3.9 %all-to-all-start.2 = ((f32[8,32,512]{2,1,0:T(8,128)}), f32[8,32,512]{2,1,0:T(8,128)S(1)}, u32[]{:S(2)}, u32[]{:S(2)}) async-start(f32[8,32,512]{2,1,0:T(8,128)} %bitcast.6), calls=%async_computation.2 | async-start | bytes 1048576 | tf_op jit(solution)/shard_map/all_to_all | solution.py:260
  105.5 4.7 %collective-permute-start.6 = (f32[32,32,128]{2,1,0:T(8,128)}, f32[32,32,128]{2,1,0:T(8,128)S(1)}, u32[]{:S(2)}, u32[]{:S(2)}) collective-permute-start(f32[32,32,128]{2,1,0:T(8,128)} %all-to-all-done.3.own_ref), channel_id=1, source_target_pairs={{0,1},{1,0},{2,3},{3,2},{4,5},{5,4},{6,7},{7,6},{8,9},{9,8},{10,11... | collective-permute-start | bytes 1572872 | tf_op jit(solution)/shard_map/ppermute | solution.py:285
  110.3 1.5 %collective-permute-done.6.other_ref = f32[32,32,128]{2,1,0:T(8,128)S(1)} collective-permute-done((f32[32,32,128]{2,1,0:T(8,128)}, f32[32,32,128]{2,1,0:T(8,128)S(1)}, u32[]{:S(2)}, u32[]{:S(2)}) %collective-permute-start.6) | collective-permute-done | bytes 524320 | tf_op jit(solution)/shard_map/ppermute | solution.py:285
  111.8 18.7 %inverse_factor.1 = f32[512,512]{1,0:T(8,128)S(1)} custom-call(s32[2]{0:T(128)S(1)} %pad_add_fusion.core_ref.place_ref, f32[32,32,128]{2,1,0:T(8,128)} %all-to-all-done.3.own_ref, f32[32,32,128]{2,1,0:T(8,128)S(1)} %collective-permute-done.6.other_ref), custom_call_target="tpu_custom_call" | custom-call | flops 536870912 | bytes 2097152 | tf_op jit(solution)/shard_map/inverse_factor/pallas_call | solution.py:154
  130.5 0.0 all-to-all-done.2
  130.6 1.3 %convolution_bitcast_fusion = f32[1,1,32,512]{3,2,1,0:T(8,128)} fusion(f32[32,512]{1,0:T(8,128)S(1)} %reduce_sum.19, f32[512,512]{1,0:T(8,128)S(1)} %inverse_factor.1), kind=kOutput, calls=%fused_computation.2 | convolution fusion | flops 100663296 | bytes 1179648 | tf_op jit(solution)/shard_map/dot_general | solution.py:18
  (1 shorter events, 0.0 us)
Async XLA Ops:
  3.3 12.0 %copy-start = (f32[2,8,1536]{2,1,0:T(8,128)S(1)}, f32[2,8,1536]{2,1,0:T(8,128)}, u32[]{:S(2)}) copy-start(f32[2,8,1536]{2,1,0:T(8,128)} %get-tuple-element.14) | copy-start | bytes 294916
  3.3 34.6 %all-to-all-start = ((f32[16,8,1536]{2,1,0:T(8,128)}), f32[16,8,1536]{2,1,0:T(8,128)S(1)}, u32[]{:S(2)}, u32[]{:S(2)}) async-start(f32[16,8,1536]{2,1,0:T(8,128)} %get-tuple-element.13), calls=%async_computation | async-start | bytes 1572864 | tf_op jit(solution)/shard_map/all_to_all | solution.py:260
  37.9 28.2 %collective-permute-start = (f32[128,1536]{1,0:T(8,128)S(1)}, f32[128,1536]{1,0:T(8,128)S(1)}, u32[]{:S(2)}, u32[]{:S(2)}) collective-permute-start(f32[128,1536]{1,0:T(8,128)S(1)} %bitcast.13), channel_id=1, source_target_pairs={{0,2},{2,4},{4,6},{6,0},{1,3},{3,5},{5,7},{7,1},{8,10},{10,12},{12... | collective-permute-start | bytes 2359304 | tf_op jit(solution)/shard_map/ppermute | solution.py:277
  41.1 25.1 %collective-permute-start.1 = (f32[128,1536]{1,0:T(8,128)S(1)}, f32[128,1536]{1,0:T(8,128)}, u32[]{:S(2)}, u32[]{:S(2)}) collective-permute-start(f32[128,1536]{1,0:T(8,128)S(1)} %bitcast.14), channel_id=1, source_target_pairs={{0,6},{2,0},{4,2},{6,4},{1,7},{3,1},{5,3},{7,5},{8,14},{10,8},{12,... | collective-permute-start | bytes 2359304 | tf_op jit(solution)/shard_map/ppermute | solution.py:278
  46.6 18.9 %all-to-all-start.1 = ((f32[16,32,128]{2,1,0:T(8,128)}), f32[16,32,128]{2,1,0:T(8,128)S(1)}, u32[]{:S(2)}, u32[]{:S(2)}) async-start(f32[16,32,128]{2,1,0:T(8,128)} %block_part.1), calls=%async_computation.1 | async-start | bytes 524288 | tf_op jit(solution)/shard_map/all_to_all | solution.py:260
  69.4 11.1 %copy-start.1 = (f32[32,128]{1,0:T(8,128)S(1)}, f32[32,128]{1,0:T(8,128)}, u32[]{:S(2)}) copy-start(f32[32,128]{1,0:T(8,128)} %reduce_sum.18) | copy-start | bytes 49156
  69.4 19.1 %collective-permute-start.4 = (f32[1536,256]{1,0:T(8,128)}, f32[1536,256]{1,0:T(8,128)}, u32[]{:S(2)}, u32[]{:S(2)}) collective-permute-start(f32[1536,256]{1,0:T(8,128)} %get-tuple-element.21), channel_id=1, source_target_pairs={{0,1},{1,0},{2,3},{3,2},{4,5},{5,4},{6,7},{7,6},{8,9},{9,8},{10,11... | collective-permute-start | bytes 4718600 | tf_op jit(solution)/shard_map/ppermute | solution.py:292
  72.3 13.8 %collective-permute-start.2 = (f32[64,1536]{1,0:T(8,128)}, f32[64,1536]{1,0:T(8,128)S(1)}, u32[]{:S(2)}, u32[]{:S(2)}) collective-permute-start(f32[64,1536]{1,0:T(8,128)} %slice.6), channel_id=1, source_target_pairs={{0,2},{2,4},{4,6},{6,0},{1,3},{3,5},{5,7},{7,1},{8,10},{10,12},{12... | collective-permute-start | bytes 1179656 | tf_op jit(solution)/shard_map/ppermute | solution.py:290
  75.9 12.6 %collective-permute-start.3 = (f32[64,1536]{1,0:T(8,128)}, f32[64,1536]{1,0:T(8,128)}, u32[]{:S(2)}, u32[]{:S(2)}) collective-permute-start(f32[64,1536]{1,0:T(8,128)} %slice.7), channel_id=1, source_target_pairs={{0,6},{2,0},{4,2},{6,4},{1,7},{3,1},{5,3},{7,5},{8,14},{10,8},{12,... | collective-permute-start | bytes 1179656 | tf_op jit(solution)/shard_map/ppermute | solution.py:290
  81.4 20.2 %all-to-all-start.3 = ((f32[32,32,128]{2,1,0:T(8,128)}), f32[32,32,128]{2,1,0:T(8,128)}, u32[]{:S(2)}, u32[]{:S(2)}) async-start(f32[32,32,128]{2,1,0:T(8,128)} %broadcast_in_dim.3), calls=%async_computation.3 | async-start | bytes 1048576 | tf_op jit(solution)/shard_map/all_to_all | solution.py:260
  91.7 7.9 %collective-permute-start.5 = (f32[256,512]{1,0:T(8,128)S(1)}, f32[256,512]{1,0:T(8,128)S(1)}, u32[]{:S(2)}, u32[]{:S(2)}) collective-permute-start(f32[256,512]{1,0:T(8,128)S(1)} %product.3), channel_id=1, source_target_pairs={{0,1},{1,0},{2,3},{3,2},{4,5},{5,4},{6,7},{7,6},{8,9},{9,8},{10,11... | collective-permute-start | bytes 1572872 | tf_op jit(solution)/shard_map/ppermute | solution.py:296
  101.6 28.9 %all-to-all-start.2 = ((f32[8,32,512]{2,1,0:T(8,128)}), f32[8,32,512]{2,1,0:T(8,128)S(1)}, u32[]{:S(2)}, u32[]{:S(2)}) async-start(f32[8,32,512]{2,1,0:T(8,128)} %bitcast.6), calls=%async_computation.2 | async-start | bytes 1048576 | tf_op jit(solution)/shard_map/all_to_all | solution.py:260
  105.5 6.3 %collective-permute-start.6 = (f32[32,32,128]{2,1,0:T(8,128)}, f32[32,32,128]{2,1,0:T(8,128)S(1)}, u32[]{:S(2)}, u32[]{:S(2)}) collective-permute-start(f32[32,32,128]{2,1,0:T(8,128)} %all-to-all-done.3.own_ref), channel_id=1, source_target_pairs={{0,1},{1,0},{2,3},{3,2},{4,5},{5,4},{6,7},{7,6},{8,9},{9,8},{10,11... | collective-permute-start | bytes 1572872 | tf_op jit(solution)/shard_map/ppermute | solution.py:285

commit v6 on v5

--- a/solution.py
+++ b/solution.py
@@ -12,6 +12,7 @@
 SWAP = [(0, 1), (1, 0)]
 AHEAD = [(x, (x + 1) % 4) for x in range(4)]
 BEHIND = [(x, (x + 3) % 4) for x in range(4)]
+ONWARD = [(2 * x + c, 2 * ((x + 1 + 2 * c) % 4) + c) for x in range(4) for c in range(2)]
 
 
 def dot(a, b, dim_a, dim_b):
@@ -163,13 +164,15 @@
     )(place, own, other)
 
 
-def prepare_kernel(counts_ref, barrier_ref, border_ref, along_ref, beside_ref, columns, arrived):
+def prepare_kernel(place_ref, counts_ref, barrier_ref, border_ref, along_ref, beside_ref, other_ref, columns, arrived, moved):
     capacity = barrier_ref.shape[1]
     copies = [
         pltpu.make_async_copy(border_ref.at[s, :, pl.ds(0, 128)], columns.at[s], arrived.at[s]) for s in range(2)
     ]
     for copy in copies:
         copy.start()
+    other = pltpu.make_async_copy(border_ref.at[1 - place_ref[0]], other_ref, moved)
+    other.start()
     position = lax.broadcasted_iota(jnp.int32, (1, capacity), 1)
     for s in range(2):
         weights = jnp.where(position < counts_ref[s], 1.0 / barrier_ref[s:s + 1, :], 0.0)
@@ -180,9 +183,10 @@
         for z in range(8):
             along_ref[2 * z + s] = weighted
         beside_ref[s] = panel
-
-
-def prepare(row_counts, barrier, border):
+    other.wait()
+
+
+def prepare(place, row_counts, barrier, border):
     capacity = border.shape[1]
     vmem = pl.BlockSpec(memory_space=pltpu.VMEM)
     return pl.pallas_call(
@@ -190,13 +194,18 @@
         out_shape=(
             jax.ShapeDtypeStruct((16, TILE, capacity), jnp.float32),
             jax.ShapeDtypeStruct((2, TILE, capacity), jnp.float32),
+            jax.ShapeDtypeStruct(border.shape[1:], jnp.float32),
         ),
-        in_specs=[pl.BlockSpec(memory_space=pltpu.SMEM), vmem, pl.BlockSpec(memory_space=pltpu.HBM)],
-        out_specs=(vmem, vmem),
-        scratch_shapes=[pltpu.VMEM((2, capacity, 128), jnp.float32), pltpu.SemaphoreType.DMA((2,))],
+        in_specs=[pl.BlockSpec(memory_space=pltpu.SMEM)] * 2 + [vmem, pl.BlockSpec(memory_space=pltpu.HBM)],
+        out_specs=(vmem, vmem, pl.BlockSpec(memory_space=pltpu.HBM)),
+        scratch_shapes=[
+            pltpu.VMEM((2, capacity, 128), jnp.float32),
+            pltpu.SemaphoreType.DMA((2,)),
+            pltpu.SemaphoreType.DMA(()),
+        ],
         compiler_params=pltpu.CompilerParams(vmem_limit_bytes=60 << 20),
         name="prepare",
-    )(row_counts, barrier, border)
+    )(place, row_counts, barrier, border)
 
 
 def block_kernel(core_ref, along_ref, beside_ref, out_ref):
@@ -268,7 +277,7 @@
     core = lax.axis_index("core")
     place = jnp.stack([core, lax.axis_index("x")])
 
-    to_along, to_beside = prepare(row_counts, barrier, border)
+    to_along, to_beside, to_other = prepare(place, row_counts, barrier, border)
     along = exchange(to_along, ("z", "core"))
     beside = lax.all_gather(to_beside, ("x", "core"), axis=0, tiled=False)
     along, beside = lax.optimization_barrier((along, beside))
@@ -279,18 +288,16 @@
 
     piece = block_part(place, along, beside)
     summed = jnp.sum(exchange(piece, ("scen", "core")), axis=0)
-    behind, ahead, summed, later = lax.optimization_barrier((behind, ahead, summed, border))
+    behind, ahead, summed, to_other = lax.optimization_barrier((behind, ahead, summed, to_other))
     copies = jnp.broadcast_to(summed, (32,) + summed.shape)
     own_half = exchange(copies, ("z", "x"))
     other_half = lax.ppermute(own_half, "core", SWAP)
     inverse = inverse_factor(place, own_half, other_half)
 
-    half = 8 * TILE
-    panels = (
-        shard, behind, ahead, lax.ppermute(behind[:half], "x", AHEAD), lax.ppermute(ahead[half:], "x", BEHIND)
-    )
-    other = lax.ppermute(lax.dynamic_index_in_dim(later, 1 - core, 0, keepdims=False), "core", SWAP)
-    mine = lax.dynamic_index_in_dim(later, core, 0, keepdims=False)
+    onward = lax.ppermute(jnp.where(core == 0, behind, ahead), ("x", "core"), ONWARD)
+    panels = (shard, behind, ahead, onward)
+    other = lax.ppermute(to_other, "core", SWAP)
+    mine = lax.dynamic_index_in_dim(border, core, 0, keepdims=False)
     schur_other = product(other, panels)
     schur_mine = product(mine, panels)
     schur_part = schur_mine + lax.ppermute(schur_other, "core", SWAP)

time: 133 us -> 172 us (1.29)
  Pallas kernels: 30 us -> 75.8 us
  blocking collectives: 13.7 us -> 32.4 us
  starting transfers between devices: 52.6 us -> 39.9 us
  waiting for transfers between devices: 25.9 us -> 16.1 us
  local copies, waits for them, and re-layouts: 6.67 us -> 2.39 us
  other arithmetic: 1.61 us -> 3.58 us
    pallas_call x1, Pallas kernels: 3.28 us -> 50.4 us  [prepare(): pl.pallas_call(prepare_kernel, out_shape=(jax.ShapeDtypeStruct((16, TILE,...]
    all_to_all x0 -> x1, blocking collectives: none -> 18.7 us  [exchange(): return lax.all_to_all(array, axes, split_axis=0, concat_axis=0, tiled=True)]
    all_to_all x4 -> x3, waiting for transfers between devices: 21.9 us -> 8.99 us  [exchange(): return lax.all_to_all(array, axes, split_axis=0, concat_axis=0, tiled=True)]
    all_to_all x4 -> x3, starting transfers between devices: 27.7 us -> 20.1 us  [exchange(): return lax.all_to_all(array, axes, split_axis=0, concat_axis=0, tiled=True)]
    ppermute x3 -> x2, starting transfers between devices: 8.51 us -> 5.09 us  [the longest x1 3.16 us: body(): lax.ppermute(jnp.where(core == 0, behind, ahead), ('x', 'core'), ONWARD)]
    ppermute x3 -> x2, waiting for transfers between devices: 2.48 us -> 5.53 us  [the longest x1 5.53 us: body(): lax.ppermute(jnp.where(core == 0, behind, ahead), ('x', 'core'), ONWARD)]
    slice x2 -> x0, local copies, waits for them, and re-layouts: 2.55 us -> none  [the longest x1 1.76 us: body(): ahead[half:]]
    squeeze x1, local copies, waits for them, and re-layouts: 3.25 us -> 1.52 us  [body(): mine = lax.dynamic_index_in_dim(border, core, 0, keepdims=False)]
  transfers between devices with their start and end apart: 11 -> 9, of which waited for: 5 -> 3; matrix products, arithmetic and copies ran while one was open for 4% -> 3% of each run, Pallas kernels for 20% -> 15%
where the time goes in v6:
time: 172 us
  Pallas kernels  75.8 us (44%)
  starting transfers between devices  39.9 us (23%)
  blocking collectives  32.4 us (19%)
  waiting for transfers between devices  16.1 us (9%)
  other arithmetic  3.58 us (2%)
  local copies, waits for them, and re-layouts  2.39 us (1%)
    pallas_call x1, Pallas kernels, prepare(): pl.pallas_call(prepare_kernel, out_shape=(jax.ShapeDtypeStruct((16, TILE,...  50.4 us
    all_to_all x3, starting transfers between devices, exchange(): return lax.all_to_all(array, axes, split_axis=0, concat_axis=0, tiled=True)  20.1 us
    all_to_all x1, blocking collectives, exchange(): return lax.all_to_all(array, axes, split_axis=0, concat_axis=0, tiled=True)  18.7 us
    pallas_call x1, Pallas kernels, inverse_factor(): pl.pallas_call(inverse_kernel, out_shape=jax.ShapeDtypeStruct(shape, jnp....  18.7 us
    all_gather x1, blocking collectives, body(): beside = lax.all_gather(to_beside, ('x', 'core'), axis=0, tiled=False)  13.7 us
    all_to_all x3, waiting for transfers between devices, exchange(): return lax.all_to_all(array, axes, split_axis=0, concat_axis=0, tiled=True)  8.99 us
    ppermute x1, waiting for transfers between devices, body(): lax.ppermute(jnp.where(core == 0, behind, ahead), ('x', 'core'), ONWARD)  5.53 us
    pallas_call x2, Pallas kernels, product(): pl.pallas_call(product_kernel, out_shape=jax.ShapeDtypeStruct((width, PAN...  5.26 us
  transfers between devices with their start and end apart: 9, of which 3 were waited for; matrix products, arithmetic and copies ran while one was open for 3% of the time, Pallas kernels for 15%

profile of v6, /device:TPU:1, one launch (start us, length us, event | category | flops | bytes accessed | tf_op | source)
XLA Modules:
  0.0 171.6 jit_solution(17993140154886430480)
XLA Ops:
  0.0 0.6 pad_add_fusion.place_ref.core_ref
  0.6 50.4 %prepare.1 = (f32[16,8,1536]{2,1,0:T(8,128)}, f32[2,8,1536]{2,1,0:T(8,128)}, f32[1536,256]{1,0:T(8,128)}) custom-call(s32[2]{0:T(128)} %pad_add_fusion.place_ref.core_ref, s32[2]{0:T(128)} %counts_ref.1, f32[2,1536]{1,0:T(2,128)} %barrier_ref.1, f32[2,1536,256]{2,1,0:T(8,128)} %border_ref.1), custom_call_target="tpu_custom_call" | custom-call | tf_op jit(solution)/shard_map/prepare/pallas_call | solution.py:192
  51.0 0.0 copy-start.1
  51.0 0.0 copy-start
  51.0 12.0 %all-to-all-start = ((f32[16,8,1536]{2,1,0:T(8,128)}), f32[16,8,1536]{2,1,0:T(8,128)S(1)}, u32[]{:S(2)}, u32[]{:S(2)}) async-start(f32[16,8,1536]{2,1,0:T(8,128)} %get-tuple-element.14), calls=%async_computation | async-start | bytes 1572864 | tf_op jit(solution)/shard_map/all_to_all | solution.py:269
  63.0 0.0 copy-done.1
  63.0 13.7 %all-gather = f32[16,8,1536]{2,1,0:T(8,128)S(1)} all-gather(f32[2,8,1536]{2,1,0:T(8,128)S(1)} %copy-done.1), channel_id=2, replica_groups=mesh['scen'=8,'z'=8,'x'=4,'core'=2] {'x','core'}, dimensions={0}, use_global_device_ids=true | all-gather | bytes 884736 | tf_op jit(solution)/shard_map/all_gather | solution.py:282
  76.7 9.0 %all-to-all-done.along_ref = f32[16,8,1536]{2,1,0:T(8,128)S(1)} async-done(((f32[16,8,1536]{2,1,0:T(8,128)}), f32[16,8,1536]{2,1,0:T(8,128)S(1)}, u32[]{:S(2)}, u32[]{:S(2)}) %all-to-all-start) | async-done | bytes 786464 | tf_op jit(solution)/shard_map/all_to_all | solution.py:269
  85.7 3.1 %collective-permute-start = (f32[128,1536]{1,0:T(8,128)S(1)}, f32[128,1536]{1,0:T(8,128)S(1)}, u32[]{:S(2)}, u32[]{:S(2)}) collective-permute-start(f32[128,1536]{1,0:T(8,128)S(1)} %bitcast.11), channel_id=1, source_target_pairs={{0,2},{2,4},{4,6},{6,0},{1,3},{3,5},{5,7},{7,1},{8,10},{10,12},{12... | collective-permute-start | bytes 2359304 | tf_op jit(solution)/shard_map/ppermute | solution.py:286
  88.8 3.4 %collective-permute-start.1 = (f32[128,1536]{1,0:T(8,128)S(1)}, f32[128,1536]{1,0:T(8,128)S(1)}, u32[]{:S(2)}, u32[]{:S(2)}) collective-permute-start(f32[128,1536]{1,0:T(8,128)S(1)} %bitcast.12), channel_id=1, source_target_pairs={{0,6},{2,0},{4,2},{6,4},{1,7},{3,1},{5,3},{7,5},{8,14},{10,8},{12,... | collective-permute-start | bytes 2359304 | tf_op jit(solution)/shard_map/ppermute | solution.py:287
  92.2 0.0 copy-done
  92.2 1.4 block_part.1
  93.6 18.7 %all_to_all.20 = f32[16,32,128]{2,1,0:T(8,128)S(1)} all-to-all(f32[16,32,128]{2,1,0:T(8,128)S(1)} %block_part.1), channel_id=1, replica_groups=mesh['scen'=8,'z'=8,'x'=4,'core'=2] {'scen','core'}, dimensions={0} | all-to-all | bytes 524288 | tf_op jit(solution)/shard_map/all_to_all | solution.py:269
  112.3 0.0 collective-permute-done.refs_1_
  112.3 0.0 collective-permute-done.1.refs_2_
  112.4 1.9 %collective-permute-start.3 = (f32[1536,256]{1,0:T(8,128)}, f32[1536,256]{1,0:T(8,128)}, u32[]{:S(2)}, u32[]{:S(2)}) collective-permute-start(f32[1536,256]{1,0:T(8,128)} %get-tuple-element.21), channel_id=1, source_target_pairs={{0,1},{1,0},{2,3},{3,2},{4,5},{5,4},{6,7},{7,6},{8,9},{9,8},{10,11... | collective-permute-start | bytes 4718600 | tf_op jit(solution)/shard_map/ppermute | solution.py:299
  114.3 1.0 broadcast_select_fusion
  115.3 3.2 %collective-permute-start.2 = (f32[128,1536]{1,0:T(8,128)}, f32[128,1536]{1,0:T(8,128)S(1)}, u32[]{:S(2)}, u32[]{:S(2)}) collective-permute-start(f32[128,1536]{1,0:T(8,128)} %broadcast_select_fusion), channel_id=1, source_target_pairs={{0,2},{1,7},{2,4},{3,1},{4,6},{5,3},{6,0},{7,5},{8,10},{9,15},{10,... | collective-permute-start | bytes 2359304 | tf_op jit(solution)/shard_map/ppermute | solution.py:297
  118.4 0.9 broadcast_in_dim.3
  119.3 4.6 %all-to-all-start.3 = ((f32[32,32,128]{2,1,0:T(8,128)}), f32[32,32,128]{2,1,0:T(8,128)}, u32[]{:S(2)}, u32[]{:S(2)}) async-start(f32[32,32,128]{2,1,0:T(8,128)} %broadcast_in_dim.3), calls=%async_computation.3 | async-start | bytes 1048576 | tf_op jit(solution)/shard_map/all_to_all | solution.py:269
  123.9 5.5 %collective-permute-done.2.refs_3_ = f32[128,1536]{1,0:T(8,128)S(1)} collective-permute-done((f32[128,1536]{1,0:T(8,128)}, f32[128,1536]{1,0:T(8,128)S(1)}, u32[]{:S(2)}, u32[]{:S(2)}) %collective-permute-start.2) | collective-permute-done | bytes 786464 | tf_op jit(solution)/shard_map/ppermute | solution.py:297
  129.5 0.0 collective-permute-done.3.columns_ref
  129.5 3.7 %product.3 = f32[256,512]{1,0:T(8,128)} custom-call(f32[1536,256]{1,0:T(8,128)} %collective-permute-done.3.columns_ref, f32[128,1536]{1,0:T(8,128)S(1)} %bitcast.13, f32[128,1536]{1,0:T(8,128)S(1)} %collective-permute-done.refs_1_, f32[128,1536]{1,0:T(8,128)S(1)} %collective-permute-done.1.refs_2_, f32[128,1536]{1,0:T(8,128)S(1)} %collective-permute-done.2.refs_3_), custom_call_target="tpu_custom_call" | custom-call | flops 1207959552 | bytes 4718592 | tf_op jit(solution)/shard_map/product/pallas_call | solution.py:255
  133.2 4.7 %collective-permute-start.4 = (f32[256,512]{1,0:T(8,128)}, f32[256,512]{1,0:T(8,128)}, u32[]{:S(2)}, u32[]{:S(2)}) collective-permute-start(f32[256,512]{1,0:T(8,128)} %product.3), channel_id=1, source_target_pairs={{0,1},{1,0},{2,3},{3,2},{4,5},{5,4},{6,7},{7,6},{8,9},{9,8},{10,11... | collective-permute-start | bytes 1572872 | tf_op jit(solution)/shard_map/ppermute | solution.py:303
  137.9 1.5 dynamic-slice_bitcast_fusion.columns_ref
  139.5 1.5 product.2
  141.0 0.0 collective-permute-done.4
  141.0 1.9 %add.8 = f32[256,512]{1,0:T(8,128)} add(f32[256,512]{1,0:T(8,128)S(1)} %product.2, f32[256,512]{1,0:T(8,128)} %collective-permute-done.4) | non-fusion elementwise | flops 131072 | bytes 1572864 | tf_op jit(solution)/shard_map/add | solution.py:303
  142.9 0.0 all-to-all-done.3.own_ref
  142.9 3.5 %all-to-all-start.2 = ((f32[8,32,512]{2,1,0:T(8,128)}), f32[8,32,512]{2,1,0:T(8,128)S(1)}, u32[]{:S(2)}, u32[]{:S(2)}) async-start(f32[8,32,512]{2,1,0:T(8,128)} %bitcast.5), calls=%async_computation.2 | async-start | bytes 1048576 | tf_op jit(solution)/shard_map/all_to_all | solution.py:269
  146.4 3.5 %collective-permute-start.5 = (f32[32,32,128]{2,1,0:T(8,128)}, f32[32,32,128]{2,1,0:T(8,128)S(1)}, u32[]{:S(2)}, u32[]{:S(2)}) collective-permute-start(f32[32,32,128]{2,1,0:T(8,128)} %all-to-all-done.3.own_ref), channel_id=1, source_target_pairs={{0,1},{1,0},{2,3},{3,2},{4,5},{5,4},{6,7},{7,6},{8,9},{9,8},{10,11... | collective-permute-start | bytes 1572872 | tf_op jit(solution)/shard_map/ppermute | solution.py:294
  149.9 1.5 collective-permute-done.5.other_ref
  151.5 18.7 %inverse_factor.1 = f32[512,512]{1,0:T(8,128)S(1)} custom-call(s32[2]{0:T(128)S(1)} %copy-done, f32[32,32,128]{2,1,0:T(8,128)} %all-to-all-done.3.own_ref, f32[32,32,128]{2,1,0:T(8,128)S(1)} %collective-permute-done.5.other_ref), custom_call_target="tpu_custom_call" | custom-call | flops 536870912 | bytes 2097152 | tf_op jit(solution)/shard_map/inverse_factor/pallas_call | solution.py:155
  170.2 0.0 all-to-all-done.2
  170.2 1.3 convolution_bitcast_fusion
  (2 shorter events, 0.1 us)
Async XLA Ops:
  51.0 12.0 %copy-start.1 = (f32[2,8,1536]{2,1,0:T(8,128)S(1)}, f32[2,8,1536]{2,1,0:T(8,128)}, u32[]{:S(2)}) copy-start(f32[2,8,1536]{2,1,0:T(8,128)} %get-tuple-element.15) | copy-start | bytes 294916
  51.0 41.1 %copy-start = (s32[2]{0:T(128)S(1)}, s32[2]{0:T(128)}, u32[]{:S(2)}) copy-start(s32[2]{0:T(128)} %pad_add_fusion.place_ref.core_ref) | copy-start | bytes 28
  51.0 34.6 %all-to-all-start = ((f32[16,8,1536]{2,1,0:T(8,128)}), f32[16,8,1536]{2,1,0:T(8,128)S(1)}, u32[]{:S(2)}, u32[]{:S(2)}) async-start(f32[16,8,1536]{2,1,0:T(8,128)} %get-tuple-element.14), calls=%async_computation | async-start | bytes 1572864 | tf_op jit(solution)/shard_map/all_to_all | solution.py:269
  85.7 26.7 %collective-permute-start = (f32[128,1536]{1,0:T(8,128)S(1)}, f32[128,1536]{1,0:T(8,128)S(1)}, u32[]{:S(2)}, u32[]{:S(2)}) collective-permute-start(f32[128,1536]{1,0:T(8,128)S(1)} %bitcast.11), channel_id=1, source_target_pairs={{0,2},{2,4},{4,6},{6,0},{1,3},{3,5},{5,7},{7,1},{8,10},{10,12},{12... | collective-permute-start | bytes 2359304 | tf_op jit(solution)/shard_map/ppermute | solution.py:286
  88.8 23.6 %collective-permute-start.1 = (f32[128,1536]{1,0:T(8,128)S(1)}, f32[128,1536]{1,0:T(8,128)S(1)}, u32[]{:S(2)}, u32[]{:S(2)}) collective-permute-start(f32[128,1536]{1,0:T(8,128)S(1)} %bitcast.12), channel_id=1, source_target_pairs={{0,6},{2,0},{4,2},{6,4},{1,7},{3,1},{5,3},{7,5},{8,14},{10,8},{12,... | collective-permute-start | bytes 2359304 | tf_op jit(solution)/shard_map/ppermute | solution.py:287
  112.4 17.1 %collective-permute-start.3 = (f32[1536,256]{1,0:T(8,128)}, f32[1536,256]{1,0:T(8,128)}, u32[]{:S(2)}, u32[]{:S(2)}) collective-permute-start(f32[1536,256]{1,0:T(8,128)} %get-tuple-element.21), channel_id=1, source_target_pairs={{0,1},{1,0},{2,3},{3,2},{4,5},{5,4},{6,7},{7,6},{8,9},{9,8},{10,11... | collective-permute-start | bytes 4718600 | tf_op jit(solution)/shard_map/ppermute | solution.py:299
  115.3 14.2 %collective-permute-start.2 = (f32[128,1536]{1,0:T(8,128)}, f32[128,1536]{1,0:T(8,128)S(1)}, u32[]{:S(2)}, u32[]{:S(2)}) collective-permute-start(f32[128,1536]{1,0:T(8,128)} %broadcast_select_fusion), channel_id=1, source_target_pairs={{0,2},{1,7},{2,4},{3,1},{4,6},{5,3},{6,0},{7,5},{8,10},{9,15},{10,... | collective-permute-start | bytes 2359304 | tf_op jit(solution)/shard_map/ppermute | solution.py:297
  119.3 23.6 %all-to-all-start.3 = ((f32[32,32,128]{2,1,0:T(8,128)}), f32[32,32,128]{2,1,0:T(8,128)}, u32[]{:S(2)}, u32[]{:S(2)}) async-start(f32[32,32,128]{2,1,0:T(8,128)} %broadcast_in_dim.3), calls=%async_computation.3 | async-start | bytes 1048576 | tf_op jit(solution)/shard_map/all_to_all | solution.py:269
  133.2 7.8 %collective-permute-start.4 = (f32[256,512]{1,0:T(8,128)}, f32[256,512]{1,0:T(8,128)}, u32[]{:S(2)}, u32[]{:S(2)}) collective-permute-start(f32[256,512]{1,0:T(8,128)} %product.3), channel_id=1, source_target_pairs={{0,1},{1,0},{2,3},{3,2},{4,5},{5,4},{6,7},{7,6},{8,9},{9,8},{10,11... | collective-permute-start | bytes 1572872 | tf_op jit(solution)/shard_map/ppermute | solution.py:303
  142.9 27.2 %all-to-all-start.2 = ((f32[8,32,512]{2,1,0:T(8,128)}), f32[8,32,512]{2,1,0:T(8,128)S(1)}, u32[]{:S(2)}, u32[]{:S(2)}) async-start(f32[8,32,512]{2,1,0:T(8,128)} %bitcast.5), calls=%async_computation.2 | async-start | bytes 1048576 | tf_op jit(solution)/shard_map/all_to_all | solution.py:269
  146.4 5.0 %collective-permute-start.5 = (f32[32,32,128]{2,1,0:T(8,128)}, f32[32,32,128]{2,1,0:T(8,128)S(1)}, u32[]{:S(2)}, u32[]{:S(2)}) collective-permute-start(f32[32,32,128]{2,1,0:T(8,128)} %all-to-all-done.3.own_ref), channel_id=1, source_target_pairs={{0,1},{1,0},{2,3},{3,2},{4,5},{5,4},{6,7},{7,6},{8,9},{9,8},{10,11... | collective-permute-start | bytes 1572872 | tf_op jit(solution)/shard_map/ppermute | solution.py:294

commit v7 on v6

--- a/solution.py
+++ b/solution.py
@@ -197,7 +197,7 @@
             jax.ShapeDtypeStruct(border.shape[1:], jnp.float32),
         ),
         in_specs=[pl.BlockSpec(memory_space=pltpu.SMEM)] * 2 + [vmem, pl.BlockSpec(memory_space=pltpu.HBM)],
-        out_specs=(vmem, vmem, pl.BlockSpec(memory_space=pltpu.HBM)),
+        out_specs=(vmem, vmem, vmem),
         scratch_shapes=[
             pltpu.VMEM((2, capacity, 128), jnp.float32),
             pltpu.SemaphoreType.DMA((2,)),
@@ -287,14 +287,17 @@
     ahead = lax.ppermute(shard, "x", BEHIND)
 
     piece = block_part(place, along, beside)
-    summed = jnp.sum(exchange(piece, ("scen", "core")), axis=0)
-    behind, ahead, summed, to_other = lax.optimization_barrier((behind, ahead, summed, to_other))
+    parts = exchange(piece, ("scen", "core"))
+    _, passed_on = lax.optimization_barrier((piece, jnp.where(core == 0, behind, ahead)))
+    onward = lax.ppermute(passed_on, ("x", "core"), ONWARD)
+    parts, _ = lax.optimization_barrier((parts, passed_on))
+    summed = jnp.sum(parts, axis=0)
+    summed, to_other = lax.optimization_barrier((summed, to_other))
     copies = jnp.broadcast_to(summed, (32,) + summed.shape)
     own_half = exchange(copies, ("z", "x"))
     other_half = lax.ppermute(own_half, "core", SWAP)
     inverse = inverse_factor(place, own_half, other_half)
 
-    onward = lax.ppermute(jnp.where(core == 0, behind, ahead), ("x", "core"), ONWARD)
     panels = (shard, behind, ahead, onward)
     other = lax.ppermute(to_other, "core", SWAP)
     mine = lax.dynamic_index_in_dim(border, core, 0, keepdims=False)

time: 172 us -> 126 us (0.73)
  Pallas kernels: 75.8 us -> 30.1 us
  blocking collectives: 32.4 us -> 13.7 us
  waiting for transfers between devices: 16.1 us -> 26.8 us
  starting transfers between devices: 39.9 us -> 47.2 us
    pallas_call x1, Pallas kernels: 50.4 us -> 4.05 us  [prepare(): pl.pallas_call(prepare_kernel, out_shape=(jax.ShapeDtypeStruct((16, TILE,...]
    all_to_all x1 -> x0, blocking collectives: 18.7 us -> none  [exchange(): return lax.all_to_all(array, axes, split_axis=0, concat_axis=0, tiled=True)]
    all_to_all x3 -> x4, starting transfers between devices: 20.1 us -> 27.3 us  [exchange(): return lax.all_to_all(array, axes, split_axis=0, concat_axis=0, tiled=True)]
    ppermute x1, waiting for transfers between devices: 0.01 us -> 5.4 us  [body(): behind = lax.ppermute(shard, 'x', AHEAD)]
    all_to_all x3 -> x4, waiting for transfers between devices: 8.99 us -> 12.1 us  [exchange(): return lax.all_to_all(array, axes, split_axis=0, concat_axis=0, tiled=True)]
    ppermute x1, waiting for transfers between devices: 0.01 us -> 2.2 us  [body(): ahead = lax.ppermute(shard, 'x', BEHIND)]
  transfers between devices with their start and end apart: 9 -> 10, of which waited for: 3 -> 6; matrix products, arithmetic and copies ran while one was open for 3% -> 4% of each run, Pallas kernels for 15% -> 21%
where the time goes in v7:
time: 126 us; the launch traced here: 125 us
  starting transfers between devices  47.2 us (37%)
  Pallas kernels  30.1 us (24%)
  waiting for transfers between devices  26.8 us (21%)
  blocking collectives  13.7 us (11%)
  other arithmetic  3.56 us (3%)
  local copies, waits for them, and re-layouts  2.39 us (2%)
  matrix products  1.34 us (1%)
    all_to_all x4, starting transfers between devices, exchange(): return lax.all_to_all(array, axes, split_axis=0, concat_axis=0, tiled=True)  27.3 us
    pallas_call x1, Pallas kernels, inverse_factor(): pl.pallas_call(inverse_kernel, out_shape=jax.ShapeDtypeStruct(shape, jnp....  18.7 us
    all_gather x1, blocking collectives, body(): beside = lax.all_gather(to_beside, ('x', 'core'), axis=0, tiled=False)  13.7 us
    all_to_all x4, waiting for transfers between devices, exchange(): return lax.all_to_all(array, axes, split_axis=0, concat_axis=0, tiled=True)  12.1 us
    ppermute x1, waiting for transfers between devices, body(): onward = lax.ppermute(passed_on, ('x', 'core'), ONWARD)  5.53 us
    ppermute x1, waiting for transfers between devices, body(): behind = lax.ppermute(shard, 'x', AHEAD)  5.4 us
    pallas_call x2, Pallas kernels, product(): pl.pallas_call(product_kernel, out_shape=jax.ShapeDtypeStruct((width, PAN...  5.28 us
    ppermute x1, starting transfers between devices, body(): schur_part = schur_mine + lax.ppermute(schur_other, 'core', SWAP)  4.73 us
  transfers between devices with their start and end apart: 10, of which 6 were waited for; matrix products, arithmetic and copies ran while one was open for 4% of the time, Pallas kernels for 21%

profile of v7, /device:TPU:1, one launch (start us, length us, event | category | flops | bytes accessed | tf_op | source)
XLA Modules:
  0.0 125.3 jit_solution(11923307923198549873)
XLA Ops:
  0.0 0.6 pad_add_fusion.place_ref.core_ref
  0.6 4.1 %prepare.1 = (f32[16,8,1536]{2,1,0:T(8,128)}, f32[2,8,1536]{2,1,0:T(8,128)}, f32[1536,256]{1,0:T(8,128)}) custom-call(s32[2]{0:T(128)} %pad_add_fusion.place_ref.core_ref, s32[2]{0:T(128)} %counts_ref.1, f32[2,1536]{1,0:T(2,128)} %barrier_ref.1, f32[2,1536,256]{2,1,0:T(8,128)} %border_ref.1), custom_call_target="tpu_custom_call" | custom-call | tf_op jit(solution)/shard_map/prepare/pallas_call | solution.py:192
  4.6 0.0 copy-start.1
  4.6 0.0 copy-start
  4.7 12.0 %all-to-all-start = ((f32[16,8,1536]{2,1,0:T(8,128)}), f32[16,8,1536]{2,1,0:T(8,128)S(1)}, u32[]{:S(2)}, u32[]{:S(2)}) async-start(f32[16,8,1536]{2,1,0:T(8,128)} %get-tuple-element.14), calls=%async_computation | async-start | bytes 1572864 | tf_op jit(solution)/shard_map/all_to_all | solution.py:269
  16.6 0.0 copy-done.1
  16.6 13.7 %all-gather = f32[16,8,1536]{2,1,0:T(8,128)S(1)} all-gather(f32[2,8,1536]{2,1,0:T(8,128)S(1)} %copy-done.1), channel_id=2, replica_groups=mesh['scen'=8,'z'=8,'x'=4,'core'=2] {'x','core'}, dimensions={0}, use_global_device_ids=true | all-gather | bytes 884736 | tf_op jit(solution)/shard_map/all_gather | solution.py:282
  30.3 9.0 %all-to-all-done.along_ref = f32[16,8,1536]{2,1,0:T(8,128)S(1)} async-done(((f32[16,8,1536]{2,1,0:T(8,128)}), f32[16,8,1536]{2,1,0:T(8,128)S(1)}, u32[]{:S(2)}, u32[]{:S(2)}) %all-to-all-start) | async-done | bytes 786464 | tf_op jit(solution)/shard_map/all_to_all | solution.py:269
  39.3 3.1 %collective-permute-start = (f32[128,1536]{1,0:T(8,128)S(1)}, f32[128,1536]{1,0:T(8,128)S(1)}, u32[]{:S(2)}, u32[]{:S(2)}) collective-permute-start(f32[128,1536]{1,0:T(8,128)S(1)} %bitcast.11), channel_id=1, source_target_pairs={{0,2},{2,4},{4,6},{6,0},{1,3},{3,5},{5,7},{7,1},{8,10},{10,12},{12... | collective-permute-start | bytes 2359304 | tf_op jit(solution)/shard_map/ppermute | solution.py:286
  42.4 3.4 %collective-permute-start.1 = (f32[128,1536]{1,0:T(8,128)S(1)}, f32[128,1536]{1,0:T(8,128)S(1)}, u32[]{:S(2)}, u32[]{:S(2)}) collective-permute-start(f32[128,1536]{1,0:T(8,128)S(1)} %bitcast.12), channel_id=1, source_target_pairs={{0,6},{2,0},{4,2},{6,4},{1,7},{3,1},{5,3},{7,5},{8,14},{10,8},{12,... | collective-permute-start | bytes 2359304 | tf_op jit(solution)/shard_map/ppermute | solution.py:287
  45.8 0.0 copy-done
  45.8 2.1 %block_part.1 = f32[16,32,128]{2,1,0:T(8,128)} custom-call(s32[2]{0:T(128)S(1)} %copy-done, f32[16,8,1536]{2,1,0:T(8,128)S(1)} %all-to-all-done.along_ref, f32[8,2,8,1536]{3,2,1,0:T(8,128)S(1)} %bitcast.15), custom_call_target="tpu_custom_call" | custom-call | tf_op jit(solution)/shard_map/block_part/pallas_call | solution.py:227
  47.9 7.2 %all-to-all-start.1 = ((f32[16,32,128]{2,1,0:T(8,128)}), f32[16,32,128]{2,1,0:T(8,128)S(1)}, u32[]{:S(2)}, u32[]{:S(2)}) async-start(f32[16,32,128]{2,1,0:T(8,128)} %block_part.1), calls=%async_computation.1 | async-start | bytes 524288 | tf_op jit(solution)/shard_map/all_to_all | solution.py:269
  55.1 5.4 %collective-permute-done.refs_1_ = f32[128,1536]{1,0:T(8,128)S(1)} collective-permute-done((f32[128,1536]{1,0:T(8,128)S(1)}, f32[128,1536]{1,0:T(8,128)S(1)}, u32[]{:S(2)}, u32[]{:S(2)}) %collective-permute-start) | collective-permute-done | bytes 786464 | tf_op jit(solution)/shard_map/ppermute | solution.py:286
  60.5 2.2 %collective-permute-done.1.refs_2_ = f32[128,1536]{1,0:T(8,128)S(1)} collective-permute-done((f32[128,1536]{1,0:T(8,128)S(1)}, f32[128,1536]{1,0:T(8,128)S(1)}, u32[]{:S(2)}, u32[]{:S(2)}) %collective-permute-start.1) | collective-permute-done | bytes 786464 | tf_op jit(solution)/shard_map/ppermute | solution.py:287
  62.7 1.0 broadcast_select_fusion
  63.7 3.1 %all-to-all-done.1 = f32[16,32,128]{2,1,0:T(8,128)S(1)} async-done(((f32[16,32,128]{2,1,0:T(8,128)}), f32[16,32,128]{2,1,0:T(8,128)S(1)}, u32[]{:S(2)}, u32[]{:S(2)}) %all-to-all-start.1) | async-done | bytes 262176 | tf_op jit(solution)/shard_map/all_to_all | solution.py:269
  66.9 1.9 %collective-permute-start.3 = (f32[1536,256]{1,0:T(8,128)}, f32[1536,256]{1,0:T(8,128)}, u32[]{:S(2)}, u32[]{:S(2)}) collective-permute-start(f32[1536,256]{1,0:T(8,128)} %get-tuple-element.21), channel_id=1, source_target_pairs={{0,1},{1,0},{2,3},{3,2},{4,5},{5,4},{6,7},{7,6},{8,9},{9,8},{10,11... | collective-permute-start | bytes 4718600 | tf_op jit(solution)/shard_map/ppermute | solution.py:302
  68.8 3.2 %collective-permute-start.2 = (f32[128,1536]{1,0:T(8,128)}, f32[128,1536]{1,0:T(8,128)S(1)}, u32[]{:S(2)}, u32[]{:S(2)}) collective-permute-start(f32[128,1536]{1,0:T(8,128)} %broadcast_select_fusion), channel_id=1, source_target_pairs={{0,2},{1,7},{2,4},{3,1},{4,6},{5,3},{6,0},{7,5},{8,10},{9,15},{10,... | collective-permute-start | bytes 2359304 | tf_op jit(solution)/shard_map/ppermute | solution.py:292
  72.0 0.9 broadcast_in_dim.3
  72.8 4.6 %all-to-all-start.3 = ((f32[32,32,128]{2,1,0:T(8,128)}), f32[32,32,128]{2,1,0:T(8,128)}, u32[]{:S(2)}, u32[]{:S(2)}) async-start(f32[32,32,128]{2,1,0:T(8,128)} %broadcast_in_dim.3), calls=%async_computation.3 | async-start | bytes 1048576 | tf_op jit(solution)/shard_map/all_to_all | solution.py:269
  77.5 5.5 %collective-permute-done.2.refs_3_ = f32[128,1536]{1,0:T(8,128)S(1)} collective-permute-done((f32[128,1536]{1,0:T(8,128)}, f32[128,1536]{1,0:T(8,128)S(1)}, u32[]{:S(2)}, u32[]{:S(2)}) %collective-permute-start.2) | collective-permute-done | bytes 786464 | tf_op jit(solution)/shard_map/ppermute | solution.py:292
  83.0 0.0 collective-permute-done.3.columns_ref
  83.0 3.8 %product.3 = f32[256,512]{1,0:T(8,128)} custom-call(f32[1536,256]{1,0:T(8,128)} %collective-permute-done.3.columns_ref, f32[128,1536]{1,0:T(8,128)S(1)} %bitcast.13, f32[128,1536]{1,0:T(8,128)S(1)} %collective-permute-done.refs_1_, f32[128,1536]{1,0:T(8,128)S(1)} %collective-permute-done.1.refs_2_, f32[128,1536]{1,0:T(8,128)S(1)} %collective-permute-done.2.refs_3_), custom_call_target="tpu_custom_call" | custom-call | flops 1207959552 | bytes 4718592 | tf_op jit(solution)/shard_map/product/pallas_call | solution.py:255
  86.8 4.7 %collective-permute-start.4 = (f32[256,512]{1,0:T(8,128)}, f32[256,512]{1,0:T(8,128)}, u32[]{:S(2)}, u32[]{:S(2)}) collective-permute-start(f32[256,512]{1,0:T(8,128)} %product.3), channel_id=1, source_target_pairs={{0,1},{1,0},{2,3},{3,2},{4,5},{5,4},{6,7},{7,6},{8,9},{9,8},{10,11... | collective-permute-start | bytes 1572872 | tf_op jit(solution)/shard_map/ppermute | solution.py:306
  91.5 1.5 %dynamic-slice_bitcast_fusion.columns_ref = f32[1536,256]{1,0:T(8,128)S(1)} fusion(f32[2,1536,256]{2,1,0:T(8,128)} %border_ref.1, s32[]{:T(128)S(6)} %select_n.12), kind=kLoop, calls=%fused_computation | loop fusion | bytes 3145732 | tf_op jit(solution)/shard_map/jit(dynamic_index_in_dim)/squeeze | solution.py:303
  93.0 1.5 %product.2 = f32[256,512]{1,0:T(8,128)S(1)} custom-call(f32[1536,256]{1,0:T(8,128)S(1)} %dynamic-slice_bitcast_fusion.columns_ref, f32[128,1536]{1,0:T(8,128)S(1)} %bitcast.14, f32[128,1536]{1,0:T(8,128)S(1)} %collective-permute-done.refs_1_, f32[128,1536]{1,0:T(8,128)S(1)} %collective-permute-done.1.refs_2_, f32[128,1536]{1,0:T(8,128)S(1)} %collective-permute-done.2.refs_3_), custom_call_target="tpu_custom_call" | custom-call | flops 1207959552 | bytes 4718592 | tf_op jit(solution)/shard_map/product/pallas_call | solution.py:255
  94.6 0.0 collective-permute-done.4
  94.6 1.9 %add.8 = f32[256,512]{1,0:T(8,128)} add(f32[256,512]{1,0:T(8,128)S(1)} %product.2, f32[256,512]{1,0:T(8,128)} %collective-permute-done.4) | non-fusion elementwise | flops 131072 | bytes 1572864 | tf_op jit(solution)/shard_map/add | solution.py:306
  96.5 0.0 all-to-all-done.3.own_ref
  96.5 3.5 %all-to-all-start.2 = ((f32[8,32,512]{2,1,0:T(8,128)}), f32[8,32,512]{2,1,0:T(8,128)S(1)}, u32[]{:S(2)}, u32[]{:S(2)}) async-start(f32[8,32,512]{2,1,0:T(8,128)} %bitcast.5), calls=%async_computation.2 | async-start | bytes 1048576 | tf_op jit(solution)/shard_map/all_to_all | solution.py:269
  100.0 3.6 %collective-permute-start.5 = (f32[32,32,128]{2,1,0:T(8,128)}, f32[32,32,128]{2,1,0:T(8,128)S(1)}, u32[]{:S(2)}, u32[]{:S(2)}) collective-permute-start(f32[32,32,128]{2,1,0:T(8,128)} %all-to-all-done.3.own_ref), channel_id=1, source_target_pairs={{0,1},{1,0},{2,3},{3,2},{4,5},{5,4},{6,7},{7,6},{8,9},{9,8},{10,11... | collective-permute-start | bytes 1572872 | tf_op jit(solution)/shard_map/ppermute | solution.py:298
  103.6 1.5 %collective-permute-done.5.other_ref = f32[32,32,128]{2,1,0:T(8,128)S(1)} collective-permute-done((f32[32,32,128]{2,1,0:T(8,128)}, f32[32,32,128]{2,1,0:T(8,128)S(1)}, u32[]{:S(2)}, u32[]{:S(2)}) %collective-permute-start.5) | collective-permute-done | bytes 524320 | tf_op jit(solution)/shard_map/ppermute | solution.py:298
  105.2 18.7 %inverse_factor.1 = f32[512,512]{1,0:T(8,128)S(1)} custom-call(s32[2]{0:T(128)S(1)} %copy-done, f32[32,32,128]{2,1,0:T(8,128)} %all-to-all-done.3.own_ref, f32[32,32,128]{2,1,0:T(8,128)S(1)} %collective-permute-done.5.other_ref), custom_call_target="tpu_custom_call" | custom-call | flops 536870912 | bytes 2097152 | tf_op jit(solution)/shard_map/inverse_factor/pallas_call | solution.py:155
  123.9 0.0 all-to-all-done.2
  123.9 1.3 %convolution_bitcast_fusion = f32[1,1,32,512]{3,2,1,0:T(8,128)} fusion(f32[32,512]{1,0:T(8,128)S(1)} %reduce_sum.19, f32[512,512]{1,0:T(8,128)S(1)} %inverse_factor.1), kind=kOutput, calls=%fused_computation.1 | convolution fusion | flops 100663296 | bytes 1179648 | tf_op jit(solution)/shard_map/dot_general | solution.py:19
  (2 shorter events, 0.1 us)
Async XLA Ops:
  4.6 12.0 %copy-start.1 = (f32[2,8,1536]{2,1,0:T(8,128)S(1)}, f32[2,8,1536]{2,1,0:T(8,128)}, u32[]{:S(2)}) copy-start(f32[2,8,1536]{2,1,0:T(8,128)} %get-tuple-element.15) | copy-start | bytes 294916
  4.6 41.2 %copy-start = (s32[2]{0:T(128)S(1)}, s32[2]{0:T(128)}, u32[]{:S(2)}) copy-start(s32[2]{0:T(128)} %pad_add_fusion.place_ref.core_ref) | copy-start | bytes 28
  4.7 34.6 %all-to-all-start = ((f32[16,8,1536]{2,1,0:T(8,128)}), f32[16,8,1536]{2,1,0:T(8,128)S(1)}, u32[]{:S(2)}, u32[]{:S(2)}) async-start(f32[16,8,1536]{2,1,0:T(8,128)} %get-tuple-element.14), calls=%async_computation | async-start | bytes 1572864 | tf_op jit(solution)/shard_map/all_to_all | solution.py:269
  39.3 21.2 %collective-permute-start = (f32[128,1536]{1,0:T(8,128)S(1)}, f32[128,1536]{1,0:T(8,128)S(1)}, u32[]{:S(2)}, u32[]{:S(2)}) collective-permute-start(f32[128,1536]{1,0:T(8,128)S(1)} %bitcast.11), channel_id=1, source_target_pairs={{0,2},{2,4},{4,6},{6,0},{1,3},{3,5},{5,7},{7,1},{8,10},{10,12},{12... | collective-permute-start | bytes 2359304 | tf_op jit(solution)/shard_map/ppermute | solution.py:286
  42.4 20.3 %collective-permute-start.1 = (f32[128,1536]{1,0:T(8,128)S(1)}, f32[128,1536]{1,0:T(8,128)S(1)}, u32[]{:S(2)}, u32[]{:S(2)}) collective-permute-start(f32[128,1536]{1,0:T(8,128)S(1)} %bitcast.12), channel_id=1, source_target_pairs={{0,6},{2,0},{4,2},{6,4},{1,7},{3,1},{5,3},{7,5},{8,14},{10,8},{12,... | collective-permute-start | bytes 2359304 | tf_op jit(solution)/shard_map/ppermute | solution.py:287
  47.9 18.9 %all-to-all-start.1 = ((f32[16,32,128]{2,1,0:T(8,128)}), f32[16,32,128]{2,1,0:T(8,128)S(1)}, u32[]{:S(2)}, u32[]{:S(2)}) async-start(f32[16,32,128]{2,1,0:T(8,128)} %block_part.1), calls=%async_computation.1 | async-start | bytes 524288 | tf_op jit(solution)/shard_map/all_to_all | solution.py:269
  66.9 16.1 %collective-permute-start.3 = (f32[1536,256]{1,0:T(8,128)}, f32[1536,256]{1,0:T(8,128)}, u32[]{:S(2)}, u32[]{:S(2)}) collective-permute-start(f32[1536,256]{1,0:T(8,128)} %get-tuple-element.21), channel_id=1, source_target_pairs={{0,1},{1,0},{2,3},{3,2},{4,5},{5,4},{6,7},{7,6},{8,9},{9,8},{10,11... | collective-permute-start | bytes 4718600 | tf_op jit(solution)/shard_map/ppermute | solution.py:302
  68.8 14.2 %collective-permute-start.2 = (f32[128,1536]{1,0:T(8,128)}, f32[128,1536]{1,0:T(8,128)S(1)}, u32[]{:S(2)}, u32[]{:S(2)}) collective-permute-start(f32[128,1536]{1,0:T(8,128)} %broadcast_select_fusion), channel_id=1, source_target_pairs={{0,2},{1,7},{2,4},{3,1},{4,6},{5,3},{6,0},{7,5},{8,10},{9,15},{10,... | collective-permute-start | bytes 2359304 | tf_op jit(solution)/shard_map/ppermute | solution.py:292
  72.8 23.7 %all-to-all-start.3 = ((f32[32,32,128]{2,1,0:T(8,128)}), f32[32,32,128]{2,1,0:T(8,128)}, u32[]{:S(2)}, u32[]{:S(2)}) async-start(f32[32,32,128]{2,1,0:T(8,128)} %broadcast_in_dim.3), calls=%async_computation.3 | async-start | bytes 1048576 | tf_op jit(solution)/shard_map/all_to_all | solution.py:269
  86.8 7.8 %collective-permute-start.4 = (f32[256,512]{1,0:T(8,128)}, f32[256,512]{1,0:T(8,128)}, u32[]{:S(2)}, u32[]{:S(2)}) collective-permute-start(f32[256,512]{1,0:T(8,128)} %product.3), channel_id=1, source_target_pairs={{0,1},{1,0},{2,3},{3,2},{4,5},{5,4},{6,7},{7,6},{8,9},{9,8},{10,11... | collective-permute-start | bytes 1572872 | tf_op jit(solution)/shard_map/ppermute | solution.py:306
  96.5 27.4 %all-to-all-start.2 = ((f32[8,32,512]{2,1,0:T(8,128)}), f32[8,32,512]{2,1,0:T(8,128)S(1)}, u32[]{:S(2)}, u32[]{:S(2)}) async-start(f32[8,32,512]{2,1,0:T(8,128)} %bitcast.5), calls=%async_computation.2 | async-start | bytes 1048576 | tf_op jit(solution)/shard_map/all_to_all | solution.py:269
  100.0 5.2 %collective-permute-start.5 = (f32[32,32,128]{2,1,0:T(8,128)}, f32[32,32,128]{2,1,0:T(8,128)S(1)}, u32[]{:S(2)}, u32[]{:S(2)}) collective-permute-start(f32[32,32,128]{2,1,0:T(8,128)} %all-to-all-done.3.own_ref), channel_id=1, source_target_pairs={{0,1},{1,0},{2,3},{3,2},{4,5},{5,4},{6,7},{7,6},{8,9},{9,8},{10,11... | collective-permute-start | bytes 1572872 | tf_op jit(solution)/shard_map/ppermute | solution.py:298

commit v8 on v7

--- a/solution.py
+++ b/solution.py
@@ -1,3 +1,4 @@
+import functools
 import jax
 import jax.numpy as jnp
 from jax import lax
@@ -22,6 +23,20 @@
     )
 
 
+def two_parts(x):
+    first = x.astype(jnp.bfloat16)
+    return first, (x - first.astype(jnp.float32)).astype(jnp.bfloat16)
+
+
+def dot_parts(a, b, dim_a, dim_b):
+    a, a_low = two_parts(a)
+    b, b_low = two_parts(b)
+    return lax.dot_general(
+        jnp.concatenate([a, a, a_low], axis=dim_a), jnp.concatenate([b, b_low, b], axis=dim_b),
+        (((dim_a,), (dim_b,)), ((), ())), preferred_element_type=jnp.float32,
+    )
+
+
 def reciprocal(x):
     return pltpu.reciprocal(x, approx=True)
 
@@ -44,14 +59,19 @@
     return first, second, x - first - second
 
 
-def factor_inverse(diagonal):
+def factor_inverse(diagonal, beside=()):
     count = BLOCK // TILE
     row_of = lax.broadcasted_iota(jnp.int32, (TILE, BLOCK), 0)
     col_of = lax.broadcasted_iota(jnp.int32, (TILE, BLOCK), 1)
     left = [diagonal[TILE * t:TILE * (t + 1), :] for t in range(count)]
     right = [jnp.where(col_of == row_of + TILE * t, jnp.float32(1.0), jnp.float32(0.0)) for t in range(count)]
     done = []
+    beside = list(beside)
     for s in range(count):
+        share = -(-len(beside) // (count - s))
+        for step in beside[:share]:
+            step()
+        beside = beside[share:]
         own = [spread(left[s][:, TILE * s + c:TILE * s + c + 1]) for c in range(TILE)]
         rest = [[spread(own[c][r:r + 1, :]) for c in range(r + 1)] for r in range(TILE)]
         up = [[spread(side[s][r:r + 1, :]) for r in range(TILE)] for side in (left, right)]
@@ -125,29 +145,54 @@
                         rest[pl.ds(at, 16), pl.ds(128 * pair, 128)] = jnp.concatenate(
                             [one[:, 64 * h:64 * (h + 1)], two[:, 64 * h:64 * (h + 1)]], axis=1
                         )
-    sums[...] = jnp.zeros_like(sums)
-    lower[...] = jnp.zeros_like(lower)
-    for a in range(0, PANEL, BLOCK):
-        b = a + BLOCK
-        inverse = factor_inverse(rest[a:b, a:b])
-        lower[a:b, a:b] = inverse
-        if a > 0:
-            lower[a:b, 0:a] = -dot(inverse, sums[a:b, 0:a], 1, 0)
-        if b < PANEL:
-            upper = dot(inverse, rest[a:b, b:PANEL], 1, 0)
-            rest[b:PANEL, b:PANEL] = rest[b:PANEL, b:PANEL] - dot(upper, upper, 0, 0)
-            sums[b:PANEL, 0:b] = sums[b:PANEL, 0:b] + dot(upper, lower[a:b, 0:b], 0, 0)
     slots = []
     for x in range(4):
         ahead = lax.rem(x - place_ref[1] + 4, 4)
         slots.append(jnp.where(ahead == 0, 0, jnp.where(ahead == 3, 1, ahead + 1)))
-    for k in range(0, PANEL, BLOCK):
-        for a in range(0, PANEL, BLOCK):
-            turned = jnp.transpose(lower[a:a + BLOCK, k:k + BLOCK]) if a >= k else jnp.zeros((BLOCK, BLOCK), jnp.float32)
-            for piece in range(0, BLOCK, 16):
-                z, x = divmod((k + piece) // 16, 4)
-                to = pl.multiple_of(slots[x] * 128 + 16 * z, 16)
-                out_ref[pl.ds(to, 16), a:a + BLOCK] = turned[piece:piece + 16, :]
+
+    def write(row, column, block):
+        turned = None if block is None else jnp.transpose(block)
+        for piece in range(0, BLOCK, 16):
+            z, x = divmod((column + piece) // 16, 4)
+            to = pl.multiple_of(slots[x] * 128 + 16 * z, 16)
+            values = jnp.zeros((16, BLOCK), jnp.float32) if turned is None else turned[piece:piece + 16, :]
+            out_ref[pl.ds(to, 16), row:row + BLOCK] = values
+
+    starts = range(0, PANEL, BLOCK)
+    at = {a: slice(a, a + BLOCK) for a in starts}
+    beside = [functools.partial(write, a, k, None) for a in starts for k in starts if k > a]
+    diagonal = rest[at[0], at[0]]
+    for a in starts:
+        inverse = factor_inverse(diagonal, beside)
+        beside = []
+        later = [i for i in starts if i > a]
+        upper = {}
+        if later:
+            near = later[0]
+            upper[near] = dot_parts(inverse, rest[at[a], at[near]], 1, 0)
+            diagonal = rest[at[near], at[near]] - dot_parts(upper[near], upper[near], 0, 0)
+
+        def finish(k, a=a, inverse=inverse):
+            block = inverse if k == a else -dot_parts(inverse, sums[at[a], at[k]], 1, 0)
+            lower[at[a], at[k]] = block
+            write(a, k, block)
+
+        def above(j, a=a, inverse=inverse, upper=upper):
+            upper[j] = dot_parts(inverse, rest[at[a], at[j]], 1, 0)
+
+        def update(i, j, upper=upper):
+            rest[at[i], at[j]] = rest[at[i], at[j]] - dot_parts(upper[i], upper[j], 0, 0)
+
+        def gather(i, k, a=a, upper=upper):
+            term = dot_parts(upper[i], lower[at[a], at[k]], 0, 0)
+            sums[at[i], at[k]] = term if k == a else sums[at[i], at[k]] + term
+
+        beside += [functools.partial(above, j) for j in later[1:]]
+        beside += [functools.partial(update, i, j) for i in later for j in later if j >= i and j > later[0]]
+        beside += [functools.partial(finish, k) for k in starts if k <= a]
+        beside += [functools.partial(gather, i, k) for i in later for k in starts if k <= a]
+    for step in beside:
+        step()
 
 
 def inverse_factor(place, own, other):
@@ -164,14 +209,14 @@
     )(place, own, other)
 
 
-def prepare_kernel(place_ref, counts_ref, barrier_ref, border_ref, along_ref, beside_ref, other_ref, columns, arrived, moved):
+def prepare_kernel(counts_ref, barrier_ref, border_ref, along_ref, beside_ref, other_ref, columns, arrived, moved):
     capacity = barrier_ref.shape[1]
     copies = [
         pltpu.make_async_copy(border_ref.at[s, :, pl.ds(0, 128)], columns.at[s], arrived.at[s]) for s in range(2)
     ]
     for copy in copies:
         copy.start()
-    other = pltpu.make_async_copy(border_ref.at[1 - place_ref[0]], other_ref, moved)
+    other = pltpu.make_async_copy(border_ref.at[1 - lax.axis_index("core")], other_ref, moved)
     other.start()
     position = lax.broadcasted_iota(jnp.int32, (1, capacity), 1)
     for s in range(2):
@@ -186,7 +231,7 @@
     other.wait()
 
 
-def prepare(place, row_counts, barrier, border):
+def prepare(row_counts, barrier, border):
     capacity = border.shape[1]
     vmem = pl.BlockSpec(memory_space=pltpu.VMEM)
     return pl.pallas_call(
@@ -196,7 +241,7 @@
             jax.ShapeDtypeStruct((2, TILE, capacity), jnp.float32),
             jax.ShapeDtypeStruct(border.shape[1:], jnp.float32),
         ),
-        in_specs=[pl.BlockSpec(memory_space=pltpu.SMEM)] * 2 + [vmem, pl.BlockSpec(memory_space=pltpu.HBM)],
+        in_specs=[pl.BlockSpec(memory_space=pltpu.SMEM), vmem, pl.BlockSpec(memory_space=pltpu.HBM)],
         out_specs=(vmem, vmem, vmem),
         scratch_shapes=[
             pltpu.VMEM((2, capacity, 128), jnp.float32),
@@ -205,14 +250,14 @@
         ],
         compiler_params=pltpu.CompilerParams(vmem_limit_bytes=60 << 20),
         name="prepare",
-    )(place, row_counts, barrier, border)
+    )(row_counts, barrier, border)
 
 
 def block_kernel(core_ref, along_ref, beside_ref, out_ref):
     along = along_ref[...].reshape(16 * TILE, -1)
     scenario = pl.ds(core_ref[0], 1)
     beside = jnp.concatenate([beside_ref[p, scenario, :, :].reshape(TILE, -1) for p in range(8)], axis=0)
-    part = dot(along, beside, 1, 1)
+    part = dot_parts(along, beside, 1, 1)
     quarter = 4 * TILE
     for c in range(2):
         first = part[2 * c * quarter:(2 * c + 1) * quarter]
@@ -234,35 +279,38 @@
     )(core, along, beside)
 
 
-def two_parts(x):
-    first = x.astype(jnp.bfloat16)
-    return first, (x - first.astype(jnp.float32)).astype(jnp.bfloat16)
-
-
 def product_kernel(columns_ref, *refs):
     *panel_refs, out_ref = refs
+    panel = jnp.concatenate([ref[...] for ref in panel_refs], axis=0)
     columns, columns_low = two_parts(columns_ref[...])
-    panel, panel_low = two_parts(jnp.concatenate([ref[...] for ref in panel_refs], axis=0))
+    panel, panel_low = two_parts(panel)
     total = jnp.dot(panel, columns, preferred_element_type=jnp.float32)
     total = total + jnp.dot(panel, columns_low, preferred_element_type=jnp.float32)
     total = total + jnp.dot(panel_low, columns, preferred_element_type=jnp.float32)
-    out_ref[...] = jnp.transpose(total)
-
-
-def product(columns, panels):
+    out_ref[:, out_ref.shape[1] - total.shape[0]:] = jnp.transpose(total)
+
+
+def further_kernel(columns_ref, panel_ref, before_ref, out_ref):
+    out_ref[:, :before_ref.shape[1]] = before_ref[...]
+    product_kernel(columns_ref, panel_ref, out_ref)
+
+
+def product(columns, panels, before=None):
     rows, width = columns.shape
+    fresh = sum(panel.shape[0] for panel in panels)
+    done = () if before is None else (before,)
     vmem = pl.BlockSpec(memory_space=pltpu.VMEM)
     return pl.pallas_call(
-        product_kernel,
-        out_shape=jax.ShapeDtypeStruct((width, PANEL), jnp.float32),
-        in_specs=[vmem] * (1 + len(panels)),
+        further_kernel if done else product_kernel,
+        out_shape=jax.ShapeDtypeStruct((width, fresh + sum(b.shape[1] for b in done)), jnp.float32),
+        in_specs=[vmem] * (1 + len(panels) + len(done)),
         out_specs=vmem,
         compiler_params=pltpu.CompilerParams(vmem_limit_bytes=32 << 20),
         cost_estimate=pl.CostEstimate(
-            flops=6 * rows * width * PANEL, bytes_accessed=4 * rows * (width + PANEL), transcendentals=0
+            flops=6 * rows * width * fresh, bytes_accessed=4 * rows * (width + fresh), transcendentals=0
         ),
-        name="product",
-    )(columns, *panels)
+        name="further" if done else "product",
+    )(columns, *panels, *done)
 
 
 def exchange(array, axes):
@@ -277,7 +325,7 @@
     core = lax.axis_index("core")
     place = jnp.stack([core, lax.axis_index("x")])
 
-    to_along, to_beside, to_other = prepare(place, row_counts, barrier, border)
+    to_along, to_beside, to_other = prepare(row_counts, barrier, border)
     along = exchange(to_along, ("z", "core"))
     beside = lax.all_gather(to_beside, ("x", "core"), axis=0, tiled=False)
     along, beside = lax.optimization_barrier((along, beside))
@@ -298,11 +346,13 @@
     other_half = lax.ppermute(own_half, "core", SWAP)
     inverse = inverse_factor(place, own_half, other_half)
 
-    panels = (shard, behind, ahead, onward)
     other = lax.ppermute(to_other, "core", SWAP)
     mine = lax.dynamic_index_in_dim(border, core, 0, keepdims=False)
-    schur_other = product(other, panels)
-    schur_mine = product(mine, panels)
+    schur_other = product(other, (shard, behind, ahead))
+    schur_mine = product(mine, (shard, behind, ahead))
+    onward, schur_other, schur_mine = lax.optimization_barrier((onward, schur_other, schur_mine))
+    schur_other = product(other, (onward,), schur_other)
+    schur_mine = product(mine, (onward,), schur_mine)
     schur_part = schur_mine + lax.ppermute(schur_other, "core", SWAP)
     owned = jnp.sum(exchange(schur_part.reshape(n_scen, rows_owned, PANEL), "scen"), axis=0)
     solved = dot(owned, inverse, 1, 0)

time: 126 us -> 124 us (0.984)
  starting transfers between devices: 47.2 us -> 51.2 us
  waiting for transfers between devices: 26.8 us -> 22.9 us
  other arithmetic: 3.56 us -> 1.98 us
    ppermute x1, waiting for transfers between devices: 5.53 us -> 0.18 us  [body(): onward = lax.ppermute(passed_on, ('x', 'core'), ONWARD)]
    ppermute x1, starting transfers between devices: 3.61 us -> 5.77 us  [body(): other_half = lax.ppermute(own_half, 'core', SWAP)]
    all_to_all x4, starting transfers between devices: 27.3 us -> 29.1 us  [exchange(): return lax.all_to_all(array, axes, split_axis=0, concat_axis=0, tiled=True)]
    pallas_call x1, Pallas kernels: 18.7 us -> 17.1 us  [inverse_factor(): pl.pallas_call(inverse_kernel, out_shape=jax.ShapeDtypeStruct(shape, jnp....]
    pallas_call x2 -> x4, Pallas kernels: 5.28 us -> 6.47 us  [product(): pl.pallas_call(further_kernel if done else product_kernel, out_shape=jax....]
  transfers between devices with their start and end apart: 10 -> 10, of which waited for: 6 -> 8; matrix products, arithmetic and copies ran while one was open for 4% -> 3% of each run, Pallas kernels for 21% -> 21%
where the time goes in v8:
time: 124 us; the launch traced here: 123 us
  starting transfers between devices  51.2 us (41%)
  Pallas kernels  29.4 us (24%)
  waiting for transfers between devices  22.9 us (18%)
  blocking collectives  13.7 us (11%)
  local copies, waits for them, and re-layouts  2.38 us (2%)
  other arithmetic  1.98 us (2%)
  matrix products  1.34 us (1%)
    all_to_all x4, starting transfers between devices, exchange(): return lax.all_to_all(array, axes, split_axis=0, concat_axis=0, tiled=True)  29.1 us
    pallas_call x1, Pallas kernels, inverse_factor(): pl.pallas_call(inverse_kernel, out_shape=jax.ShapeDtypeStruct(shape, jnp....  17.1 us
    all_gather x1, blocking collectives, body(): beside = lax.all_gather(to_beside, ('x', 'core'), axis=0, tiled=False)  13.7 us
    all_to_all x4, waiting for transfers between devices, exchange(): return lax.all_to_all(array, axes, split_axis=0, concat_axis=0, tiled=True)  12.5 us
    pallas_call x4, Pallas kernels, product(): pl.pallas_call(further_kernel if done else product_kernel, out_shape=jax....  6.47 us
    ppermute x1, starting transfers between devices, body(): other_half = lax.ppermute(own_half, 'core', SWAP)  5.77 us
    ppermute x1, waiting for transfers between devices, body(): behind = lax.ppermute(shard, 'x', AHEAD)  5.64 us
    ppermute x1, starting transfers between devices, body(): schur_part = schur_mine + lax.ppermute(schur_other, 'core', SWAP)  4.74 us
  transfers between devices with their start and end apart: 10, of which 8 were waited for; matrix products, arithmetic and copies ran while one was open for 3% of the time, Pallas kernels for 21%

profile of v8, /device:TPU:1, one launch (start us, length us, event | category | flops | bytes accessed | tf_op | source)
XLA Modules:
  0.0 123.1 jit_solution(17171414102779543904)
XLA Ops:
  0.0 4.1 %prepare.1 = (f32[16,8,1536]{2,1,0:T(8,128)}, f32[2,8,1536]{2,1,0:T(8,128)}, f32[1536,256]{1,0:T(8,128)}) custom-call(s32[2]{0:T(128)} %counts_ref.1, f32[2,1536]{1,0:T(2,128)} %barrier_ref.1, f32[2,1536,256]{2,1,0:T(8,128)} %border_ref.1), custom_call_target="tpu_custom_call" | custom-call | tf_op jit(solution)/shard_map/prepare/pallas_call | solution.py:237
  4.1 0.0 copy-start
  4.1 12.0 %all-to-all-start = ((f32[16,8,1536]{2,1,0:T(8,128)}), f32[16,8,1536]{2,1,0:T(8,128)S(1)}, u32[]{:S(2)}, u32[]{:S(2)}) async-start(f32[16,8,1536]{2,1,0:T(8,128)} %get-tuple-element.17), calls=%async_computation | async-start | bytes 1572864 | tf_op jit(solution)/shard_map/all_to_all | solution.py:317
  16.0 0.0 copy-done
  16.1 13.7 %all-gather = f32[16,8,1536]{2,1,0:T(8,128)S(1)} all-gather(f32[2,8,1536]{2,1,0:T(8,128)S(1)} %copy-done), channel_id=2, replica_groups=mesh['scen'=8,'z'=8,'x'=4,'core'=2] {'x','core'}, dimensions={0}, use_global_device_ids=true | all-gather | bytes 884736 | tf_op jit(solution)/shard_map/all_gather | solution.py:330
  29.7 9.0 %all-to-all-done.along_ref = f32[16,8,1536]{2,1,0:T(8,128)S(1)} async-done(((f32[16,8,1536]{2,1,0:T(8,128)}), f32[16,8,1536]{2,1,0:T(8,128)S(1)}, u32[]{:S(2)}, u32[]{:S(2)}) %all-to-all-start) | async-done | bytes 786464 | tf_op jit(solution)/shard_map/all_to_all | solution.py:317
  38.7 3.1 %collective-permute-start = (f32[128,1536]{1,0:T(8,128)S(1)}, f32[128,1536]{1,0:T(8,128)S(1)}, u32[]{:S(2)}, u32[]{:S(2)}) collective-permute-start(f32[128,1536]{1,0:T(8,128)S(1)} %bitcast.11), channel_id=1, source_target_pairs={{0,2},{2,4},{4,6},{6,0},{1,3},{3,5},{5,7},{7,1},{8,10},{10,12},{12... | collective-permute-start | bytes 2359304 | tf_op jit(solution)/shard_map/ppermute | solution.py:334
  41.8 3.4 %collective-permute-start.1 = (f32[128,1536]{1,0:T(8,128)S(1)}, f32[128,1536]{1,0:T(8,128)S(1)}, u32[]{:S(2)}, u32[]{:S(2)}) collective-permute-start(f32[128,1536]{1,0:T(8,128)S(1)} %bitcast.12), channel_id=1, source_target_pairs={{0,6},{2,0},{4,2},{6,4},{1,7},{3,1},{5,3},{7,5},{8,14},{10,8},{12,... | collective-permute-start | bytes 2359304 | tf_op jit(solution)/shard_map/ppermute | solution.py:335
  45.2 0.1 pad_add_fusion.core_ref.place_ref
  45.3 1.8 %block_part.1 = f32[16,32,128]{2,1,0:T(8,128)} custom-call(s32[2]{0:T(128)S(1)} %pad_add_fusion.core_ref.place_ref, f32[16,8,1536]{2,1,0:T(8,128)S(1)} %all-to-all-done.along_ref, f32[8,2,8,1536]{3,2,1,0:T(8,128)S(1)} %bitcast.15), custom_call_target="tpu_custom_call" | custom-call | tf_op jit(solution)/shard_map/block_part/pallas_call | solution.py:272
  47.1 7.2 %all-to-all-start.1 = ((f32[16,32,128]{2,1,0:T(8,128)}), f32[16,32,128]{2,1,0:T(8,128)S(1)}, u32[]{:S(2)}, u32[]{:S(2)}) async-start(f32[16,32,128]{2,1,0:T(8,128)} %block_part.1), calls=%async_computation.1 | async-start | bytes 524288 | tf_op jit(solution)/shard_map/all_to_all | solution.py:317
  54.3 5.6 %collective-permute-done.refs_1_ = f32[128,1536]{1,0:T(8,128)S(1)} collective-permute-done((f32[128,1536]{1,0:T(8,128)S(1)}, f32[128,1536]{1,0:T(8,128)S(1)}, u32[]{:S(2)}, u32[]{:S(2)}) %collective-permute-start) | collective-permute-done | bytes 786464 | tf_op jit(solution)/shard_map/ppermute | solution.py:334
  59.9 2.2 %collective-permute-done.1.refs_2_ = f32[128,1536]{1,0:T(8,128)S(1)} collective-permute-done((f32[128,1536]{1,0:T(8,128)S(1)}, f32[128,1536]{1,0:T(8,128)S(1)}, u32[]{:S(2)}, u32[]{:S(2)}) %collective-permute-start.1) | collective-permute-done | bytes 786464 | tf_op jit(solution)/shard_map/ppermute | solution.py:335
  62.1 1.0 broadcast_select_fusion
  63.1 2.9 %all-to-all-done.1 = f32[16,32,128]{2,1,0:T(8,128)S(1)} async-done(((f32[16,32,128]{2,1,0:T(8,128)}), f32[16,32,128]{2,1,0:T(8,128)S(1)}, u32[]{:S(2)}, u32[]{:S(2)}) %all-to-all-start.1) | async-done | bytes 262176 | tf_op jit(solution)/shard_map/all_to_all | solution.py:317
  66.0 1.9 %collective-permute-start.3 = (f32[1536,256]{1,0:T(8,128)}, f32[1536,256]{1,0:T(8,128)}, u32[]{:S(2)}, u32[]{:S(2)}) collective-permute-start(f32[1536,256]{1,0:T(8,128)} %get-tuple-element.24), channel_id=1, source_target_pairs={{0,1},{1,0},{2,3},{3,2},{4,5},{5,4},{6,7},{7,6},{8,9},{9,8},{10,11... | collective-permute-start | bytes 4718600 | tf_op jit(solution)/shard_map/ppermute | solution.py:349
  68.0 3.2 %collective-permute-start.2 = (f32[128,1536]{1,0:T(8,128)}, f32[128,1536]{1,0:T(8,128)S(1)}, u32[]{:S(2)}, u32[]{:S(2)}) collective-permute-start(f32[128,1536]{1,0:T(8,128)} %broadcast_select_fusion), channel_id=1, source_target_pairs={{0,2},{1,7},{2,4},{3,1},{4,6},{5,3},{6,0},{7,5},{8,10},{9,15},{10,... | collective-permute-start | bytes 2359304 | tf_op jit(solution)/shard_map/ppermute | solution.py:340
  71.2 0.9 broadcast_in_dim.3
  72.0 4.6 %all-to-all-start.3 = ((f32[32,32,128]{2,1,0:T(8,128)}), f32[32,32,128]{2,1,0:T(8,128)}, u32[]{:S(2)}, u32[]{:S(2)}) async-start(f32[32,32,128]{2,1,0:T(8,128)} %broadcast_in_dim.3), calls=%async_computation.3 | async-start | bytes 1048576 | tf_op jit(solution)/shard_map/all_to_all | solution.py:317
  76.6 1.5 %dynamic-slice_bitcast_fusion.columns_ref = f32[1536,256]{1,0:T(8,128)S(1)} fusion(f32[2,1536,256]{2,1,0:T(8,128)} %border_ref.1, s32[]{:T(128)S(6)} %select_n.12), kind=kLoop, calls=%fused_computation | loop fusion | bytes 3145732 | tf_op jit(solution)/shard_map/jit(dynamic_index_in_dim)/squeeze | solution.py:350
  78.2 1.2 product.3.before_ref
  79.4 0.0 collective-permute-done.3.columns_ref
  79.4 2.6 %product.2.before_ref = f32[256,384]{1,0:T(8,128)S(1)} custom-call(f32[1536,256]{1,0:T(8,128)} %collective-permute-done.3.columns_ref, f32[128,1536]{1,0:T(8,128)S(1)} %bitcast.14, f32[128,1536]{1,0:T(8,128)S(1)} %collective-permute-done.refs_1_, f32[128,1536]{1,0:T(8,128)S(1)} %collective-permute-done.1.refs_2_), custom_call_target="tpu_custom_call" | custom-call | flops 905969664 | bytes 3932160 | tf_op jit(solution)/shard_map/product/pallas_call | solution.py:303
  82.0 0.2 collective-permute-done.2.panel_ref
  82.2 2.0 %further.3 = f32[256,512]{1,0:T(8,128)S(1)} custom-call(f32[1536,256]{1,0:T(8,128)} %collective-permute-done.3.columns_ref, f32[128,1536]{1,0:T(8,128)S(1)} %collective-permute-done.2.panel_ref, f32[256,384]{1,0:T(8,128)S(1)} %product.2.before_ref), custom_call_target="tpu_custom_call" | custom-call | flops 301989888 | bytes 2359296 | tf_op jit(solution)/shard_map/further/pallas_call | solution.py:303
  84.2 4.7 %collective-permute-start.4 = (f32[256,512]{1,0:T(8,128)S(1)}, f32[256,512]{1,0:T(8,128)S(1)}, u32[]{:S(2)}, u32[]{:S(2)}) collective-permute-start(f32[256,512]{1,0:T(8,128)S(1)} %further.3), channel_id=1, source_target_pairs={{0,1},{1,0},{2,3},{3,2},{4,5},{5,4},{6,7},{7,6},{8,9},{9,8},{10,11... | collective-permute-start | bytes 1572872 | tf_op jit(solution)/shard_map/ppermute | solution.py:356
  89.0 0.6 further.2
  89.6 0.9 collective-permute-done.4
  90.5 0.9 add.8
  91.4 0.6 all-to-all-done.3.own_ref
  92.0 5.3 %all-to-all-start.2 = ((f32[8,32,512]{2,1,0:T(8,128)}), f32[8,32,512]{2,1,0:T(8,128)S(1)}, u32[]{:S(2)}, u32[]{:S(2)}) async-start(f32[8,32,512]{2,1,0:T(8,128)} %bitcast.5), calls=%async_computation.2 | async-start | bytes 1048576 | tf_op jit(solution)/shard_map/all_to_all | solution.py:317
  97.3 5.8 %collective-permute-start.5 = (f32[32,32,128]{2,1,0:T(8,128)}, f32[32,32,128]{2,1,0:T(8,128)S(1)}, u32[]{:S(2)}, u32[]{:S(2)}) collective-permute-start(f32[32,32,128]{2,1,0:T(8,128)} %all-to-all-done.3.own_ref), channel_id=1, source_target_pairs={{0,1},{1,0},{2,3},{3,2},{4,5},{5,4},{6,7},{7,6},{8,9},{9,8},{10,11... | collective-permute-start | bytes 1572872 | tf_op jit(solution)/shard_map/ppermute | solution.py:346
  103.0 1.5 %collective-permute-done.5.other_ref = f32[32,32,128]{2,1,0:T(8,128)S(1)} collective-permute-done((f32[32,32,128]{2,1,0:T(8,128)}, f32[32,32,128]{2,1,0:T(8,128)S(1)}, u32[]{:S(2)}, u32[]{:S(2)}) %collective-permute-start.5) | collective-permute-done | bytes 524320 | tf_op jit(solution)/shard_map/ppermute | solution.py:346
  104.6 17.1 %inverse_factor.1 = f32[512,512]{1,0:T(8,128)S(1)} custom-call(s32[2]{0:T(128)S(1)} %pad_add_fusion.core_ref.place_ref, f32[32,32,128]{2,1,0:T(8,128)} %all-to-all-done.3.own_ref, f32[32,32,128]{2,1,0:T(8,128)S(1)} %collective-permute-done.5.other_ref), custom_call_target="tpu_custom_call" | custom-call | flops 536870912 | bytes 2097152 | tf_op jit(solution)/shard_map/inverse_factor/pallas_call | solution.py:200
  121.7 0.0 all-to-all-done.2
  121.7 1.3 %convolution_bitcast_fusion = f32[1,1,32,512]{3,2,1,0:T(8,128)} fusion(f32[32,512]{1,0:T(8,128)S(1)} %reduce_sum.19, f32[512,512]{1,0:T(8,128)S(1)} %inverse_factor.1), kind=kOutput, calls=%fused_computation.1 | convolution fusion | flops 100663296 | bytes 1179648 | tf_op jit(solution)/shard_map/dot_general | solution.py:20
  (2 shorter events, 0.1 us)
Async XLA Ops:
  4.1 12.0 %copy-start = (f32[2,8,1536]{2,1,0:T(8,128)S(1)}, f32[2,8,1536]{2,1,0:T(8,128)}, u32[]{:S(2)}) copy-start(f32[2,8,1536]{2,1,0:T(8,128)} %get-tuple-element.18) | copy-start | bytes 294916
  4.1 34.6 %all-to-all-start = ((f32[16,8,1536]{2,1,0:T(8,128)}), f32[16,8,1536]{2,1,0:T(8,128)S(1)}, u32[]{:S(2)}, u32[]{:S(2)}) async-start(f32[16,8,1536]{2,1,0:T(8,128)} %get-tuple-element.17), calls=%async_computation | async-start | bytes 1572864 | tf_op jit(solution)/shard_map/all_to_all | solution.py:317
  38.7 21.2 %collective-permute-start = (f32[128,1536]{1,0:T(8,128)S(1)}, f32[128,1536]{1,0:T(8,128)S(1)}, u32[]{:S(2)}, u32[]{:S(2)}) collective-permute-start(f32[128,1536]{1,0:T(8,128)S(1)} %bitcast.11), channel_id=1, source_target_pairs={{0,2},{2,4},{4,6},{6,0},{1,3},{3,5},{5,7},{7,1},{8,10},{10,12},{12... | collective-permute-start | bytes 2359304 | tf_op jit(solution)/shard_map/ppermute | solution.py:334
  41.8 20.3 %collective-permute-start.1 = (f32[128,1536]{1,0:T(8,128)S(1)}, f32[128,1536]{1,0:T(8,128)S(1)}, u32[]{:S(2)}, u32[]{:S(2)}) collective-permute-start(f32[128,1536]{1,0:T(8,128)S(1)} %bitcast.12), channel_id=1, source_target_pairs={{0,6},{2,0},{4,2},{6,4},{1,7},{3,1},{5,3},{7,5},{8,14},{10,8},{12,... | collective-permute-start | bytes 2359304 | tf_op jit(solution)/shard_map/ppermute | solution.py:335
  47.1 18.9 %all-to-all-start.1 = ((f32[16,32,128]{2,1,0:T(8,128)}), f32[16,32,128]{2,1,0:T(8,128)S(1)}, u32[]{:S(2)}, u32[]{:S(2)}) async-start(f32[16,32,128]{2,1,0:T(8,128)} %block_part.1), calls=%async_computation.1 | async-start | bytes 524288 | tf_op jit(solution)/shard_map/all_to_all | solution.py:317
  66.0 13.3 %collective-permute-start.3 = (f32[1536,256]{1,0:T(8,128)}, f32[1536,256]{1,0:T(8,128)}, u32[]{:S(2)}, u32[]{:S(2)}) collective-permute-start(f32[1536,256]{1,0:T(8,128)} %get-tuple-element.24), channel_id=1, source_target_pairs={{0,1},{1,0},{2,3},{3,2},{4,5},{5,4},{6,7},{7,6},{8,9},{9,8},{10,11... | collective-permute-start | bytes 4718600 | tf_op jit(solution)/shard_map/ppermute | solution.py:349
  68.0 14.2 %collective-permute-start.2 = (f32[128,1536]{1,0:T(8,128)}, f32[128,1536]{1,0:T(8,128)S(1)}, u32[]{:S(2)}, u32[]{:S(2)}) collective-permute-start(f32[128,1536]{1,0:T(8,128)} %broadcast_select_fusion), channel_id=1, source_target_pairs={{0,2},{1,7},{2,4},{3,1},{4,6},{5,3},{6,0},{7,5},{8,10},{9,15},{10,... | collective-permute-start | bytes 2359304 | tf_op jit(solution)/shard_map/ppermute | solution.py:340
  72.0 20.0 %all-to-all-start.3 = ((f32[32,32,128]{2,1,0:T(8,128)}), f32[32,32,128]{2,1,0:T(8,128)}, u32[]{:S(2)}, u32[]{:S(2)}) async-start(f32[32,32,128]{2,1,0:T(8,128)} %broadcast_in_dim.3), calls=%async_computation.3 | async-start | bytes 1048576 | tf_op jit(solution)/shard_map/all_to_all | solution.py:317
  84.2 6.3 %collective-permute-start.4 = (f32[256,512]{1,0:T(8,128)S(1)}, f32[256,512]{1,0:T(8,128)S(1)}, u32[]{:S(2)}, u32[]{:S(2)}) collective-permute-start(f32[256,512]{1,0:T(8,128)S(1)} %further.3), channel_id=1, source_target_pairs={{0,1},{1,0},{2,3},{3,2},{4,5},{5,4},{6,7},{7,6},{8,9},{9,8},{10,11... | collective-permute-start | bytes 1572872 | tf_op jit(solution)/shard_map/ppermute | solution.py:356
  92.0 29.7 %all-to-all-start.2 = ((f32[8,32,512]{2,1,0:T(8,128)}), f32[8,32,512]{2,1,0:T(8,128)S(1)}, u32[]{:S(2)}, u32[]{:S(2)}) async-start(f32[8,32,512]{2,1,0:T(8,128)} %bitcast.5), calls=%async_computation.2 | async-start | bytes 1048576 | tf_op jit(solution)/shard_map/all_to_all | solution.py:317
  97.3 7.3 %collective-permute-start.5 = (f32[32,32,128]{2,1,0:T(8,128)}, f32[32,32,128]{2,1,0:T(8,128)S(1)}, u32[]{:S(2)}, u32[]{:S(2)}) collective-permute-start(f32[32,32,128]{2,1,0:T(8,128)} %all-to-all-done.3.own_ref), channel_id=1, source_target_pairs={{0,1},{1,0},{2,3},{3,2},{4,5},{5,4},{6,7},{7,6},{8,9},{9,8},{10,11... | collective-permute-start | bytes 1572872 | tf_op jit(solution)/shard_map/ppermute | solution.py:346

commit v9 on v8

--- a/solution.py
+++ b/solution.py
@@ -133,18 +133,29 @@
 
 
 def inverse_kernel(place_ref, own_ref, other_ref, out_ref, rest, sums, lower):
-    core = place_ref[0]
-    for half_ref, half in ((own_ref, core), (other_ref, 1 - core)):
+    first = place_ref[0] == 0
+    side = BLOCK // 2
+    for z in range(8):
         for x in range(4):
-            for k in range(2):
-                for pair in range(4):
-                    one = half_ref[8 * pair + x, 16 * k:16 * (k + 1), :]
-                    two = half_ref[8 * pair + 4 + x, 16 * k:16 * (k + 1), :]
-                    for h in range(2):
-                        at = pl.multiple_of(half * 256, 256) + h * 128 + k * 64 + x * 16
-                        rest[pl.ds(at, 16), pl.ds(128 * pair, 128)] = jnp.concatenate(
-                            [one[:, 64 * h:64 * (h + 1)], two[:, 64 * h:64 * (h + 1)]], axis=1
-                        )
+            own, other = own_ref[4 * z + x], other_ref[4 * z + x]
+            halves = [jnp.where(first, own, other), jnp.where(first, other, own)]
+            middle = jnp.concatenate([half[16:16 + TILE, :side] for half in halves], axis=0)
+            pieces = [halves[0][:16, :side], halves[0][:16, side:], middle, halves[1][:16, :side], halves[1][:16, side:]]
+            for d, piece in enumerate(pieces):
+                to = 64 * ((z + d) % 8) + 16 * x
+                rest[to:to + 16, side * z:side * (z + 1)] = piece
+    low = lax.broadcasted_iota(jnp.int32, (BLOCK, BLOCK), 0) >= side
+    near = lax.broadcasted_iota(jnp.int32, (BLOCK, BLOCK), 1) < side
+    for i in range(0, PANEL, BLOCK):
+        for j in range(i, PANEL, BLOCK):
+            here, there = rest[j:j + BLOCK, i:i + BLOCK], rest[i:i + BLOCK, j:j + BLOCK]
+            turned = jnp.transpose(there)
+            if j == i:
+                rest[j:j + BLOCK, i:i + BLOCK] = jnp.where(low | near, here, turned)
+            elif j == i + 2 * BLOCK:
+                rest[j:j + BLOCK, i:i + BLOCK] = jnp.where(low & near, turned, here)
+            elif j == i + 3 * BLOCK:
+                rest[j:j + BLOCK, i:i + BLOCK] = turned
     slots = []
     for x in range(4):
         ahead = lax.rem(x - place_ref[1] + 4, 4)
@@ -169,7 +180,7 @@
         upper = {}
         if later:
             near = later[0]
-            upper[near] = dot_parts(inverse, rest[at[a], at[near]], 1, 0)
+            upper[near] = dot_parts(inverse, rest[at[near], at[a]], 1, 1)
             diagonal = rest[at[near], at[near]] - dot_parts(upper[near], upper[near], 0, 0)
 
         def finish(k, a=a, inverse=inverse):
@@ -178,10 +189,10 @@
             write(a, k, block)
 
         def above(j, a=a, inverse=inverse, upper=upper):
-            upper[j] = dot_parts(inverse, rest[at[a], at[j]], 1, 0)
+            upper[j] = dot_parts(inverse, rest[at[j], at[a]], 1, 1)
 
         def update(i, j, upper=upper):
-            rest[at[i], at[j]] = rest[at[i], at[j]] - dot_parts(upper[i], upper[j], 0, 0)
+            rest[at[j], at[i]] = rest[at[j], at[i]] - dot_parts(upper[j], upper[i], 0, 0)
 
         def gather(i, k, a=a, upper=upper):
             term = dot_parts(upper[i], lower[at[a], at[k]], 0, 0)
@@ -253,30 +264,39 @@
     )(row_counts, barrier, border)
 
 
-def block_kernel(core_ref, along_ref, beside_ref, out_ref):
+def block_kernel(along_ref, beside_ref, out_ref, part_ref):
     along = along_ref[...].reshape(16 * TILE, -1)
-    scenario = pl.ds(core_ref[0], 1)
+    scenario = pl.ds(lax.axis_index("core"), 1)
     beside = jnp.concatenate([beside_ref[p, scenario, :, :].reshape(TILE, -1) for p in range(8)], axis=0)
-    part = dot_parts(along, beside, 1, 1)
-    quarter = 4 * TILE
-    for c in range(2):
-        first = part[2 * c * quarter:(2 * c + 1) * quarter]
-        second = part[(2 * c + 1) * quarter:(2 * c + 2) * quarter]
-        packed = jnp.concatenate([first, second], axis=1)
-        for y in range(8):
-            out_ref[2 * y + c] = packed
-
-
-def block_part(core, along, beside):
+    part_ref[...] = dot_parts(along, beside, 1, 1)
+    z = lax.axis_index("z")
+    rows = [part_ref[pl.ds(pl.multiple_of(lax.rem(z + d, 8) * 16, 16), 16), :] for d in range(5)]
+    packed = [
+        jnp.concatenate(
+            [
+                jnp.concatenate([rows[3 * c], rows[3 * c + 1]], axis=1),
+                jnp.concatenate([rows[2][TILE * c:TILE * (c + 1)]] * 2, axis=1),
+            ],
+            axis=0,
+        )
+        for c in range(2)
+    ]
+    for y in range(8):
+        for c in range(2):
+            out_ref[2 * y + c] = packed[c]
+
+
+def block_part(along, beside):
     vmem = pl.BlockSpec(memory_space=pltpu.VMEM)
     return pl.pallas_call(
         block_kernel,
-        out_shape=jax.ShapeDtypeStruct((16, 4 * TILE, 16 * TILE), jnp.float32),
-        in_specs=[pl.BlockSpec(memory_space=pltpu.SMEM), vmem, vmem],
+        out_shape=jax.ShapeDtypeStruct((16, 3 * TILE, 16 * TILE), jnp.float32),
+        in_specs=[vmem, vmem],
         out_specs=vmem,
+        scratch_shapes=[pltpu.VMEM((16 * TILE, 8 * TILE), jnp.float32)],
         compiler_params=pltpu.CompilerParams(vmem_limit_bytes=16 << 20),
         name="block_part",
-    )(core, along, beside)
+    )(along, beside)
 
 
 def product_kernel(columns_ref, *refs):
@@ -334,7 +354,7 @@
     behind = lax.ppermute(shard, "x", AHEAD)
     ahead = lax.ppermute(shard, "x", BEHIND)
 
-    piece = block_part(place, along, beside)
+    piece = block_part(along, beside)
     parts = exchange(piece, ("scen", "core"))
     _, passed_on = lax.optimization_barrier((piece, jnp.where(core == 0, behind, ahead)))
     onward = lax.ppermute(passed_on, ("x", "core"), ONWARD)

time: 124 us -> 120 us (0.968)
  waiting for transfers between devices: 22.9 us -> 20.3 us
  Pallas kernels: 29.4 us -> 28.1 us
    all_to_all x4, waiting for transfers between devices: 12.5 us -> 9.85 us  [exchange(): return lax.all_to_all(array, axes, split_axis=0, concat_axis=0, tiled=True)]
  transfers between devices with their start and end apart: 10 -> 10, of which waited for: 8 -> 6; matrix products, arithmetic and copies ran while one was open for 3% -> 4% of each run, Pallas kernels for 21% -> 20%
where the time goes in v9:
time: 120 us
  starting transfers between devices  51.7 us (43%)
  Pallas kernels  28.1 us (23%)
  waiting for transfers between devices  20.3 us (17%)
  blocking collectives  13.7 us (11%)
  local copies, waits for them, and re-layouts  2.29 us (2%)
  other arithmetic  1.98 us (2%)
  matrix products  1.34 us (1%)
    all_to_all x4, starting transfers between devices, exchange(): return lax.all_to_all(array, axes, split_axis=0, concat_axis=0, tiled=True)  30.1 us
    pallas_call x1, Pallas kernels, inverse_factor(): pl.pallas_call(inverse_kernel, out_shape=jax.ShapeDtypeStruct(shape, jnp....  16.6 us
    all_gather x1, blocking collectives, body(): beside = lax.all_gather(to_beside, ('x', 'core'), axis=0, tiled=False)  13.7 us
    all_to_all x4, waiting for transfers between devices, exchange(): return lax.all_to_all(array, axes, split_axis=0, concat_axis=0, tiled=True)  9.85 us
    ppermute x1, waiting for transfers between devices, body(): behind = lax.ppermute(shard, 'x', AHEAD)  6.29 us
    pallas_call x4, Pallas kernels, product(): pl.pallas_call(further_kernel if done else product_kernel, out_shape=jax....  6.27 us
    ppermute x1, starting transfers between devices, body(): other_half = lax.ppermute(own_half, 'core', SWAP)  5.2 us
    ppermute x1, starting transfers between devices, body(): schur_part = schur_mine + lax.ppermute(schur_other, 'core', SWAP)  4.47 us
  transfers between devices with their start and end apart: 10, of which 6 were waited for; matrix products, arithmetic and copies ran while one was open for 4% of the time, Pallas kernels for 20%

profile of v9, /device:TPU:1, one launch (start us, length us, event | category | flops | bytes accessed | tf_op | source)
XLA Modules:
  0.0 119.6 jit_solution(403063531359401784)
XLA Ops:
  0.0 4.1 %prepare.1 = (f32[16,8,1536]{2,1,0:T(8,128)}, f32[2,8,1536]{2,1,0:T(8,128)}, f32[1536,256]{1,0:T(8,128)}) custom-call(s32[2]{0:T(128)} %counts_ref.1, f32[2,1536]{1,0:T(2,128)} %barrier_ref.1, f32[2,1536,256]{2,1,0:T(8,128)} %border_ref.1), custom_call_target="tpu_custom_call" | custom-call | tf_op jit(solution)/shard_map/prepare/pallas_call | solution.py:248
  4.1 0.0 copy-start
  4.1 12.0 %all-to-all-start = ((f32[16,8,1536]{2,1,0:T(8,128)}), f32[16,8,1536]{2,1,0:T(8,128)S(1)}, u32[]{:S(2)}, u32[]{:S(2)}) async-start(f32[16,8,1536]{2,1,0:T(8,128)} %get-tuple-element.17), calls=%async_computation | async-start | bytes 1572864 | tf_op jit(solution)/shard_map/all_to_all | solution.py:337
  16.0 0.0 copy-done
  16.1 13.7 %all-gather = f32[16,8,1536]{2,1,0:T(8,128)S(1)} all-gather(f32[2,8,1536]{2,1,0:T(8,128)S(1)} %copy-done), channel_id=2, replica_groups=mesh['scen'=8,'z'=8,'x'=4,'core'=2] {'x','core'}, dimensions={0}, use_global_device_ids=true | all-gather | bytes 884736 | tf_op jit(solution)/shard_map/all_gather | solution.py:350
  29.7 9.0 %all-to-all-done.along_ref = f32[16,8,1536]{2,1,0:T(8,128)S(1)} async-done(((f32[16,8,1536]{2,1,0:T(8,128)}), f32[16,8,1536]{2,1,0:T(8,128)S(1)}, u32[]{:S(2)}, u32[]{:S(2)}) %all-to-all-start) | async-done | bytes 786464 | tf_op jit(solution)/shard_map/all_to_all | solution.py:337
  38.7 3.1 %collective-permute-start = (f32[128,1536]{1,0:T(8,128)S(1)}, f32[128,1536]{1,0:T(8,128)S(1)}, u32[]{:S(2)}, u32[]{:S(2)}) collective-permute-start(f32[128,1536]{1,0:T(8,128)S(1)} %bitcast.11), channel_id=1, source_target_pairs={{0,2},{2,4},{4,6},{6,0},{1,3},{3,5},{5,7},{7,1},{8,10},{10,12},{12... | collective-permute-start | bytes 2359304 | tf_op jit(solution)/shard_map/ppermute | solution.py:354
  41.8 3.4 %collective-permute-start.1 = (f32[128,1536]{1,0:T(8,128)S(1)}, f32[128,1536]{1,0:T(8,128)S(1)}, u32[]{:S(2)}, u32[]{:S(2)}) collective-permute-start(f32[128,1536]{1,0:T(8,128)S(1)} %bitcast.12), channel_id=1, source_target_pairs={{0,6},{2,0},{4,2},{6,4},{1,7},{3,1},{5,3},{7,5},{8,14},{10,8},{12,... | collective-permute-start | bytes 2359304 | tf_op jit(solution)/shard_map/ppermute | solution.py:355
  45.2 1.2 %block_part.1 = f32[16,24,128]{2,1,0:T(8,128)} custom-call(f32[16,8,1536]{2,1,0:T(8,128)S(1)} %all-to-all-done.along_ref, f32[8,2,8,1536]{3,2,1,0:T(8,128)S(1)} %bitcast.15), custom_call_target="tpu_custom_call" | custom-call | tf_op jit(solution)/shard_map/block_part/pallas_call | solution.py:291
  46.4 7.2 %all-to-all-start.1 = ((f32[16,24,128]{2,1,0:T(8,128)}), f32[16,24,128]{2,1,0:T(8,128)S(1)}, u32[]{:S(2)}, u32[]{:S(2)}) async-start(f32[16,24,128]{2,1,0:T(8,128)} %block_part.1), calls=%async_computation.1 | async-start | bytes 393216 | tf_op jit(solution)/shard_map/all_to_all | solution.py:337
  53.7 6.3 %collective-permute-done.refs_1_ = f32[128,1536]{1,0:T(8,128)S(1)} collective-permute-done((f32[128,1536]{1,0:T(8,128)S(1)}, f32[128,1536]{1,0:T(8,128)S(1)}, u32[]{:S(2)}, u32[]{:S(2)}) %collective-permute-start) | collective-permute-done | bytes 786464 | tf_op jit(solution)/shard_map/ppermute | solution.py:354
  59.9 2.2 %collective-permute-done.1.refs_2_ = f32[128,1536]{1,0:T(8,128)S(1)} collective-permute-done((f32[128,1536]{1,0:T(8,128)S(1)}, f32[128,1536]{1,0:T(8,128)S(1)}, u32[]{:S(2)}, u32[]{:S(2)}) %collective-permute-start.1) | collective-permute-done | bytes 786464 | tf_op jit(solution)/shard_map/ppermute | solution.py:355
  62.1 1.0 broadcast_select_fusion
  63.1 0.9 all-to-all-done.1
  64.0 1.9 %collective-permute-start.3 = (f32[1536,256]{1,0:T(8,128)}, f32[1536,256]{1,0:T(8,128)}, u32[]{:S(2)}, u32[]{:S(2)}) collective-permute-start(f32[1536,256]{1,0:T(8,128)} %get-tuple-element.24), channel_id=1, source_target_pairs={{0,1},{1,0},{2,3},{3,2},{4,5},{5,4},{6,7},{7,6},{8,9},{9,8},{10,11... | collective-permute-start | bytes 4718600 | tf_op jit(solution)/shard_map/ppermute | solution.py:369
  65.9 3.5 %collective-permute-start.2 = (f32[128,1536]{1,0:T(8,128)}, f32[128,1536]{1,0:T(8,128)S(1)}, u32[]{:S(2)}, u32[]{:S(2)}) collective-permute-start(f32[128,1536]{1,0:T(8,128)} %broadcast_select_fusion), channel_id=1, source_target_pairs={{0,2},{1,7},{2,4},{3,1},{4,6},{5,3},{6,0},{7,5},{8,10},{9,15},{10,... | collective-permute-start | bytes 2359304 | tf_op jit(solution)/shard_map/ppermute | solution.py:360
  69.4 0.8 broadcast_in_dim.3
  70.2 4.7 %all-to-all-start.3 = ((f32[32,24,128]{2,1,0:T(8,128)}), f32[32,24,128]{2,1,0:T(8,128)S(1)}, u32[]{:S(2)}, u32[]{:S(2)}) async-start(f32[32,24,128]{2,1,0:T(8,128)} %broadcast_in_dim.3), calls=%async_computation.3 | async-start | bytes 786432 | tf_op jit(solution)/shard_map/all_to_all | solution.py:337
  74.9 1.5 %dynamic-slice_bitcast_fusion.columns_ref = f32[1536,256]{1,0:T(8,128)S(1)} fusion(f32[2,1536,256]{2,1,0:T(8,128)} %border_ref.1, s32[]{:T(128)S(6)} %select_n.12), kind=kLoop, calls=%fused_computation | loop fusion | bytes 3145732 | tf_op jit(solution)/shard_map/jit(dynamic_index_in_dim)/squeeze | solution.py:370
  76.4 1.2 product.3.before_ref
  77.6 0.0 collective-permute-done.3.columns_ref
  77.6 2.6 %product.2.before_ref = f32[256,384]{1,0:T(8,128)S(1)} custom-call(f32[1536,256]{1,0:T(8,128)} %collective-permute-done.3.columns_ref, f32[128,1536]{1,0:T(8,128)S(1)} %bitcast.14, f32[128,1536]{1,0:T(8,128)S(1)} %collective-permute-done.refs_1_, f32[128,1536]{1,0:T(8,128)S(1)} %collective-permute-done.1.refs_2_), custom_call_target="tpu_custom_call" | custom-call | flops 905969664 | bytes 3932160 | tf_op jit(solution)/shard_map/product/pallas_call | solution.py:323
  80.1 0.0 collective-permute-done.2.panel_ref
  80.2 2.0 %further.3 = f32[256,512]{1,0:T(8,128)S(1)} custom-call(f32[1536,256]{1,0:T(8,128)} %collective-permute-done.3.columns_ref, f32[128,1536]{1,0:T(8,128)S(1)} %collective-permute-done.2.panel_ref, f32[256,384]{1,0:T(8,128)S(1)} %product.2.before_ref), custom_call_target="tpu_custom_call" | custom-call | flops 301989888 | bytes 2359296 | tf_op jit(solution)/shard_map/further/pallas_call | solution.py:323
  82.1 4.5 %collective-permute-start.4 = (f32[256,512]{1,0:T(8,128)S(1)}, f32[256,512]{1,0:T(8,128)S(1)}, u32[]{:S(2)}, u32[]{:S(2)}) collective-permute-start(f32[256,512]{1,0:T(8,128)S(1)} %further.3), channel_id=1, source_target_pairs={{0,1},{1,0},{2,3},{3,2},{4,5},{5,4},{6,7},{7,6},{8,9},{9,8},{10,11... | collective-permute-start | bytes 1572872 | tf_op jit(solution)/shard_map/ppermute | solution.py:376
  86.6 0.6 further.2
  87.2 0.9 collective-permute-done.4
  88.1 0.9 add.8
  89.0 0.0 all-to-all-done.3.own_ref
  89.0 6.3 %all-to-all-start.2 = ((f32[8,32,512]{2,1,0:T(8,128)}), f32[8,32,512]{2,1,0:T(8,128)S(1)}, u32[]{:S(2)}, u32[]{:S(2)}) async-start(f32[8,32,512]{2,1,0:T(8,128)} %bitcast.3), calls=%async_computation.2 | async-start | bytes 1048576 | tf_op jit(solution)/shard_map/all_to_all | solution.py:337
  95.3 5.2 %collective-permute-start.5 = (f32[32,24,128]{2,1,0:T(8,128)S(1)}, f32[32,24,128]{2,1,0:T(8,128)S(1)}, u32[]{:S(2)}, u32[]{:S(2)}) collective-permute-start(f32[32,24,128]{2,1,0:T(8,128)S(1)} %all-to-all-done.3.own_ref), channel_id=1, source_target_pairs={{0,1},{1,0},{2,3},{3,2},{4,5},{5,4},{6,7},{7,6},{8,9},{9,8},{10,11... | collective-permute-start | bytes 1179656 | tf_op jit(solution)/shard_map/ppermute | solution.py:366
  100.5 0.1 pad_add_fusion.place_ref
  100.6 1.1 collective-permute-done.5.other_ref
  101.6 16.6 %inverse_factor.1 = f32[512,512]{1,0:T(8,128)S(1)} custom-call(s32[2]{0:T(128)S(1)} %pad_add_fusion.place_ref, f32[32,24,128]{2,1,0:T(8,128)S(1)} %all-to-all-done.3.own_ref, f32[32,24,128]{2,1,0:T(8,128)S(1)} %collective-permute-done.5.other_ref), custom_call_target="tpu_custom_call" | custom-call | flops 536870912 | bytes 2097152 | tf_op jit(solution)/shard_map/inverse_factor/pallas_call | solution.py:211
  118.2 0.0 all-to-all-done.2
  118.3 1.3 %convolution_bitcast_fusion = f32[1,1,32,512]{3,2,1,0:T(8,128)} fusion(f32[32,512]{1,0:T(8,128)S(1)} %reduce_sum.19, f32[512,512]{1,0:T(8,128)S(1)} %inverse_factor.1), kind=kOutput, calls=%fused_computation.1 | convolution fusion | flops 100663296 | bytes 1179648 | tf_op jit(solution)/shard_map/dot_general | solution.py:20
  (2 shorter events, 0.1 us)
Async XLA Ops:
  4.1 12.0 %copy-start = (f32[2,8,1536]{2,1,0:T(8,128)S(1)}, f32[2,8,1536]{2,1,0:T(8,128)}, u32[]{:S(2)}) copy-start(f32[2,8,1536]{2,1,0:T(8,128)} %get-tuple-element.18) | copy-start | bytes 294916
  4.1 34.6 %all-to-all-start = ((f32[16,8,1536]{2,1,0:T(8,128)}), f32[16,8,1536]{2,1,0:T(8,128)S(1)}, u32[]{:S(2)}, u32[]{:S(2)}) async-start(f32[16,8,1536]{2,1,0:T(8,128)} %get-tuple-element.17), calls=%async_computation | async-start | bytes 1572864 | tf_op jit(solution)/shard_map/all_to_all | solution.py:337
  38.7 21.2 %collective-permute-start = (f32[128,1536]{1,0:T(8,128)S(1)}, f32[128,1536]{1,0:T(8,128)S(1)}, u32[]{:S(2)}, u32[]{:S(2)}) collective-permute-start(f32[128,1536]{1,0:T(8,128)S(1)} %bitcast.11), channel_id=1, source_target_pairs={{0,2},{2,4},{4,6},{6,0},{1,3},{3,5},{5,7},{7,1},{8,10},{10,12},{12... | collective-permute-start | bytes 2359304 | tf_op jit(solution)/shard_map/ppermute | solution.py:354
  41.8 20.3 %collective-permute-start.1 = (f32[128,1536]{1,0:T(8,128)S(1)}, f32[128,1536]{1,0:T(8,128)S(1)}, u32[]{:S(2)}, u32[]{:S(2)}) collective-permute-start(f32[128,1536]{1,0:T(8,128)S(1)} %bitcast.12), channel_id=1, source_target_pairs={{0,6},{2,0},{4,2},{6,4},{1,7},{3,1},{5,3},{7,5},{8,14},{10,8},{12,... | collective-permute-start | bytes 2359304 | tf_op jit(solution)/shard_map/ppermute | solution.py:355
  46.4 17.6 %all-to-all-start.1 = ((f32[16,24,128]{2,1,0:T(8,128)}), f32[16,24,128]{2,1,0:T(8,128)S(1)}, u32[]{:S(2)}, u32[]{:S(2)}) async-start(f32[16,24,128]{2,1,0:T(8,128)} %block_part.1), calls=%async_computation.1 | async-start | bytes 393216 | tf_op jit(solution)/shard_map/all_to_all | solution.py:337
  64.0 13.6 %collective-permute-start.3 = (f32[1536,256]{1,0:T(8,128)}, f32[1536,256]{1,0:T(8,128)}, u32[]{:S(2)}, u32[]{:S(2)}) collective-permute-start(f32[1536,256]{1,0:T(8,128)} %get-tuple-element.24), channel_id=1, source_target_pairs={{0,1},{1,0},{2,3},{3,2},{4,5},{5,4},{6,7},{7,6},{8,9},{9,8},{10,11... | collective-permute-start | bytes 4718600 | tf_op jit(solution)/shard_map/ppermute | solution.py:369
  65.9 14.2 %collective-permute-start.2 = (f32[128,1536]{1,0:T(8,128)}, f32[128,1536]{1,0:T(8,128)S(1)}, u32[]{:S(2)}, u32[]{:S(2)}) collective-permute-start(f32[128,1536]{1,0:T(8,128)} %broadcast_select_fusion), channel_id=1, source_target_pairs={{0,2},{1,7},{2,4},{3,1},{4,6},{5,3},{6,0},{7,5},{8,10},{9,15},{10,... | collective-permute-start | bytes 2359304 | tf_op jit(solution)/shard_map/ppermute | solution.py:360
  70.2 18.8 %all-to-all-start.3 = ((f32[32,24,128]{2,1,0:T(8,128)}), f32[32,24,128]{2,1,0:T(8,128)S(1)}, u32[]{:S(2)}, u32[]{:S(2)}) async-start(f32[32,24,128]{2,1,0:T(8,128)} %broadcast_in_dim.3), calls=%async_computation.3 | async-start | bytes 786432 | tf_op jit(solution)/shard_map/all_to_all | solution.py:337
  82.1 6.0 %collective-permute-start.4 = (f32[256,512]{1,0:T(8,128)S(1)}, f32[256,512]{1,0:T(8,128)S(1)}, u32[]{:S(2)}, u32[]{:S(2)}) collective-permute-start(f32[256,512]{1,0:T(8,128)S(1)} %further.3), channel_id=1, source_target_pairs={{0,1},{1,0},{2,3},{3,2},{4,5},{5,4},{6,7},{7,6},{8,9},{9,8},{10,11... | collective-permute-start | bytes 1572872 | tf_op jit(solution)/shard_map/ppermute | solution.py:376
  89.0 29.2 %all-to-all-start.2 = ((f32[8,32,512]{2,1,0:T(8,128)}), f32[8,32,512]{2,1,0:T(8,128)S(1)}, u32[]{:S(2)}, u32[]{:S(2)}) async-start(f32[8,32,512]{2,1,0:T(8,128)} %bitcast.3), calls=%async_computation.2 | async-start | bytes 1048576 | tf_op jit(solution)/shard_map/all_to_all | solution.py:337
  95.3 6.4 %collective-permute-start.5 = (f32[32,24,128]{2,1,0:T(8,128)S(1)}, f32[32,24,128]{2,1,0:T(8,128)S(1)}, u32[]{:S(2)}, u32[]{:S(2)}) collective-permute-start(f32[32,24,128]{2,1,0:T(8,128)S(1)} %all-to-all-done.3.own_ref), channel_id=1, source_target_pairs={{0,1},{1,0},{2,3},{3,2},{4,5},{5,4},{6,7},{7,6},{8,9},{9,8},{10,11... | collective-permute-start | bytes 1179656 | tf_op jit(solution)/shard_map/ppermute | solution.py:366

commit v10 on v9

--- a/solution.py
+++ b/solution.py
@@ -348,6 +348,8 @@
     to_along, to_beside, to_other = prepare(row_counts, barrier, border)
     along = exchange(to_along, ("z", "core"))
     beside = lax.all_gather(to_beside, ("x", "core"), axis=0, tiled=False)
+    beside, to_other = lax.optimization_barrier((beside, to_other))
+    other = lax.ppermute(to_other, "core", SWAP)
     along, beside = lax.optimization_barrier((along, beside))
 
     shard = along.reshape(16 * TILE, capacity)
@@ -360,13 +362,11 @@
     onward = lax.ppermute(passed_on, ("x", "core"), ONWARD)
     parts, _ = lax.optimization_barrier((parts, passed_on))
     summed = jnp.sum(parts, axis=0)
-    summed, to_other = lax.optimization_barrier((summed, to_other))
     copies = jnp.broadcast_to(summed, (32,) + summed.shape)
     own_half = exchange(copies, ("z", "x"))
     other_half = lax.ppermute(own_half, "core", SWAP)
     inverse = inverse_factor(place, own_half, other_half)
 
-    other = lax.ppermute(to_other, "core", SWAP)
     mine = lax.dynamic_index_in_dim(border, core, 0, keepdims=False)
     schur_other = product(other, (shard, behind, ahead))
     schur_mine = product(mine, (shard, behind, ahead))

time: 120 us -> 117 us (0.975)
  waiting for transfers between devices: 20.3 us -> 18.6 us
  starting transfers between devices: 51.7 us -> 50.4 us
    ppermute x1, waiting for transfers between devices: 6.29 us -> 3.68 us  [body(): behind = lax.ppermute(shard, 'x', AHEAD)]
    ppermute x1, starting transfers between devices: 4.47 us -> 2.51 us  [body(): schur_part = schur_mine + lax.ppermute(schur_other, 'core', SWAP)]
    ppermute x1, waiting for transfers between devices: 0.01 us -> 1.4 us  [body(): onward = lax.ppermute(passed_on, ('x', 'core'), ONWARD)]
  transfers between devices with their start and end apart: 10 -> 10, of which waited for: 6 -> 6; matrix products, arithmetic and copies ran while one was open for 4% -> 4% of each run, Pallas kernels for 20% -> 21%
where the time goes in v10:
time: 117 us
  starting transfers between devices  50.4 us (43%)
  Pallas kernels  28.1 us (24%)
  waiting for transfers between devices  18.6 us (16%)
  blocking collectives  13.7 us (12%)
  local copies, waits for them, and re-layouts  2.29 us (2%)
  other arithmetic  1.98 us (2%)
  matrix products  1.34 us (1%)
    all_to_all x4, starting transfers between devices, exchange(): return lax.all_to_all(array, axes, split_axis=0, concat_axis=0, tiled=True)  30.3 us
    pallas_call x1, Pallas kernels, inverse_factor(): pl.pallas_call(inverse_kernel, out_shape=jax.ShapeDtypeStruct(shape, jnp....  16.6 us
    all_gather x1, blocking collectives, body(): beside = lax.all_gather(to_beside, ('x', 'core'), axis=0, tiled=False)  13.7 us
    all_to_all x4, waiting for transfers between devices, exchange(): return lax.all_to_all(array, axes, split_axis=0, concat_axis=0, tiled=True)  8.99 us
    pallas_call x4, Pallas kernels, product(): pl.pallas_call(further_kernel if done else product_kernel, out_shape=jax....  6.28 us
    ppermute x1, starting transfers between devices, body(): other_half = lax.ppermute(own_half, 'core', SWAP)  4.6 us
    ppermute x1, starting transfers between devices, body(): onward = lax.ppermute(passed_on, ('x', 'core'), ONWARD)  4.57 us
    pallas_call x1, Pallas kernels, prepare(): pl.pallas_call(prepare_kernel, out_shape=(jax.ShapeDtypeStruct((16, TILE,...  4.05 us
  transfers between devices with their start and end apart: 10, of which 6 were waited for; matrix products, arithmetic and copies ran while one was open for 4% of the time, Pallas kernels for 21%

profile of v10, /device:TPU:1, one launch (start us, length us, event | category | flops | bytes accessed | tf_op | source)
XLA Modules:
  0.0 116.5 jit_solution(6924267043030211780)
XLA Ops:
  0.0 4.1 %prepare.1 = (f32[16,8,1536]{2,1,0:T(8,128)}, f32[2,8,1536]{2,1,0:T(8,128)}, f32[1536,256]{1,0:T(8,128)}) custom-call(s32[2]{0:T(128)} %counts_ref.1, f32[2,1536]{1,0:T(2,128)} %barrier_ref.1, f32[2,1536,256]{2,1,0:T(8,128)} %border_ref.1), custom_call_target="tpu_custom_call" | custom-call | tf_op jit(solution)/shard_map/prepare/pallas_call | solution.py:248
  4.1 0.0 copy-start
  4.1 12.0 %all-to-all-start = ((f32[16,8,1536]{2,1,0:T(8,128)}), f32[16,8,1536]{2,1,0:T(8,128)S(1)}, u32[]{:S(2)}, u32[]{:S(2)}) async-start(f32[16,8,1536]{2,1,0:T(8,128)} %get-tuple-element.17), calls=%async_computation | async-start | bytes 1572864 | tf_op jit(solution)/shard_map/all_to_all | solution.py:337
  16.0 0.0 copy-done
  16.1 13.7 %all-gather = f32[16,8,1536]{2,1,0:T(8,128)S(1)} all-gather(f32[2,8,1536]{2,1,0:T(8,128)S(1)} %copy-done), channel_id=2, replica_groups=mesh['scen'=8,'z'=8,'x'=4,'core'=2] {'x','core'}, dimensions={0}, use_global_device_ids=true | all-gather | bytes 884736 | tf_op jit(solution)/shard_map/all_gather | solution.py:350
  29.7 9.0 %all-to-all-done.along_ref = f32[16,8,1536]{2,1,0:T(8,128)S(1)} async-done(((f32[16,8,1536]{2,1,0:T(8,128)}), f32[16,8,1536]{2,1,0:T(8,128)S(1)}, u32[]{:S(2)}, u32[]{:S(2)}) %all-to-all-start) | async-done | bytes 786464 | tf_op jit(solution)/shard_map/all_to_all | solution.py:337
  38.7 3.1 %collective-permute-start = (f32[128,1536]{1,0:T(8,128)S(1)}, f32[128,1536]{1,0:T(8,128)S(1)}, u32[]{:S(2)}, u32[]{:S(2)}) collective-permute-start(f32[128,1536]{1,0:T(8,128)S(1)} %bitcast.11), channel_id=1, source_target_pairs={{0,2},{2,4},{4,6},{6,0},{1,3},{3,5},{5,7},{7,1},{8,10},{10,12},{12... | collective-permute-start | bytes 2359304 | tf_op jit(solution)/shard_map/ppermute | solution.py:356
  41.8 3.4 %collective-permute-start.1 = (f32[128,1536]{1,0:T(8,128)S(1)}, f32[128,1536]{1,0:T(8,128)S(1)}, u32[]{:S(2)}, u32[]{:S(2)}) collective-permute-start(f32[128,1536]{1,0:T(8,128)S(1)} %bitcast.12), channel_id=1, source_target_pairs={{0,6},{2,0},{4,2},{6,4},{1,7},{3,1},{5,3},{7,5},{8,14},{10,8},{12,... | collective-permute-start | bytes 2359304 | tf_op jit(solution)/shard_map/ppermute | solution.py:357
  45.2 1.9 %collective-permute-start.3 = (f32[1536,256]{1,0:T(8,128)}, f32[1536,256]{1,0:T(8,128)}, u32[]{:S(2)}, u32[]{:S(2)}) collective-permute-start(f32[1536,256]{1,0:T(8,128)} %get-tuple-element.24), channel_id=1, source_target_pairs={{0,1},{1,0},{2,3},{3,2},{4,5},{5,4},{6,7},{7,6},{8,9},{9,8},{10,11... | collective-permute-start | bytes 4718600 | tf_op jit(solution)/shard_map/ppermute | solution.py:352
  47.1 1.2 %block_part.1 = f32[16,24,128]{2,1,0:T(8,128)} custom-call(f32[16,8,1536]{2,1,0:T(8,128)S(1)} %all-to-all-done.along_ref, f32[8,2,8,1536]{3,2,1,0:T(8,128)S(1)} %bitcast.15), custom_call_target="tpu_custom_call" | custom-call | tf_op jit(solution)/shard_map/block_part/pallas_call | solution.py:291
  48.4 7.6 %all-to-all-start.2 = ((f32[16,24,128]{2,1,0:T(8,128)}), f32[16,24,128]{2,1,0:T(8,128)S(1)}, u32[]{:S(2)}, u32[]{:S(2)}) async-start(f32[16,24,128]{2,1,0:T(8,128)} %block_part.1), calls=%async_computation.2 | async-start | bytes 393216 | tf_op jit(solution)/shard_map/all_to_all | solution.py:337
  56.0 3.7 %collective-permute-done.refs_1_ = f32[128,1536]{1,0:T(8,128)S(1)} collective-permute-done((f32[128,1536]{1,0:T(8,128)S(1)}, f32[128,1536]{1,0:T(8,128)S(1)}, u32[]{:S(2)}, u32[]{:S(2)}) %collective-permute-start) | collective-permute-done | bytes 786464 | tf_op jit(solution)/shard_map/ppermute | solution.py:356
  59.7 2.5 %collective-permute-done.1.refs_2_ = f32[128,1536]{1,0:T(8,128)S(1)} collective-permute-done((f32[128,1536]{1,0:T(8,128)S(1)}, f32[128,1536]{1,0:T(8,128)S(1)}, u32[]{:S(2)}, u32[]{:S(2)}) %collective-permute-start.1) | collective-permute-done | bytes 786464 | tf_op jit(solution)/shard_map/ppermute | solution.py:357
  62.1 1.0 broadcast_select_fusion
  63.1 4.6 %collective-permute-start.2 = (f32[128,1536]{1,0:T(8,128)}, f32[128,1536]{1,0:T(8,128)S(1)}, u32[]{:S(2)}, u32[]{:S(2)}) collective-permute-start(f32[128,1536]{1,0:T(8,128)} %broadcast_select_fusion), channel_id=1, source_target_pairs={{0,2},{1,7},{2,4},{3,1},{4,6},{5,3},{6,0},{7,5},{8,10},{9,15},{10,... | collective-permute-start | bytes 2359304 | tf_op jit(solution)/shard_map/ppermute | solution.py:362
  67.7 0.0 all-to-all-done.2
  67.7 0.8 broadcast_in_dim.3
  68.5 3.9 %all-to-all-start.3 = ((f32[32,24,128]{2,1,0:T(8,128)}), f32[32,24,128]{2,1,0:T(8,128)S(1)}, u32[]{:S(2)}, u32[]{:S(2)}) async-start(f32[32,24,128]{2,1,0:T(8,128)} %broadcast_in_dim.3), calls=%async_computation.3 | async-start | bytes 786432 | tf_op jit(solution)/shard_map/all_to_all | solution.py:337
  72.4 1.5 %dynamic-slice_bitcast_fusion.columns_ref = f32[1536,256]{1,0:T(8,128)S(1)} fusion(f32[2,1536,256]{2,1,0:T(8,128)} %border_ref.1, s32[]{:T(128)S(6)} %select_n.12), kind=kLoop, calls=%fused_computation | loop fusion | bytes 3145732 | tf_op jit(solution)/shard_map/jit(dynamic_index_in_dim)/squeeze | solution.py:370
  73.9 0.0 collective-permute-done.3.columns_ref
  73.9 2.6 %product.2.before_ref = f32[256,384]{1,0:T(8,128)S(1)} custom-call(f32[1536,256]{1,0:T(8,128)} %collective-permute-done.3.columns_ref, f32[128,1536]{1,0:T(8,128)S(1)} %bitcast.13, f32[128,1536]{1,0:T(8,128)S(1)} %collective-permute-done.refs_1_, f32[128,1536]{1,0:T(8,128)S(1)} %collective-permute-done.1.refs_2_), custom_call_target="tpu_custom_call" | custom-call | flops 905969664 | bytes 3932160 | tf_op jit(solution)/shard_map/product/pallas_call | solution.py:323
  76.5 1.2 product.3.before_ref
  77.7 1.4 %collective-permute-done.2.panel_ref = f32[128,1536]{1,0:T(8,128)S(1)} collective-permute-done((f32[128,1536]{1,0:T(8,128)}, f32[128,1536]{1,0:T(8,128)S(1)}, u32[]{:S(2)}, u32[]{:S(2)}) %collective-permute-start.2) | collective-permute-done | bytes 786464 | tf_op jit(solution)/shard_map/ppermute | solution.py:362
  79.1 2.0 %further.3 = f32[256,512]{1,0:T(8,128)S(1)} custom-call(f32[1536,256]{1,0:T(8,128)} %collective-permute-done.3.columns_ref, f32[128,1536]{1,0:T(8,128)S(1)} %collective-permute-done.2.panel_ref, f32[256,384]{1,0:T(8,128)S(1)} %product.2.before_ref), custom_call_target="tpu_custom_call" | custom-call | flops 301989888 | bytes 2359296 | tf_op jit(solution)/shard_map/further/pallas_call | solution.py:323
  81.1 2.5 %collective-permute-start.4 = (f32[256,512]{1,0:T(8,128)S(1)}, f32[256,512]{1,0:T(8,128)S(1)}, u32[]{:S(2)}, u32[]{:S(2)}) collective-permute-start(f32[256,512]{1,0:T(8,128)S(1)} %further.3), channel_id=1, source_target_pairs={{0,1},{1,0},{2,3},{3,2},{4,5},{5,4},{6,7},{7,6},{8,9},{9,8},{10,11... | collective-permute-start | bytes 1572872 | tf_op jit(solution)/shard_map/ppermute | solution.py:376
  83.6 0.6 further.2
  84.2 0.9 collective-permute-done.4
  85.1 0.9 add.8
  86.0 0.0 all-to-all-done.3.own_ref
  86.0 6.8 %all-to-all-start.1 = ((f32[8,32,512]{2,1,0:T(8,128)}), f32[8,32,512]{2,1,0:T(8,128)S(1)}, u32[]{:S(2)}, u32[]{:S(2)}) async-start(f32[8,32,512]{2,1,0:T(8,128)} %bitcast.3), calls=%async_computation.1 | async-start | bytes 1048576 | tf_op jit(solution)/shard_map/all_to_all | solution.py:337
  92.8 4.6 %collective-permute-start.5 = (f32[32,24,128]{2,1,0:T(8,128)S(1)}, f32[32,24,128]{2,1,0:T(8,128)S(1)}, u32[]{:S(2)}, u32[]{:S(2)}) collective-permute-start(f32[32,24,128]{2,1,0:T(8,128)S(1)} %all-to-all-done.3.own_ref), channel_id=1, source_target_pairs={{0,1},{1,0},{2,3},{3,2},{4,5},{5,4},{6,7},{7,6},{8,9},{9,8},{10,11... | collective-permute-start | bytes 1179656 | tf_op jit(solution)/shard_map/ppermute | solution.py:367
  97.4 0.1 pad_add_fusion.place_ref
  97.5 1.1 collective-permute-done.5.other_ref
  98.5 16.6 %inverse_factor.1 = f32[512,512]{1,0:T(8,128)S(1)} custom-call(s32[2]{0:T(128)S(1)} %pad_add_fusion.place_ref, f32[32,24,128]{2,1,0:T(8,128)S(1)} %all-to-all-done.3.own_ref, f32[32,24,128]{2,1,0:T(8,128)S(1)} %collective-permute-done.5.other_ref), custom_call_target="tpu_custom_call" | custom-call | flops 536870912 | bytes 2097152 | tf_op jit(solution)/shard_map/inverse_factor/pallas_call | solution.py:211
  115.1 0.0 all-to-all-done.1
  115.2 1.3 %convolution_bitcast_fusion = f32[1,1,32,512]{3,2,1,0:T(8,128)} fusion(f32[32,512]{1,0:T(8,128)S(1)} %reduce_sum.18, f32[512,512]{1,0:T(8,128)S(1)} %inverse_factor.1), kind=kOutput, calls=%fused_computation.1 | convolution fusion | flops 100663296 | bytes 1179648 | tf_op jit(solution)/shard_map/dot_general | solution.py:20
  (2 shorter events, 0.1 us)
Async XLA Ops:
  4.1 12.0 %copy-start = (f32[2,8,1536]{2,1,0:T(8,128)S(1)}, f32[2,8,1536]{2,1,0:T(8,128)}, u32[]{:S(2)}) copy-start(f32[2,8,1536]{2,1,0:T(8,128)} %get-tuple-element.18) | copy-start | bytes 294916
  4.1 34.6 %all-to-all-start = ((f32[16,8,1536]{2,1,0:T(8,128)}), f32[16,8,1536]{2,1,0:T(8,128)S(1)}, u32[]{:S(2)}, u32[]{:S(2)}) async-start(f32[16,8,1536]{2,1,0:T(8,128)} %get-tuple-element.17), calls=%async_computation | async-start | bytes 1572864 | tf_op jit(solution)/shard_map/all_to_all | solution.py:337
  38.7 20.9 %collective-permute-start = (f32[128,1536]{1,0:T(8,128)S(1)}, f32[128,1536]{1,0:T(8,128)S(1)}, u32[]{:S(2)}, u32[]{:S(2)}) collective-permute-start(f32[128,1536]{1,0:T(8,128)S(1)} %bitcast.11), channel_id=1, source_target_pairs={{0,2},{2,4},{4,6},{6,0},{1,3},{3,5},{5,7},{7,1},{8,10},{10,12},{12... | collective-permute-start | bytes 2359304 | tf_op jit(solution)/shard_map/ppermute | solution.py:356
  41.8 20.3 %collective-permute-start.1 = (f32[128,1536]{1,0:T(8,128)S(1)}, f32[128,1536]{1,0:T(8,128)S(1)}, u32[]{:S(2)}, u32[]{:S(2)}) collective-permute-start(f32[128,1536]{1,0:T(8,128)S(1)} %bitcast.12), channel_id=1, source_target_pairs={{0,6},{2,0},{4,2},{6,4},{1,7},{3,1},{5,3},{7,5},{8,14},{10,8},{12,... | collective-permute-start | bytes 2359304 | tf_op jit(solution)/shard_map/ppermute | solution.py:357
  45.2 28.7 %collective-permute-start.3 = (f32[1536,256]{1,0:T(8,128)}, f32[1536,256]{1,0:T(8,128)}, u32[]{:S(2)}, u32[]{:S(2)}) collective-permute-start(f32[1536,256]{1,0:T(8,128)} %get-tuple-element.24), channel_id=1, source_target_pairs={{0,1},{1,0},{2,3},{3,2},{4,5},{5,4},{6,7},{7,6},{8,9},{9,8},{10,11... | collective-permute-start | bytes 4718600 | tf_op jit(solution)/shard_map/ppermute | solution.py:352
  48.4 19.3 %all-to-all-start.2 = ((f32[16,24,128]{2,1,0:T(8,128)}), f32[16,24,128]{2,1,0:T(8,128)S(1)}, u32[]{:S(2)}, u32[]{:S(2)}) async-start(f32[16,24,128]{2,1,0:T(8,128)} %block_part.1), calls=%async_computation.2 | async-start | bytes 393216 | tf_op jit(solution)/shard_map/all_to_all | solution.py:337
  63.1 15.9 %collective-permute-start.2 = (f32[128,1536]{1,0:T(8,128)}, f32[128,1536]{1,0:T(8,128)S(1)}, u32[]{:S(2)}, u32[]{:S(2)}) collective-permute-start(f32[128,1536]{1,0:T(8,128)} %broadcast_select_fusion), channel_id=1, source_target_pairs={{0,2},{1,7},{2,4},{3,1},{4,6},{5,3},{6,0},{7,5},{8,10},{9,15},{10,... | collective-permute-start | bytes 2359304 | tf_op jit(solution)/shard_map/ppermute | solution.py:362
  68.5 17.5 %all-to-all-start.3 = ((f32[32,24,128]{2,1,0:T(8,128)}), f32[32,24,128]{2,1,0:T(8,128)S(1)}, u32[]{:S(2)}, u32[]{:S(2)}) async-start(f32[32,24,128]{2,1,0:T(8,128)} %broadcast_in_dim.3), calls=%async_computation.3 | async-start | bytes 786432 | tf_op jit(solution)/shard_map/all_to_all | solution.py:337
  81.1 4.0 %collective-permute-start.4 = (f32[256,512]{1,0:T(8,128)S(1)}, f32[256,512]{1,0:T(8,128)S(1)}, u32[]{:S(2)}, u32[]{:S(2)}) collective-permute-start(f32[256,512]{1,0:T(8,128)S(1)} %further.3), channel_id=1, source_target_pairs={{0,1},{1,0},{2,3},{3,2},{4,5},{5,4},{6,7},{7,6},{8,9},{9,8},{10,11... | collective-permute-start | bytes 1572872 | tf_op jit(solution)/shard_map/ppermute | solution.py:376
  86.0 29.2 %all-to-all-start.1 = ((f32[8,32,512]{2,1,0:T(8,128)}), f32[8,32,512]{2,1,0:T(8,128)S(1)}, u32[]{:S(2)}, u32[]{:S(2)}) async-start(f32[8,32,512]{2,1,0:T(8,128)} %bitcast.3), calls=%async_computation.1 | async-start | bytes 1048576 | tf_op jit(solution)/shard_map/all_to_all | solution.py:337
  92.8 5.8 %collective-permute-start.5 = (f32[32,24,128]{2,1,0:T(8,128)S(1)}, f32[32,24,128]{2,1,0:T(8,128)S(1)}, u32[]{:S(2)}, u32[]{:S(2)}) collective-permute-start(f32[32,24,128]{2,1,0:T(8,128)S(1)} %all-to-all-done.3.own_ref), channel_id=1, source_target_pairs={{0,1},{1,0},{2,3},{3,2},{4,5},{5,4},{6,7},{7,6},{8,9},{9,8},{10,11... | collective-permute-start | bytes 1179656 | tf_op jit(solution)/shard_map/ppermute | solution.py:367

commit v11 on v10

--- a/solution.py
+++ b/solution.py
@@ -375,7 +375,7 @@
     schur_mine = product(mine, (onward,), schur_mine)
     schur_part = schur_mine + lax.ppermute(schur_other, "core", SWAP)
     owned = jnp.sum(exchange(schur_part.reshape(n_scen, rows_owned, PANEL), "scen"), axis=0)
-    solved = dot(owned, inverse, 1, 0)
+    solved = jnp.dot(owned, inverse, precision=lax.Precision.HIGH, preferred_element_type=jnp.float32)
     return solved.reshape(1, 1, rows_owned, PANEL)
 
 

time: 117 us -> 117 us (level)
  no operation moved by 1% of the time
where the time goes in v11:
time: 117 us; the launch traced here: 116 us
  starting transfers between devices  50.4 us (43%)
  Pallas kernels  28.1 us (24%)
  waiting for transfers between devices  18.6 us (16%)
  blocking collectives  13.7 us (12%)
  local copies, waits for them, and re-layouts  2.29 us (2%)
  other arithmetic  1.98 us (2%)
    all_to_all x4, starting transfers between devices, exchange(): return lax.all_to_all(array, axes, split_axis=0, concat_axis=0, tiled=True)  30.3 us
    pallas_call x1, Pallas kernels, inverse_factor(): pl.pallas_call(inverse_kernel, out_shape=jax.ShapeDtypeStruct(shape, jnp....  16.6 us
    all_gather x1, blocking collectives, body(): beside = lax.all_gather(to_beside, ('x', 'core'), axis=0, tiled=False)  13.7 us
    all_to_all x4, waiting for transfers between devices, exchange(): return lax.all_to_all(array, axes, split_axis=0, concat_axis=0, tiled=True)  8.99 us
    pallas_call x4, Pallas kernels, product(): pl.pallas_call(further_kernel if done else product_kernel, out_shape=jax....  6.28 us
    ppermute x1, starting transfers between devices, body(): other_half = lax.ppermute(own_half, 'core', SWAP)  4.6 us
    ppermute x1, starting transfers between devices, body(): onward = lax.ppermute(passed_on, ('x', 'core'), ONWARD)  4.57 us
    pallas_call x1, Pallas kernels, prepare(): pl.pallas_call(prepare_kernel, out_shape=(jax.ShapeDtypeStruct((16, TILE,...  4.05 us
  transfers between devices with their start and end apart: 10, of which 6 were waited for; matrix products, arithmetic and copies ran while one was open for 4% of the time, Pallas kernels for 21%

profile of v11, /device:TPU:1, one launch (start us, length us, event | category | flops | bytes accessed | tf_op | source)
XLA Modules:
  0.0 116.2 jit_solution(3118903463229090963)
XLA Ops:
  0.0 4.1 %prepare.1 = (f32[16,8,1536]{2,1,0:T(8,128)}, f32[2,8,1536]{2,1,0:T(8,128)}, f32[1536,256]{1,0:T(8,128)}) custom-call(s32[2]{0:T(128)} %counts_ref.1, f32[2,1536]{1,0:T(2,128)} %barrier_ref.1, f32[2,1536,256]{2,1,0:T(8,128)} %border_ref.1), custom_call_target="tpu_custom_call" | custom-call | tf_op jit(solution)/shard_map/prepare/pallas_call | solution.py:248
  4.1 0.0 copy-start
  4.1 12.0 %all-to-all-start = ((f32[16,8,1536]{2,1,0:T(8,128)}), f32[16,8,1536]{2,1,0:T(8,128)S(1)}, u32[]{:S(2)}, u32[]{:S(2)}) async-start(f32[16,8,1536]{2,1,0:T(8,128)} %get-tuple-element.17), calls=%async_computation | async-start | bytes 1572864 | tf_op jit(solution)/shard_map/all_to_all | solution.py:337
  16.0 0.0 copy-done
  16.1 13.7 %all-gather = f32[16,8,1536]{2,1,0:T(8,128)S(1)} all-gather(f32[2,8,1536]{2,1,0:T(8,128)S(1)} %copy-done), channel_id=2, replica_groups=mesh['scen'=8,'z'=8,'x'=4,'core'=2] {'x','core'}, dimensions={0}, use_global_device_ids=true | all-gather | bytes 884736 | tf_op jit(solution)/shard_map/all_gather | solution.py:350
  29.7 9.0 %all-to-all-done.along_ref = f32[16,8,1536]{2,1,0:T(8,128)S(1)} async-done(((f32[16,8,1536]{2,1,0:T(8,128)}), f32[16,8,1536]{2,1,0:T(8,128)S(1)}, u32[]{:S(2)}, u32[]{:S(2)}) %all-to-all-start) | async-done | bytes 786464 | tf_op jit(solution)/shard_map/all_to_all | solution.py:337
  38.7 3.1 %collective-permute-start = (f32[128,1536]{1,0:T(8,128)S(1)}, f32[128,1536]{1,0:T(8,128)S(1)}, u32[]{:S(2)}, u32[]{:S(2)}) collective-permute-start(f32[128,1536]{1,0:T(8,128)S(1)} %bitcast.11), channel_id=1, source_target_pairs={{0,2},{2,4},{4,6},{6,0},{1,3},{3,5},{5,7},{7,1},{8,10},{10,12},{12... | collective-permute-start | bytes 2359304 | tf_op jit(solution)/shard_map/ppermute | solution.py:356
  41.8 3.4 %collective-permute-start.1 = (f32[128,1536]{1,0:T(8,128)S(1)}, f32[128,1536]{1,0:T(8,128)S(1)}, u32[]{:S(2)}, u32[]{:S(2)}) collective-permute-start(f32[128,1536]{1,0:T(8,128)S(1)} %bitcast.12), channel_id=1, source_target_pairs={{0,6},{2,0},{4,2},{6,4},{1,7},{3,1},{5,3},{7,5},{8,14},{10,8},{12,... | collective-permute-start | bytes 2359304 | tf_op jit(solution)/shard_map/ppermute | solution.py:357
  45.2 1.9 %collective-permute-start.3 = (f32[1536,256]{1,0:T(8,128)}, f32[1536,256]{1,0:T(8,128)}, u32[]{:S(2)}, u32[]{:S(2)}) collective-permute-start(f32[1536,256]{1,0:T(8,128)} %get-tuple-element.24), channel_id=1, source_target_pairs={{0,1},{1,0},{2,3},{3,2},{4,5},{5,4},{6,7},{7,6},{8,9},{9,8},{10,11... | collective-permute-start | bytes 4718600 | tf_op jit(solution)/shard_map/ppermute | solution.py:352
  47.1 1.2 %block_part.1 = f32[16,24,128]{2,1,0:T(8,128)} custom-call(f32[16,8,1536]{2,1,0:T(8,128)S(1)} %all-to-all-done.along_ref, f32[8,2,8,1536]{3,2,1,0:T(8,128)S(1)} %bitcast.15), custom_call_target="tpu_custom_call" | custom-call | tf_op jit(solution)/shard_map/block_part/pallas_call | solution.py:291
  48.4 7.6 %all-to-all-start.2 = ((f32[16,24,128]{2,1,0:T(8,128)}), f32[16,24,128]{2,1,0:T(8,128)S(1)}, u32[]{:S(2)}, u32[]{:S(2)}) async-start(f32[16,24,128]{2,1,0:T(8,128)} %block_part.1), calls=%async_computation.2 | async-start | bytes 393216 | tf_op jit(solution)/shard_map/all_to_all | solution.py:337
  56.0 3.7 %collective-permute-done.refs_1_ = f32[128,1536]{1,0:T(8,128)S(1)} collective-permute-done((f32[128,1536]{1,0:T(8,128)S(1)}, f32[128,1536]{1,0:T(8,128)S(1)}, u32[]{:S(2)}, u32[]{:S(2)}) %collective-permute-start) | collective-permute-done | bytes 786464 | tf_op jit(solution)/shard_map/ppermute | solution.py:356
  59.7 2.5 %collective-permute-done.1.refs_2_ = f32[128,1536]{1,0:T(8,128)S(1)} collective-permute-done((f32[128,1536]{1,0:T(8,128)S(1)}, f32[128,1536]{1,0:T(8,128)S(1)}, u32[]{:S(2)}, u32[]{:S(2)}) %collective-permute-start.1) | collective-permute-done | bytes 786464 | tf_op jit(solution)/shard_map/ppermute | solution.py:357
  62.1 1.0 broadcast_select_fusion
  63.1 4.6 %collective-permute-start.2 = (f32[128,1536]{1,0:T(8,128)}, f32[128,1536]{1,0:T(8,128)S(1)}, u32[]{:S(2)}, u32[]{:S(2)}) collective-permute-start(f32[128,1536]{1,0:T(8,128)} %broadcast_select_fusion), channel_id=1, source_target_pairs={{0,2},{1,7},{2,4},{3,1},{4,6},{5,3},{6,0},{7,5},{8,10},{9,15},{10,... | collective-permute-start | bytes 2359304 | tf_op jit(solution)/shard_map/ppermute | solution.py:362
  67.7 0.0 all-to-all-done.2
  67.7 0.8 broadcast_in_dim.3
  68.5 3.9 %all-to-all-start.3 = ((f32[32,24,128]{2,1,0:T(8,128)}), f32[32,24,128]{2,1,0:T(8,128)S(1)}, u32[]{:S(2)}, u32[]{:S(2)}) async-start(f32[32,24,128]{2,1,0:T(8,128)} %broadcast_in_dim.3), calls=%async_computation.3 | async-start | bytes 786432 | tf_op jit(solution)/shard_map/all_to_all | solution.py:337
  72.4 1.5 %dynamic-slice_bitcast_fusion.columns_ref = f32[1536,256]{1,0:T(8,128)S(1)} fusion(f32[2,1536,256]{2,1,0:T(8,128)} %border_ref.1, s32[]{:T(128)S(6)} %select_n.12), kind=kLoop, calls=%fused_computation | loop fusion | bytes 3145732 | tf_op jit(solution)/shard_map/jit(dynamic_index_in_dim)/squeeze | solution.py:370
  73.9 0.0 collective-permute-done.3.columns_ref
  73.9 2.6 %product.2.before_ref = f32[256,384]{1,0:T(8,128)S(1)} custom-call(f32[1536,256]{1,0:T(8,128)} %collective-permute-done.3.columns_ref, f32[128,1536]{1,0:T(8,128)S(1)} %bitcast.13, f32[128,1536]{1,0:T(8,128)S(1)} %collective-permute-done.refs_1_, f32[128,1536]{1,0:T(8,128)S(1)} %collective-permute-done.1.refs_2_), custom_call_target="tpu_custom_call" | custom-call | flops 905969664 | bytes 3932160 | tf_op jit(solution)/shard_map/product/pallas_call | solution.py:323
  76.5 1.2 product.3.before_ref
  77.7 1.4 %collective-permute-done.2.panel_ref = f32[128,1536]{1,0:T(8,128)S(1)} collective-permute-done((f32[128,1536]{1,0:T(8,128)}, f32[128,1536]{1,0:T(8,128)S(1)}, u32[]{:S(2)}, u32[]{:S(2)}) %collective-permute-start.2) | collective-permute-done | bytes 786464 | tf_op jit(solution)/shard_map/ppermute | solution.py:362
  79.1 2.0 %further.3 = f32[256,512]{1,0:T(8,128)S(1)} custom-call(f32[1536,256]{1,0:T(8,128)} %collective-permute-done.3.columns_ref, f32[128,1536]{1,0:T(8,128)S(1)} %collective-permute-done.2.panel_ref, f32[256,384]{1,0:T(8,128)S(1)} %product.2.before_ref), custom_call_target="tpu_custom_call" | custom-call | flops 301989888 | bytes 2359296 | tf_op jit(solution)/shard_map/further/pallas_call | solution.py:323
  81.1 2.5 %collective-permute-start.4 = (f32[256,512]{1,0:T(8,128)S(1)}, f32[256,512]{1,0:T(8,128)S(1)}, u32[]{:S(2)}, u32[]{:S(2)}) collective-permute-start(f32[256,512]{1,0:T(8,128)S(1)} %further.3), channel_id=1, source_target_pairs={{0,1},{1,0},{2,3},{3,2},{4,5},{5,4},{6,7},{7,6},{8,9},{9,8},{10,11... | collective-permute-start | bytes 1572872 | tf_op jit(solution)/shard_map/ppermute | solution.py:376
  83.6 0.6 further.2
  84.2 0.9 collective-permute-done.4
  85.1 0.9 add.8
  86.0 0.0 all-to-all-done.3.own_ref
  86.0 6.8 %all-to-all-start.1 = ((f32[8,32,512]{2,1,0:T(8,128)}), f32[8,32,512]{2,1,0:T(8,128)S(1)}, u32[]{:S(2)}, u32[]{:S(2)}) async-start(f32[8,32,512]{2,1,0:T(8,128)} %bitcast.3), calls=%async_computation.1 | async-start | bytes 1048576 | tf_op jit(solution)/shard_map/all_to_all | solution.py:337
  92.8 4.6 %collective-permute-start.5 = (f32[32,24,128]{2,1,0:T(8,128)S(1)}, f32[32,24,128]{2,1,0:T(8,128)S(1)}, u32[]{:S(2)}, u32[]{:S(2)}) collective-permute-start(f32[32,24,128]{2,1,0:T(8,128)S(1)} %all-to-all-done.3.own_ref), channel_id=1, source_target_pairs={{0,1},{1,0},{2,3},{3,2},{4,5},{5,4},{6,7},{7,6},{8,9},{9,8},{10,11... | collective-permute-start | bytes 1179656 | tf_op jit(solution)/shard_map/ppermute | solution.py:367
  97.4 0.1 pad_add_fusion.place_ref
  97.5 1.1 collective-permute-done.5.other_ref
  98.5 16.6 %inverse_factor.1 = f32[512,512]{1,0:T(8,128)S(1)} custom-call(s32[2]{0:T(128)S(1)} %pad_add_fusion.place_ref, f32[32,24,128]{2,1,0:T(8,128)S(1)} %all-to-all-done.3.own_ref, f32[32,24,128]{2,1,0:T(8,128)S(1)} %collective-permute-done.5.other_ref), custom_call_target="tpu_custom_call" | custom-call | flops 536870912 | bytes 2097152 | tf_op jit(solution)/shard_map/inverse_factor/pallas_call | solution.py:211
  115.1 0.0 all-to-all-done.1
  115.2 1.0 convolution_bitcast_fusion
  (2 shorter events, 0.1 us)
Async XLA Ops:
  4.1 12.0 %copy-start = (f32[2,8,1536]{2,1,0:T(8,128)S(1)}, f32[2,8,1536]{2,1,0:T(8,128)}, u32[]{:S(2)}) copy-start(f32[2,8,1536]{2,1,0:T(8,128)} %get-tuple-element.18) | copy-start | bytes 294916
  4.1 34.6 %all-to-all-start = ((f32[16,8,1536]{2,1,0:T(8,128)}), f32[16,8,1536]{2,1,0:T(8,128)S(1)}, u32[]{:S(2)}, u32[]{:S(2)}) async-start(f32[16,8,1536]{2,1,0:T(8,128)} %get-tuple-element.17), calls=%async_computation | async-start | bytes 1572864 | tf_op jit(solution)/shard_map/all_to_all | solution.py:337
  38.7 20.9 %collective-permute-start = (f32[128,1536]{1,0:T(8,128)S(1)}, f32[128,1536]{1,0:T(8,128)S(1)}, u32[]{:S(2)}, u32[]{:S(2)}) collective-permute-start(f32[128,1536]{1,0:T(8,128)S(1)} %bitcast.11), channel_id=1, source_target_pairs={{0,2},{2,4},{4,6},{6,0},{1,3},{3,5},{5,7},{7,1},{8,10},{10,12},{12... | collective-permute-start | bytes 2359304 | tf_op jit(solution)/shard_map/ppermute | solution.py:356
  41.8 20.3 %collective-permute-start.1 = (f32[128,1536]{1,0:T(8,128)S(1)}, f32[128,1536]{1,0:T(8,128)S(1)}, u32[]{:S(2)}, u32[]{:S(2)}) collective-permute-start(f32[128,1536]{1,0:T(8,128)S(1)} %bitcast.12), channel_id=1, source_target_pairs={{0,6},{2,0},{4,2},{6,4},{1,7},{3,1},{5,3},{7,5},{8,14},{10,8},{12,... | collective-permute-start | bytes 2359304 | tf_op jit(solution)/shard_map/ppermute | solution.py:357
  45.2 28.7 %collective-permute-start.3 = (f32[1536,256]{1,0:T(8,128)}, f32[1536,256]{1,0:T(8,128)}, u32[]{:S(2)}, u32[]{:S(2)}) collective-permute-start(f32[1536,256]{1,0:T(8,128)} %get-tuple-element.24), channel_id=1, source_target_pairs={{0,1},{1,0},{2,3},{3,2},{4,5},{5,4},{6,7},{7,6},{8,9},{9,8},{10,11... | collective-permute-start | bytes 4718600 | tf_op jit(solution)/shard_map/ppermute | solution.py:352
  48.4 19.3 %all-to-all-start.2 = ((f32[16,24,128]{2,1,0:T(8,128)}), f32[16,24,128]{2,1,0:T(8,128)S(1)}, u32[]{:S(2)}, u32[]{:S(2)}) async-start(f32[16,24,128]{2,1,0:T(8,128)} %block_part.1), calls=%async_computation.2 | async-start | bytes 393216 | tf_op jit(solution)/shard_map/all_to_all | solution.py:337
  63.1 15.9 %collective-permute-start.2 = (f32[128,1536]{1,0:T(8,128)}, f32[128,1536]{1,0:T(8,128)S(1)}, u32[]{:S(2)}, u32[]{:S(2)}) collective-permute-start(f32[128,1536]{1,0:T(8,128)} %broadcast_select_fusion), channel_id=1, source_target_pairs={{0,2},{1,7},{2,4},{3,1},{4,6},{5,3},{6,0},{7,5},{8,10},{9,15},{10,... | collective-permute-start | bytes 2359304 | tf_op jit(solution)/shard_map/ppermute | solution.py:362
  68.5 17.5 %all-to-all-start.3 = ((f32[32,24,128]{2,1,0:T(8,128)}), f32[32,24,128]{2,1,0:T(8,128)S(1)}, u32[]{:S(2)}, u32[]{:S(2)}) async-start(f32[32,24,128]{2,1,0:T(8,128)} %broadcast_in_dim.3), calls=%async_computation.3 | async-start | bytes 786432 | tf_op jit(solution)/shard_map/all_to_all | solution.py:337
  81.1 4.0 %collective-permute-start.4 = (f32[256,512]{1,0:T(8,128)S(1)}, f32[256,512]{1,0:T(8,128)S(1)}, u32[]{:S(2)}, u32[]{:S(2)}) collective-permute-start(f32[256,512]{1,0:T(8,128)S(1)} %further.3), channel_id=1, source_target_pairs={{0,1},{1,0},{2,3},{3,2},{4,5},{5,4},{6,7},{7,6},{8,9},{9,8},{10,11... | collective-permute-start | bytes 1572872 | tf_op jit(solution)/shard_map/ppermute | solution.py:376
  86.0 29.2 %all-to-all-start.1 = ((f32[8,32,512]{2,1,0:T(8,128)}), f32[8,32,512]{2,1,0:T(8,128)S(1)}, u32[]{:S(2)}, u32[]{:S(2)}) async-start(f32[8,32,512]{2,1,0:T(8,128)} %bitcast.3), calls=%async_computation.1 | async-start | bytes 1048576 | tf_op jit(solution)/shard_map/all_to_all | solution.py:337
  92.8 5.8 %collective-permute-start.5 = (f32[32,24,128]{2,1,0:T(8,128)S(1)}, f32[32,24,128]{2,1,0:T(8,128)S(1)}, u32[]{:S(2)}, u32[]{:S(2)}) collective-permute-start(f32[32,24,128]{2,1,0:T(8,128)S(1)} %all-to-all-done.3.own_ref), channel_id=1, source_target_pairs={{0,1},{1,0},{2,3},{3,2},{4,5},{5,4},{6,7},{7,6},{8,9},{9,8},{10,11... | collective-permute-start | bytes 1179656 | tf_op jit(solution)/shard_map/ppermute | solution.py:367

commit v12 on v10

--- a/solution.py
+++ b/solution.py
@@ -348,8 +348,6 @@
     to_along, to_beside, to_other = prepare(row_counts, barrier, border)
     along = exchange(to_along, ("z", "core"))
     beside = lax.all_gather(to_beside, ("x", "core"), axis=0, tiled=False)
-    beside, to_other = lax.optimization_barrier((beside, to_other))
-    other = lax.ppermute(to_other, "core", SWAP)
     along, beside = lax.optimization_barrier((along, beside))
 
     shard = along.reshape(16 * TILE, capacity)
@@ -358,6 +356,8 @@
 
     piece = block_part(along, beside)
     parts = exchange(piece, ("scen", "core"))
+    behind, to_other = lax.optimization_barrier((behind, to_other))
+    other = lax.ppermute(to_other, "core", SWAP)
     _, passed_on = lax.optimization_barrier((piece, jnp.where(core == 0, behind, ahead)))
     onward = lax.ppermute(passed_on, ("x", "core"), ONWARD)
     parts, _ = lax.optimization_barrier((parts, passed_on))

time: 117 us -> 129 us (1.10)
  waiting for transfers between devices: 18.6 us -> 34.4 us
  starting transfers between devices: 50.4 us -> 46.1 us
    ppermute x1, waiting for transfers between devices: 3.68 us -> 14.4 us  [body(): behind = lax.ppermute(shard, 'x', AHEAD)]
    all_to_all x4, waiting for transfers between devices: 8.99 us -> 17.6 us  [exchange(): return lax.all_to_all(array, axes, split_axis=0, concat_axis=0, tiled=True)]
    ppermute x1, waiting for transfers between devices: 2.49 us -> 0.01 us  [body(): ahead = lax.ppermute(shard, 'x', BEHIND)]
    ppermute x1, waiting for transfers between devices: 1.4 us -> 0.01 us  [body(): onward = lax.ppermute(passed_on, ('x', 'core'), ONWARD)]
    all_to_all x4, starting transfers between devices: 30.3 us -> 28.9 us  [exchange(): return lax.all_to_all(array, axes, split_axis=0, concat_axis=0, tiled=True)]
  transfers between devices with their start and end apart: 10 -> 10, of which waited for: 6 -> 6; matrix products, arithmetic and copies ran while one was open for 4% -> 3% of each run, Pallas kernels for 21% -> 19%
where the time goes in v12:
time: 129 us; the launch traced here: 128 us
  starting transfers between devices  46.1 us (36%)
  waiting for transfers between devices  34.4 us (27%)
  Pallas kernels  28.1 us (22%)
  blocking collectives  13.7 us (11%)
  local copies, waits for them, and re-layouts  2.29 us (2%)
  other arithmetic  1.98 us (2%)
  matrix products  1.34 us (1%)
    all_to_all x4, starting transfers between devices, exchange(): return lax.all_to_all(array, axes, split_axis=0, concat_axis=0, tiled=True)  28.9 us
    all_to_all x4, waiting for transfers between devices, exchange(): return lax.all_to_all(array, axes, split_axis=0, concat_axis=0, tiled=True)  17.6 us
    pallas_call x1, Pallas kernels, inverse_factor(): pl.pallas_call(inverse_kernel, out_shape=jax.ShapeDtypeStruct(shape, jnp....  16.6 us
    ppermute x1, waiting for transfers between devices, body(): behind = lax.ppermute(shard, 'x', AHEAD)  14.4 us
    all_gather x1, blocking collectives, body(): beside = lax.all_gather(to_beside, ('x', 'core'), axis=0, tiled=False)  13.7 us
    pallas_call x4, Pallas kernels, product(): pl.pallas_call(further_kernel if done else product_kernel, out_shape=jax....  6.27 us
    pallas_call x1, Pallas kernels, prepare(): pl.pallas_call(prepare_kernel, out_shape=(jax.ShapeDtypeStruct((16, TILE,...  4.05 us
    ppermute x1, starting transfers between devices, body(): onward = lax.ppermute(passed_on, ('x', 'core'), ONWARD)  3.46 us
  transfers between devices with their start and end apart: 10, of which 6 were waited for; matrix products, arithmetic and copies ran while one was open for 3% of the time, Pallas kernels for 19%

profile of v12, /device:TPU:1, one launch (start us, length us, event | category | flops | bytes accessed | tf_op | source)
XLA Modules:
  0.0 128.1 jit_solution(4665330082724340550)
XLA Ops:
  0.0 4.1 %prepare.1 = (f32[16,8,1536]{2,1,0:T(8,128)}, f32[2,8,1536]{2,1,0:T(8,128)}, f32[1536,256]{1,0:T(8,128)}) custom-call(s32[2]{0:T(128)} %counts_ref.1, f32[2,1536]{1,0:T(2,128)} %barrier_ref.1, f32[2,1536,256]{2,1,0:T(8,128)} %border_ref.1), custom_call_target="tpu_custom_call" | custom-call | tf_op jit(solution)/shard_map/prepare/pallas_call | solution.py:248
  4.1 0.0 copy-start
  4.1 12.0 %all-to-all-start = ((f32[16,8,1536]{2,1,0:T(8,128)}), f32[16,8,1536]{2,1,0:T(8,128)S(1)}, u32[]{:S(2)}, u32[]{:S(2)}) async-start(f32[16,8,1536]{2,1,0:T(8,128)} %get-tuple-element.17), calls=%async_computation | async-start | bytes 1572864 | tf_op jit(solution)/shard_map/all_to_all | solution.py:337
  16.0 0.0 copy-done
  16.1 13.7 %all-gather = f32[16,8,1536]{2,1,0:T(8,128)S(1)} all-gather(f32[2,8,1536]{2,1,0:T(8,128)S(1)} %copy-done), channel_id=2, replica_groups=mesh['scen'=8,'z'=8,'x'=4,'core'=2] {'x','core'}, dimensions={0}, use_global_device_ids=true | all-gather | bytes 884736 | tf_op jit(solution)/shard_map/all_gather | solution.py:350
  29.7 9.0 %all-to-all-done.along_ref = f32[16,8,1536]{2,1,0:T(8,128)S(1)} async-done(((f32[16,8,1536]{2,1,0:T(8,128)}), f32[16,8,1536]{2,1,0:T(8,128)S(1)}, u32[]{:S(2)}, u32[]{:S(2)}) %all-to-all-start) | async-done | bytes 786464 | tf_op jit(solution)/shard_map/all_to_all | solution.py:337
  38.7 3.1 %collective-permute-start = (f32[128,1536]{1,0:T(8,128)S(1)}, f32[128,1536]{1,0:T(8,128)S(1)}, u32[]{:S(2)}, u32[]{:S(2)}) collective-permute-start(f32[128,1536]{1,0:T(8,128)S(1)} %bitcast.11), channel_id=1, source_target_pairs={{0,2},{2,4},{4,6},{6,0},{1,3},{3,5},{5,7},{7,1},{8,10},{10,12},{12... | collective-permute-start | bytes 2359304 | tf_op jit(solution)/shard_map/ppermute | solution.py:354
  41.8 3.4 %collective-permute-start.1 = (f32[128,1536]{1,0:T(8,128)S(1)}, f32[128,1536]{1,0:T(8,128)S(1)}, u32[]{:S(2)}, u32[]{:S(2)}) collective-permute-start(f32[128,1536]{1,0:T(8,128)S(1)} %bitcast.12), channel_id=1, source_target_pairs={{0,6},{2,0},{4,2},{6,4},{1,7},{3,1},{5,3},{7,5},{8,14},{10,8},{12,... | collective-permute-start | bytes 2359304 | tf_op jit(solution)/shard_map/ppermute | solution.py:355
  45.2 14.4 %collective-permute-done.refs_1_ = f32[128,1536]{1,0:T(8,128)S(1)} collective-permute-done((f32[128,1536]{1,0:T(8,128)S(1)}, f32[128,1536]{1,0:T(8,128)S(1)}, u32[]{:S(2)}, u32[]{:S(2)}) %collective-permute-start) | collective-permute-done | bytes 786464 | tf_op jit(solution)/shard_map/ppermute | solution.py:354
  59.7 1.9 %collective-permute-start.3 = (f32[1536,256]{1,0:T(8,128)}, f32[1536,256]{1,0:T(8,128)}, u32[]{:S(2)}, u32[]{:S(2)}) collective-permute-start(f32[1536,256]{1,0:T(8,128)} %get-tuple-element.24), channel_id=1, source_target_pairs={{0,1},{1,0},{2,3},{3,2},{4,5},{5,4},{6,7},{7,6},{8,9},{9,8},{10,11... | collective-permute-start | bytes 4718600 | tf_op jit(solution)/shard_map/ppermute | solution.py:360
  61.6 1.2 block_part.1
  62.8 7.6 %all-to-all-start.2 = ((f32[16,24,128]{2,1,0:T(8,128)}), f32[16,24,128]{2,1,0:T(8,128)S(1)}, u32[]{:S(2)}, u32[]{:S(2)}) async-start(f32[16,24,128]{2,1,0:T(8,128)} %block_part.1), calls=%async_computation.2 | async-start | bytes 393216 | tf_op jit(solution)/shard_map/all_to_all | solution.py:337
  70.4 0.0 collective-permute-done.1.refs_2_
  70.4 1.0 broadcast_select_fusion
  71.4 3.5 %collective-permute-start.2 = (f32[128,1536]{1,0:T(8,128)}, f32[128,1536]{1,0:T(8,128)S(1)}, u32[]{:S(2)}, u32[]{:S(2)}) collective-permute-start(f32[128,1536]{1,0:T(8,128)} %broadcast_select_fusion), channel_id=1, source_target_pairs={{0,2},{1,7},{2,4},{3,1},{4,6},{5,3},{6,0},{7,5},{8,10},{9,15},{10,... | collective-permute-start | bytes 2359304 | tf_op jit(solution)/shard_map/ppermute | solution.py:362
  74.9 5.9 %all-to-all-done.2 = f32[16,24,128]{2,1,0:T(8,128)S(1)} async-done(((f32[16,24,128]{2,1,0:T(8,128)}), f32[16,24,128]{2,1,0:T(8,128)S(1)}, u32[]{:S(2)}, u32[]{:S(2)}) %all-to-all-start.2) | async-done | bytes 196640 | tf_op jit(solution)/shard_map/all_to_all | solution.py:337
  80.8 0.8 broadcast_in_dim.3
  81.5 5.8 %all-to-all-start.3 = ((f32[32,24,128]{2,1,0:T(8,128)}), f32[32,24,128]{2,1,0:T(8,128)S(1)}, u32[]{:S(2)}, u32[]{:S(2)}) async-start(f32[32,24,128]{2,1,0:T(8,128)} %broadcast_in_dim.3), calls=%async_computation.3 | async-start | bytes 786432 | tf_op jit(solution)/shard_map/all_to_all | solution.py:337
  87.4 1.5 %dynamic-slice_bitcast_fusion.columns_ref = f32[1536,256]{1,0:T(8,128)S(1)} fusion(f32[2,1536,256]{2,1,0:T(8,128)} %border_ref.1, s32[]{:T(128)S(6)} %select_n.12), kind=kLoop, calls=%fused_computation | loop fusion | bytes 3145732 | tf_op jit(solution)/shard_map/jit(dynamic_index_in_dim)/squeeze | solution.py:370
  88.9 1.2 product.3.before_ref
  90.1 0.0 collective-permute-done.3.columns_ref
  90.1 2.6 %product.2.before_ref = f32[256,384]{1,0:T(8,128)S(1)} custom-call(f32[1536,256]{1,0:T(8,128)} %collective-permute-done.3.columns_ref, f32[128,1536]{1,0:T(8,128)S(1)} %bitcast.14, f32[128,1536]{1,0:T(8,128)S(1)} %collective-permute-done.refs_1_, f32[128,1536]{1,0:T(8,128)S(1)} %collective-permute-done.1.refs_2_), custom_call_target="tpu_custom_call" | custom-call | flops 905969664 | bytes 3932160 | tf_op jit(solution)/shard_map/product/pallas_call | solution.py:323
  92.6 0.0 collective-permute-done.2.panel_ref
  92.6 2.0 %further.3 = f32[256,512]{1,0:T(8,128)S(1)} custom-call(f32[1536,256]{1,0:T(8,128)} %collective-permute-done.3.columns_ref, f32[128,1536]{1,0:T(8,128)S(1)} %collective-permute-done.2.panel_ref, f32[256,384]{1,0:T(8,128)S(1)} %product.2.before_ref), custom_call_target="tpu_custom_call" | custom-call | flops 301989888 | bytes 2359296 | tf_op jit(solution)/shard_map/further/pallas_call | solution.py:323
  94.6 1.9 %collective-permute-start.4 = (f32[256,512]{1,0:T(8,128)S(1)}, f32[256,512]{1,0:T(8,128)S(1)}, u32[]{:S(2)}, u32[]{:S(2)}) collective-permute-start(f32[256,512]{1,0:T(8,128)S(1)} %further.3), channel_id=1, source_target_pairs={{0,1},{1,0},{2,3},{3,2},{4,5},{5,4},{6,7},{7,6},{8,9},{9,8},{10,11... | collective-permute-start | bytes 1572872 | tf_op jit(solution)/shard_map/ppermute | solution.py:376
  96.6 0.6 further.2
  97.1 1.3 %collective-permute-done.4 = f32[256,512]{1,0:T(8,128)S(1)} collective-permute-done((f32[256,512]{1,0:T(8,128)S(1)}, f32[256,512]{1,0:T(8,128)S(1)}, u32[]{:S(2)}, u32[]{:S(2)}) %collective-permute-start.4) | collective-permute-done | bytes 524320 | tf_op jit(solution)/shard_map/ppermute | solution.py:376
  98.4 0.9 add.8
  99.3 2.7 %all-to-all-done.3.own_ref = f32[32,24,128]{2,1,0:T(8,128)S(1)} async-done(((f32[32,24,128]{2,1,0:T(8,128)}), f32[32,24,128]{2,1,0:T(8,128)S(1)}, u32[]{:S(2)}, u32[]{:S(2)}) %all-to-all-start.3) | async-done | bytes 393248 | tf_op jit(solution)/shard_map/all_to_all | solution.py:337
  102.0 3.5 %all-to-all-start.1 = ((f32[8,32,512]{2,1,0:T(8,128)}), f32[8,32,512]{2,1,0:T(8,128)S(1)}, u32[]{:S(2)}, u32[]{:S(2)}) async-start(f32[8,32,512]{2,1,0:T(8,128)} %bitcast.3), calls=%async_computation.1 | async-start | bytes 1048576 | tf_op jit(solution)/shard_map/all_to_all | solution.py:337
  105.5 3.4 %collective-permute-start.5 = (f32[32,24,128]{2,1,0:T(8,128)S(1)}, f32[32,24,128]{2,1,0:T(8,128)S(1)}, u32[]{:S(2)}, u32[]{:S(2)}) collective-permute-start(f32[32,24,128]{2,1,0:T(8,128)S(1)} %all-to-all-done.3.own_ref), channel_id=1, source_target_pairs={{0,1},{1,0},{2,3},{3,2},{4,5},{5,4},{6,7},{7,6},{8,9},{9,8},{10,11... | collective-permute-start | bytes 1179656 | tf_op jit(solution)/shard_map/ppermute | solution.py:367
  109.0 0.1 pad_add_fusion.place_ref
  109.0 1.1 collective-permute-done.5.other_ref
  110.1 16.6 %inverse_factor.1 = f32[512,512]{1,0:T(8,128)S(1)} custom-call(s32[2]{0:T(128)S(1)} %pad_add_fusion.place_ref, f32[32,24,128]{2,1,0:T(8,128)S(1)} %all-to-all-done.3.own_ref, f32[32,24,128]{2,1,0:T(8,128)S(1)} %collective-permute-done.5.other_ref), custom_call_target="tpu_custom_call" | custom-call | flops 536870912 | bytes 2097152 | tf_op jit(solution)/shard_map/inverse_factor/pallas_call | solution.py:211
  126.7 0.0 all-to-all-done.1
  126.8 1.3 %convolution_bitcast_fusion = f32[1,1,32,512]{3,2,1,0:T(8,128)} fusion(f32[32,512]{1,0:T(8,128)S(1)} %reduce_sum.18, f32[512,512]{1,0:T(8,128)S(1)} %inverse_factor.1), kind=kOutput, calls=%fused_computation.1 | convolution fusion | flops 100663296 | bytes 1179648 | tf_op jit(solution)/shard_map/dot_general | solution.py:20
  (2 shorter events, 0.1 us)
Async XLA Ops:
  4.1 12.0 %copy-start = (f32[2,8,1536]{2,1,0:T(8,128)S(1)}, f32[2,8,1536]{2,1,0:T(8,128)}, u32[]{:S(2)}) copy-start(f32[2,8,1536]{2,1,0:T(8,128)} %get-tuple-element.18) | copy-start | bytes 294916
  4.1 34.6 %all-to-all-start = ((f32[16,8,1536]{2,1,0:T(8,128)}), f32[16,8,1536]{2,1,0:T(8,128)S(1)}, u32[]{:S(2)}, u32[]{:S(2)}) async-start(f32[16,8,1536]{2,1,0:T(8,128)} %get-tuple-element.17), calls=%async_computation | async-start | bytes 1572864 | tf_op jit(solution)/shard_map/all_to_all | solution.py:337
  38.7 20.9 %collective-permute-start = (f32[128,1536]{1,0:T(8,128)S(1)}, f32[128,1536]{1,0:T(8,128)S(1)}, u32[]{:S(2)}, u32[]{:S(2)}) collective-permute-start(f32[128,1536]{1,0:T(8,128)S(1)} %bitcast.11), channel_id=1, source_target_pairs={{0,2},{2,4},{4,6},{6,0},{1,3},{3,5},{5,7},{7,1},{8,10},{10,12},{12... | collective-permute-start | bytes 2359304 | tf_op jit(solution)/shard_map/ppermute | solution.py:354
  41.8 28.6 %collective-permute-start.1 = (f32[128,1536]{1,0:T(8,128)S(1)}, f32[128,1536]{1,0:T(8,128)S(1)}, u32[]{:S(2)}, u32[]{:S(2)}) collective-permute-start(f32[128,1536]{1,0:T(8,128)S(1)} %bitcast.12), channel_id=1, source_target_pairs={{0,6},{2,0},{4,2},{6,4},{1,7},{3,1},{5,3},{7,5},{8,14},{10,8},{12,... | collective-permute-start | bytes 2359304 | tf_op jit(solution)/shard_map/ppermute | solution.py:355
  59.7 30.4 %collective-permute-start.3 = (f32[1536,256]{1,0:T(8,128)}, f32[1536,256]{1,0:T(8,128)}, u32[]{:S(2)}, u32[]{:S(2)}) collective-permute-start(f32[1536,256]{1,0:T(8,128)} %get-tuple-element.24), channel_id=1, source_target_pairs={{0,1},{1,0},{2,3},{3,2},{4,5},{5,4},{6,7},{7,6},{8,9},{9,8},{10,11... | collective-permute-start | bytes 4718600 | tf_op jit(solution)/shard_map/ppermute | solution.py:360
  62.8 17.9 %all-to-all-start.2 = ((f32[16,24,128]{2,1,0:T(8,128)}), f32[16,24,128]{2,1,0:T(8,128)S(1)}, u32[]{:S(2)}, u32[]{:S(2)}) async-start(f32[16,24,128]{2,1,0:T(8,128)} %block_part.1), calls=%async_computation.2 | async-start | bytes 393216 | tf_op jit(solution)/shard_map/all_to_all | solution.py:337
  71.4 21.2 %collective-permute-start.2 = (f32[128,1536]{1,0:T(8,128)}, f32[128,1536]{1,0:T(8,128)S(1)}, u32[]{:S(2)}, u32[]{:S(2)}) collective-permute-start(f32[128,1536]{1,0:T(8,128)} %broadcast_select_fusion), channel_id=1, source_target_pairs={{0,2},{1,7},{2,4},{3,1},{4,6},{5,3},{6,0},{7,5},{8,10},{9,15},{10,... | collective-permute-start | bytes 2359304 | tf_op jit(solution)/shard_map/ppermute | solution.py:362
  81.5 20.5 %all-to-all-start.3 = ((f32[32,24,128]{2,1,0:T(8,128)}), f32[32,24,128]{2,1,0:T(8,128)S(1)}, u32[]{:S(2)}, u32[]{:S(2)}) async-start(f32[32,24,128]{2,1,0:T(8,128)} %broadcast_in_dim.3), calls=%async_computation.3 | async-start | bytes 786432 | tf_op jit(solution)/shard_map/all_to_all | solution.py:337
  94.6 3.8 %collective-permute-start.4 = (f32[256,512]{1,0:T(8,128)S(1)}, f32[256,512]{1,0:T(8,128)S(1)}, u32[]{:S(2)}, u32[]{:S(2)}) collective-permute-start(f32[256,512]{1,0:T(8,128)S(1)} %further.3), channel_id=1, source_target_pairs={{0,1},{1,0},{2,3},{3,2},{4,5},{5,4},{6,7},{7,6},{8,9},{9,8},{10,11... | collective-permute-start | bytes 1572872 | tf_op jit(solution)/shard_map/ppermute | solution.py:376
  102.0 24.7 %all-to-all-start.1 = ((f32[8,32,512]{2,1,0:T(8,128)}), f32[8,32,512]{2,1,0:T(8,128)S(1)}, u32[]{:S(2)}, u32[]{:S(2)}) async-start(f32[8,32,512]{2,1,0:T(8,128)} %bitcast.3), calls=%async_computation.1 | async-start | bytes 1048576 | tf_op jit(solution)/shard_map/all_to_all | solution.py:337
  105.5 4.6 %collective-permute-start.5 = (f32[32,24,128]{2,1,0:T(8,128)S(1)}, f32[32,24,128]{2,1,0:T(8,128)S(1)}, u32[]{:S(2)}, u32[]{:S(2)}) collective-permute-start(f32[32,24,128]{2,1,0:T(8,128)S(1)} %all-to-all-done.3.own_ref), channel_id=1, source_target_pairs={{0,1},{1,0},{2,3},{3,2},{4,5},{5,4},{6,7},{7,6},{8,9},{9,8},{10,11... | collective-permute-start | bytes 1179656 | tf_op jit(solution)/shard_map/ppermute | solution.py:367
